TPU v7x, 128 devices: a whole 4x4x4 slice. The times are simulated.
128 devices in a mesh: member: 8 (over x, core), node: 16 (over z, y).
Axes of the slice: x: 4, y: 4, z: 4, core: 2. Of those that a mesh axis runs over, the one named last changes fastest.
Arguments:
- latents: bfloat16 [8, 6144, 1024], P('member', 'node'), may hold values from -6 to 6
- grid_embed: bfloat16 [16384, 1024], P('node'), may hold values from -6 to 6
- neighbours: int32 [3, 16384], P(None, 'node'), may hold values from 0 to 383
- edge_coef: float32 [3, 16384], P(None, 'node'), may hold values from 0.1 to 1
- w_value: bfloat16 [1024, 1024], replicated, may hold values from -0.1875 to 0.1875
- gain: float32 [1024], replicated, may hold values from 0.25 to 1.75
- w_hidden: bfloat16 [1024, 2048], replicated, may hold values from -0.1875 to 0.1875
- output_weight: bfloat16 [100, 2048], replicated, may hold values from -0.125 to 0.125
- targets: float32 [100, 16384], P(None, 'node'), may hold values from -6 to 6
- var_weight: float32 [100], replicated, may hold values from 0.2 to 2
- area: float32 [16384], P('node'), may hold values from 0.3 to 3
- valid_counts: int32 [16], replicated, may hold values from 512 to 1024, as said below
Outputs:
- grad_value: float32 [1024, 1024], P(('member', 'node'))
- grad_gain: float32 [1024], P(('member', 'node'))
- grad_hidden: float32 [1024, 2048], P(('member', 'node'))
- grad_out: float32 [100, 2048], P(None, ('member', 'node'))
- grad_latents: bfloat16 [8, 6144, 1024], P('member', 'node')
Inputs may be any that keep to these rules, and one draw needn't show every extreme that they name: `neighbours`: an entry n in column g of partition p names mesh node p * 384 + n. `valid_counts`: some partition has all 1024 slots valid and some exactly half of them.
All inputs are finite; a program needn't handle non-finite values.
Results may differ from a plain program's by a relative error of at most 0.012.
Values may be sent and summed in bfloat16 or wider, within the bound.
No kernel may reach another device: no remote copies, remote signals or barrier semaphores. Data moves between devices by JAX's collectives and lax.ppermute only.
A program may use at most 128 MiB of HBM per device.

v0:
```python
import jax
import jax.numpy as jnp
from jax import lax
from jax.sharding import PartitionSpec as P

kernel_width = 0.25
fair_alpha = 0.95
norm_eps = 1e-05


def decode_forward(
    latent_rows, embedded, neighbour_rows, coef_rows, w_value, gain, w_hidden, output_weight
):
    node_values = jnp.dot(latent_rows, w_value, preferred_element_type=jnp.float32).astype(
        jnp.bfloat16
    )
    gathered = node_values[neighbour_rows]
    message = jnp.sum(coef_rows[:, :, None] * gathered.astype(jnp.float32), axis=0)
    summed = embedded.astype(jnp.float32) + message
    inverse_root_mean_square = lax.rsqrt(
        jnp.mean(summed * summed, axis=-1, keepdims=True) + norm_eps
    )
    unit_norm_rows = summed * inverse_root_mean_square
    normalized_rows = (unit_norm_rows * gain).astype(jnp.bfloat16)
    preactivation = jnp.dot(normalized_rows, w_hidden, preferred_element_type=jnp.float32)
    hidden_activation = jax.nn.gelu(preactivation).astype(jnp.bfloat16)
    member_prediction = lax.dot_general(
        output_weight,
        hidden_activation,
        (((1,), (1,)), ((), ())),
        preferred_element_type=jnp.float32,
    )
    return (
        member_prediction,
        (
            unit_norm_rows,
            inverse_root_mean_square,
            normalized_rows,
            preactivation,
            hidden_activation,
        ),
    )


def ensemble_terms(member_own_field, ensemble, target_row_values, weight_matrix):
    member_count = ensemble.shape[0]
    misfit = member_own_field - target_row_values
    distance = jnp.sqrt(misfit * misfit + kernel_width * kernel_width)
    deltas = member_own_field[None] - ensemble
    pair_dist = jnp.sqrt(deltas * deltas + kernel_width * kernel_width)
    spread = (1.0 - (1.0 - fair_alpha) / member_count) / (2.0 * member_count * (member_count - 1))
    activation_slopes = misfit / distance / member_count - 2.0 * spread * jnp.sum(
        deltas / pair_dist, axis=0
    )
    return weight_matrix * activation_slopes


def backward_upper(slope_rows, saved_tensors, w_hidden, output_weight):
    unit_norm_rows, inverse_root_mean_square, normalized_rows, preactivation, hidden_activation = (
        saved_tensors
    )
    grad_out = jnp.dot(slope_rows, hidden_activation, preferred_element_type=jnp.float32)
    hidden_grad = lax.dot_general(
        slope_rows, output_weight, (((0,), (0,)), ((), ())), preferred_element_type=jnp.float32
    )
    _, gelu_back = jax.vjp(jax.nn.gelu, preactivation)
    pre_grad = gelu_back(hidden_grad)[0].astype(jnp.bfloat16)
    grad_hidden = lax.dot_general(
        normalized_rows, pre_grad, (((0,), (0,)), ((), ())), preferred_element_type=jnp.float32
    )
    normed_grad = lax.dot_general(
        pre_grad, w_hidden, (((1,), (1,)), ((), ())), preferred_element_type=jnp.float32
    )
    return (grad_out, grad_hidden, normed_grad)


def backward_lower(
    normed_grad, saved_tensors, latent_rows, neighbour_rows, coef_rows, w_value, gain
):
    unit_norm_rows, inverse_root_mean_square, normalized_rows, preactivation, hidden_activation = (
        saved_tensors
    )
    grad_gain = jnp.sum(normed_grad * unit_norm_rows, axis=0)
    unit_grad = normed_grad * gain
    summed_grad = inverse_root_mean_square * (
        unit_grad - unit_norm_rows * jnp.mean(unit_grad * unit_norm_rows, axis=-1, keepdims=True)
    )
    edge_grads = coef_rows[:, :, None] * summed_grad[None]
    width = summed_grad.shape[1]
    value_grad = jax.ops.segment_sum(
        edge_grads.reshape(-1, width), neighbour_rows.reshape(-1), num_segments=latent_rows.shape[0]
    ).astype(jnp.bfloat16)
    grad_value = lax.dot_general(
        latent_rows, value_grad, (((0,), (0,)), ((), ())), preferred_element_type=jnp.float32
    )
    latent_grad = lax.dot_general(
        value_grad, w_value, (((1,), (1,)), ((), ())), preferred_element_type=jnp.float32
    ).astype(jnp.bfloat16)
    return (grad_value, grad_gain, latent_grad)


def per_device(
    latents,
    grid_embed,
    neighbours,
    edge_coef,
    w_value,
    gain,
    w_hidden,
    output_weight,
    targets,
    var_weight,
    area,
    valid_counts,
):
    node_index = lax.axis_index("node")
    grid_rows = grid_embed.shape[0]
    latent_rows = latents[0]
    member_prediction, saved_tensors = decode_forward(
        latent_rows, grid_embed, neighbours, edge_coef, w_value, gain, w_hidden, output_weight
    )
    live_count = jnp.sum(
        jnp.where(jnp.arange(valid_counts.shape[0]) == node_index, valid_counts, 0)
    )
    live = (jnp.arange(grid_rows) < live_count).astype(jnp.float32)
    weight_matrix = var_weight[:, None] * (area * live)[None, :] / var_weight.shape[0]
    all_members_joined = lax.all_gather(member_prediction[None], "member", axis=0, tiled=True)
    activation_slopes = ensemble_terms(
        member_prediction, all_members_joined, targets, weight_matrix
    )
    slope_rows = activation_slopes.astype(jnp.bfloat16)
    grad_out, grad_hidden, normed_grad = backward_upper(
        slope_rows, saved_tensors, w_hidden, output_weight
    )
    grad_value, grad_gain, latent_grad = backward_lower(
        normed_grad, saved_tensors, latent_rows, neighbours, edge_coef, w_value, gain
    )
    value_sum, gain_sum, hidden_sum, out_sum = (
        lax.psum_scatter(grad_value, ("member", "node"), scatter_dimension=0, tiled=True),
        lax.psum_scatter(grad_gain, ("member", "node"), scatter_dimension=0, tiled=True),
        lax.psum_scatter(grad_hidden, ("member", "node"), scatter_dimension=0, tiled=True),
        lax.psum_scatter(grad_out, ("member", "node"), scatter_dimension=1, tiled=True),
    )
    return (value_sum, gain_sum, hidden_sum, out_sum, latent_grad[None])


def solution(mesh):
    in_specs = (
        P("member", "node", None),
        P("node", None),
        P(None, "node"),
        P(None, "node"),
        P(),
        P(),
        P(),
        P(),
        P(None, "node"),
        P(),
        P("node"),
        P(),
    )
    out_specs = (
        P(("member", "node"), None),
        P(("member", "node")),
        P(("member", "node"), None),
        P(None, ("member", "node")),
        P("member", "node", None),
    )
    return jax.shard_map(
        per_device, mesh=mesh, in_specs=in_specs, out_specs=out_specs, check_vma=False
    )
```

profile of v0, /device:TPU:0, one launch (start us, length us, event | category | flops | bytes accessed | tf_op | source)
XLA Modules:
  0.0 2029.9 jit_solution(9551280929715133499)
XLA Ops:
  7.2 0.0 copy-start
  7.2 0.0 all-gather.4.cloned.1.call-start
  7.2 0.9 compare_select_fusion
  8.1 0.7 copy-done
  8.8 2.1 convolution_convert_fusion.1
  10.9 0.0 copy-start.10
  10.9 14.0 gather_fusion
  24.9 0.0 copy-done.10
  24.9 4.5 fusion
  29.4 0.0 copy-done.6
  29.4 0.0 copy-start.9
  29.4 0.0 copy-start.14
  29.4 0.6 multiply_reduce_fusion.2
  30.0 0.0 copy-start.1
  30.1 0.0 copy-done.9
  30.1 3.0 copy-done.14
  33.1 0.0 copy-start.8
  33.1 8.5 multiply_convert_fusion
  41.7 0.0 copy-done.1
  41.7 0.0 copy-start.11
  41.7 0.0 copy-start.15
  41.7 0.0 copy-start.12
  41.7 2.0 copy-done.3
  43.6 0.0 copy-done.8
  43.6 0.0 copy-start.13
  43.6 2.2 fusion.19
  45.8 0.0 copy-start.5
  45.8 0.0 all-gather.4.cloned.1.call-update
  45.9 0.2 reduce-scatter.8.cloned.1.call-start
  46.1 0.0 copy-done.11
  46.2 0.0 copy-done.15
  46.2 0.6 fusion.16
  46.8 0.0 copy-done.12
  46.8 0.6 fusion.15
  47.5 29.9 %all-gather.4.cloned.1.call-done = f32[8,100,1024]{2,1,0:T(8,128)} async-done(((f32[1,100,1024]{2,1,0:T(8,128)}), f32[8,100,1024]{2,1,0:T(8,128)}) %all-gather.4.cloned.1.call-update) | async-done | bytes 3276816 | tf_op jit(solution)/shard_map/all_gather | solution.py:127
  77.3 2.9 multiply_reduce_fusion.3
  80.2 0.0 copy-done.13
  80.2 0.0 copy-done.5
  80.3 1.2 multiply_convert_fusion.2
  81.4 0.0 copy-done.4
  81.5 2.8 fusion.20
  84.2 9.6 fusion.7
  93.8 0.0 reduce-scatter.8.cloned.1.call-update
  93.9 0.3 reduce-scatter.10.cloned.1.call-start
  94.1 0.0 copy-start.2
  94.1 9.7 multiply_reduce_fusion
  103.8 0.0 copy-done.2
  103.9 0.8 subtract_multiply_fusion
  104.7 0.0 copy-start.7
  104.7 5.5 bitcast_multiply_fusion
  110.1 28.9 %scatter_custom_fusion = f32[384,1024]{1,0:T(8,128)} fusion(s32[3072]{0:T(1024)S(1)} %reshape.42, f32[3072,1024]{1,0:T(8,128)} %bitcast_multiply_fusion, f32[]{:T(128)} %constant.16.clone.1), kind=kCustom, calls=%fused_computation.28 | custom fusion | flops 3145728 | bytes 1573376 | tf_op jit(solution)/shard_map/scatter-add | solution.py:90
  139.0 0.0 copy-done.7
  139.0 4.6 convolution_bitcast_fusion
  143.6 5.3 copy.19
  149.0 0.0 reduce-scatter.10.cloned.1.call-update
  149.0 0.3 reduce-scatter.6.cloned.1.call-start
  149.3 11.4 fusion.17
  160.7 0.0 reduce-scatter.6.cloned.1.call-update
  160.7 66.6 %all-reduce = f32[1024]{0:T(1024)S(1)} all-reduce(f32[1024]{0:T(1024)S(1)} %get-tuple-element.15), channel_id=4, replica_groups=mesh['member'=8,'node'=16] {'member','node'}, use_global_device_ids=true, to_apply=%region_8.9.clone | all-reduce | flops 1024 | bytes 8192
  227.3 0.6 dynamic-slice
  227.9 3.3 fusion.8
  231.2 502.0 %reduce-scatter.8.cloned.1.call-done = f32[100,16]{0,1:T(8,128)} async-done(((f32[100,2048]{0,1:T(8,128)}), f32[100,16]{0,1:T(8,128)}) %reduce-scatter.8.cloned.1.call-update) | async-done | bytes 6416 | tf_op jit(solution)/shard_map/reduce_scatter | solution.py:142
  733.2 641.9 %reduce-scatter.10.cloned.1.call-done = f32[8,1024]{1,0:T(8,128)} async-done(((f32[1024,1024]{1,0:T(8,128)}), f32[8,1024]{1,0:T(8,128)}) %reduce-scatter.10.cloned.1.call-update) | async-done | bytes 32784
  1375.0 648.3 %reduce-scatter.6.cloned.1.call-done = f32[8,2048]{1,0:T(8,128)} async-done(((f32[1024,2048]{1,0:T(8,128)}), f32[8,2048]{1,0:T(8,128)}) %reduce-scatter.6.cloned.1.call-update) | async-done | bytes 65552 | tf_op jit(solution)/shard_map/reduce_scatter | solution.py:141
  (9 shorter events, 0.1 us)
Async XLA Ops:
  7.2 1.6 copy-start
  7.2 70.1 %all-gather.4.cloned.1.call-start = ((), (), s32[]{:S(2)}) async-start(), calls=%async_computation.5 | async-start | bytes 3833856 | tf_op jit(solution)/shard_map/all_gather | solution.py:127
  10.9 14.0 copy-start.10
  24.9 4.5 copy-start.6
  29.4 0.7 copy-start.9
  29.4 3.7 copy-start.14
  30.0 11.6 copy-start.1
  33.1 10.5 copy-start.8
  41.7 2.0 copy-start.3
  41.7 4.4 copy-start.11
  41.7 4.5 copy-start.15
  41.7 5.1 copy-start.12
  43.6 36.6 %copy-start.13 = (f32[100]{0:T(128)S(1)}, f32[100]{0:T(128)}, u32[]{:S(2)}) copy-start(f32[100]{0:T(128)} %param.21) | copy-start | bytes 1204
  45.8 34.4 %copy-start.5 = (f32[1024,100]{0,1:T(8,128)S(1)}, f32[1024,100]{0,1:T(8,128)}, u32[]{:S(2)}) copy-start(f32[1024,100]{0,1:T(8,128)} %fusion.19) | copy-start | bytes 1228804
  45.9 687.3 %reduce-scatter.8.cloned.1.call-start = ((), (), s32[]{:S(2)}) async-start(), calls=%async_computation.4 | async-start | bytes 1056768 | tf_op jit(solution)/shard_map/reduce_scatter | solution.py:142
  77.3 4.1 copy-start.4
  93.9 1281.2 %reduce-scatter.10.cloned.1.call-start = ((), (), s32[]{:S(2)}) async-start(), calls=%async_computation.6 | async-start | bytes 4227072
  94.1 9.7 copy-start.2
  104.7 34.3 %copy-start.7 = (bf16[1,384,1024]{2,1,0:T(8,128)(2,1)S(1)}, bf16[1,384,1024]{2,1,0:T(8,128)(2,1)}, u32[]{:S(2)}) copy-start(bf16[1,384,1024]{2,1,0:T(8,128)(2,1)} %param.12) | copy-start | bytes 2359300
  149.0 1874.3 %reduce-scatter.6.cloned.1.call-start = ((), (), s32[]{:S(2)}) async-start(), calls=%async_computation.3 | async-start | bytes 8454144 | tf_op jit(solution)/shard_map/reduce_scatter | solution.py:141
Sparse Core Ops, SparseCore 0:
  46.0 31.2 all-gather.3
  94.0 639.1 reduce-scatter.7
  736.2 638.7 reduce-scatter.9
  1377.8 645.4 reduce-scatter.5
where the time goes:
time: 2030 us
  waiting for transfers between devices  1820 us (90%)
  blocking collectives  66.6 us (3%)
  matrix products  54.3 us (3%)
  other arithmetic  46.5 us (2%)
  local copies, waits for them, and re-layouts  25.7 us (1%)
    reduce_scatter x1, waiting for transfers between devices, per_device(): lax.psum_scatter(grad_hidden, ('member', 'node'), scatter_dimension=0, ti...  648 us
    unnamed x5, waiting for transfers between devices  642 us
    reduce_scatter x1, waiting for transfers between devices, per_device(): lax.psum_scatter(grad_out, ('member', 'node'), scatter_dimension=1, tiled...  502 us
    unnamed x1, blocking collectives  66.6 us
  transfers between devices with their start and end apart: 4, of which 4 were waited for; matrix products, arithmetic and copies ran while one was open for 4% of the time, Pallas kernels for 0%

commit v1 on v0

v1 whole, which is shorter than its diff:
```python
import itertools

import jax
import jax.numpy as jnp
from jax import lax
from jax.experimental import pallas as pl
from jax.experimental.pallas import tpu as pltpu
from jax.sharding import PartitionSpec as P

BF = jnp.bfloat16
F32 = jnp.float32
kernel_width = 0.25
fair_alpha = 0.95
norm_eps = 1e-05
members = 8
GELU_C = 0.7978845608028654
VMEM = 56 * 1024 * 1024
ORDER_A1 = "xzy"
ORDER_A2 = "zyx"
ORDER_B = "yxz"
AXES = ("member", "node")


def flat(x, c, z, y):
    return ((x * 2 + c) * 4 + z) * 4 + y


def core_pairs():
    return [
        (flat(x, c, z, y), flat(x, 1 - c, z, y))
        for x, c, z, y in itertools.product(range(4), range(2), range(4), range(4))
    ]


def ring_pairs(axis, step):
    pairs = []
    for x, c, z, y in itertools.product(range(4), range(2), range(4), range(4)):
        to = {"x": x, "z": z, "y": y}
        to[axis] ^= (1, 3)[c ^ step]
        pairs.append((flat(x, c, z, y), flat(to["x"], c, to["z"], to["y"])))
    return pairs


def own_place():
    member, node = lax.axis_index("member"), lax.axis_index("node")
    return {"x": member // 2, "c": member % 2, "z": node // 4, "y": node % 4}


def shard_at(position, own, order):
    core = own["c"] ^ ((position >> 6) & 1)
    first, second = 1 + 2 * core, 3 - 2 * core
    place = {}
    for t, axis in enumerate(order):
        a, b = (position >> (5 - 2 * t)) & 1, (position >> (4 - 2 * t)) & 1
        place[axis] = own[axis] ^ (a * first) ^ (b * second)
    return flat(place["x"], core, place["z"], place["y"])


def points_at(position, own):
    core = own["c"] ^ (position >> 2)
    first, second = 1 + 2 * core, 3 - 2 * core
    x = own["x"] ^ (((position >> 1) & 1) * first) ^ ((position & 1) * second)
    return x * 2 + core


def dot(a, b, dims=((1,), (0,))):
    return lax.dot_general(a, b, (dims, ((), ())), preferred_element_type=F32)


def reorder(source, target, own, order, columns=None):
    def body(q, carry):
        blocks = []
        for k in range(2):
            shard = shard_at(2 * q + k, own, order)
            blocks.append(source[pl.ds(pl.multiple_of(shard * 8, 8), 8), :])
        rows = pl.ds(pl.multiple_of(q * 16, 16), 16)
        target[rows, :] = jnp.concatenate(blocks, axis=0).astype(BF)
        return carry

    lax.fori_loop(0, 64, body, 0, unroll=4)


def forward_kernel(
    lat_ref, wv_ref, nb_ref, cf_ref, emb_ref, gain_ref, wh_ref, ow_ref,
    fc_ref, hid_ref, dg_ref, nta_ref, ntb_ref, unit_ref, inv_ref, st_ref,
    nrm, total, turned,
):
    j = pl.program_id(0)
    nodes, points = st_ref.shape
    own = own_place()

    @pl.when(j == 0)
    def _():
        values = dot(lat_ref[...], wv_ref[...]).astype(BF)
        rows_of = lax.broadcasted_iota(jnp.int32, (nodes, 256), 0)
        for r in range(points // 256):
            rows = slice(256 * r, 256 * r + 256)
            st = jnp.zeros((nodes, 256), F32)
            for k in range(3):
                st = st + jnp.where(nb_ref[k : k + 1, rows] == rows_of, cf_ref[k : k + 1, rows], 0.0)
            st = st.astype(BF)
            st_ref[:, rows] = st
            summed = emb_ref[rows, :].astype(F32) + dot(st, values, ((0,), (0,)))
            inv = lax.rsqrt(jnp.mean(summed * summed, axis=-1, keepdims=True) + norm_eps)
            unit = summed * inv
            inv_ref[rows, :] = inv
            unit_ref[rows, :] = unit.astype(BF)
            normed = (unit * gain_ref[...]).astype(BF)
            nrm[rows, :] = normed
            turned[:, rows] = normed.astype(F32).T
        reorder(turned, nta_ref, own, ORDER_A1)
        reorder(turned, ntb_ref, own, ORDER_A2)
        total[...] = jnp.zeros_like(total)

    step = 256
    for r in range(points // step):
        rows = slice(step * r, step * r + step)
        pre = dot(nrm[rows, :], wh_ref[...])
        square = pre * pre
        t = jnp.tanh(GELU_C * pre * (1.0 + 0.044715 * square))
        cdf = 0.5 + 0.5 * t
        slope = cdf + 0.5 * GELU_C * pre * (1.0 - t * t) * (1.0 + 3 * 0.044715 * square)
        hid_ref[rows, :] = (pre * cdf).astype(BF)
        dg_ref[rows, :] = slope.astype(BF)
    total[0:100, :] += dot(ow_ref[...], hid_ref[...], ((1,), (1,)))

    @pl.when(j == pl.num_programs(0) - 1)
    def _():
        for p in range(8):
            first = pl.multiple_of(points_at(p, own) * 128, 128)
            fc_ref[p] = total[:, pl.ds(first, 128)]


def slopes_kernel(vc_ref, f_ref, r0_ref, r1_ref, r2_ref, tg_ref, vw_ref, area_ref, keep_ref, send_ref, held):
    member, node = lax.axis_index("member"), lax.axis_index("node")
    first = pl.multiple_of(member * 128, 128)
    mine = pl.ds(first, 128)
    place = first + lax.broadcasted_iota(jnp.int32, (1, 128), 1)
    live = jnp.where(place < vc_ref[node], area_ref[:, mine], 0.0)
    spread = (1.0 - (1.0 - fair_alpha) / members) / (2.0 * members * (members - 1))
    fields = [
        f_ref.at[0], r0_ref.at[0], r1_ref.at[0], r1_ref.at[2],
        r2_ref.at[0], r2_ref.at[1], r2_ref.at[2], r2_ref.at[3],
    ]
    held[:, 96:112, :] = jnp.zeros((8, 16, 128), F32)
    for top in range(0, 100, 8):
        rows = slice(top, min(top + 8, 100))
        f = [field[rows, :] for field in fields]
        sums = [jnp.zeros_like(f[0]) for _ in f]
        for a in range(8):
            for b in range(a + 1, 8):
                d = f[a] - f[b]
                s = d * lax.rsqrt(d * d + kernel_width * kernel_width)
                sums[a] = sums[a] + s
                sums[b] = sums[b] - s
        target = tg_ref[rows, mine]
        weight = vw_ref[rows, :] * live * 0.01
        for a in range(8):
            d = f[a] - target
            s = d * lax.rsqrt(d * d + kernel_width * kernel_width)
            held[a, rows, :] = weight * (s * (1.0 / members) - 2.0 * spread * sums[a])
    for a in range(4):
        keep_ref[a] = held[a].astype(BF)
        send_ref[a] = held[4 + a].astype(BF)


def upper_kernel(last_piece, *refs):
    if last_piece:
        (s0, s1, s2, s3, ow_ref, dg_ref, hid_ref, nt_ref, go_first,
         pg_ref, keep_ref, send_ref, slopes, turned, own_w, go, go_turned) = refs
    else:
        (s0, s1, s2, s3, ow_ref, dg_ref, hid_ref, nt_ref,
         pg_ref, keep_ref, send_ref, go, slopes, turned, own_w) = refs
    j = pl.program_id(0)
    points = dg_ref.shape[0]
    half = keep_ref.shape[0]
    own = own_place()

    @pl.when(j == 0)
    def _():
        parts = [s0.at[0], s1.at[0], s2.at[0], s2.at[2], s3.at[0], s3.at[1], s3.at[2], s3.at[3]]
        for p in range(8):
            block = jnp.concatenate([parts[p][...].astype(F32), jnp.zeros((16, 128), F32)], axis=0)
            at = pl.ds(pl.multiple_of(points_at(p, own) * 128, 128), 128)
            slopes[:, at] = block.astype(BF)
            turned[at, :] = block.T.astype(BF)
        own_w[...] = jnp.zeros_like(own_w)

    def tile():
        own_w[0:100, :] = ow_ref[...]
        for r in range(points // 256):
            rows = slice(256 * r, 256 * r + 256)
            grad = dot(turned[rows, :], own_w[...])
            pg_ref[rows, :] = (dg_ref[rows, :].astype(F32) * grad).astype(BF)
        go[:, pl.ds(pl.multiple_of(j * 256, 256), 256)] = dot(slopes[...], hid_ref[...])
        keep_ref[...] = dot(nt_ref[0:half, :], pg_ref[...]).astype(BF)
        send_ref[...] = dot(nt_ref[half:, :], pg_ref[...]).astype(BF)

    if not last_piece:
        tile()
        return

    pl.when(j < 4)(tile)

    @pl.when(j == 4)
    def _():
        go_turned[0:1024, :] = go_first[...].T
        go_turned[1024:2048, :] = go[...].T
        for ref, start in ((keep_ref, 0), (send_ref, 64)):

            def body(q, carry, ref=ref, start=start):
                blocks = []
                for k in range(2):
                    shard = shard_at(start + 2 * q + k, own, ORDER_A2)
                    block = go_turned[pl.ds(pl.multiple_of(shard * 16, 16), 16), :]
                    blocks.append(jnp.concatenate([block[0:8], block[8:16]], axis=1))
                rows = pl.ds(pl.multiple_of(q * 16, 16), 16)
                ref[rows, :] = jnp.concatenate(blocks, axis=0).astype(BF)
                return carry

            lax.fori_loop(0, 32, body, 0, unroll=4)


def lower_kernel(
    pga_ref, pgb_ref, wh_ref, unit_ref, inv_ref, gain_ref, st_ref, lat_ref, wv_ref,
    keep_ref, send_ref, gl_ref,
    gain_sum, value_sum, turned, lat_turned, gain_turned, placed,
):
    j = pl.program_id(0)
    width = lat_ref.shape[1]
    half = keep_ref.shape[0]
    own = own_place()

    @pl.when(j == 0)
    def _():
        gain_sum[...] = jnp.zeros_like(gain_sum)
        value_sum[...] = jnp.zeros_like(value_sum)
        turned[...] = lat_ref[...].astype(F32).T
        reorder(turned, lat_turned, own, ORDER_B)

    normed_grad = dot(pga_ref[...], wh_ref[:, 0:1024], ((1,), (1,)))
    normed_grad = normed_grad + dot(pgb_ref[...], wh_ref[:, 1024:2048], ((1,), (1,)))
    unit = unit_ref[...].astype(F32)
    product = normed_grad * unit
    gain_sum[...] += jnp.sum(product, axis=0, keepdims=True)
    mean = jnp.mean(product * gain_ref[...], axis=-1, keepdims=True)
    summed_grad = inv_ref[...] * (normed_grad * gain_ref[...] - unit * mean)
    value_sum[...] += dot(st_ref[...], summed_grad.astype(BF))

    @pl.when(j == pl.num_programs(0) - 1)
    def _():
        value_grad = value_sum[...].astype(BF)
        keep_ref[:, 0:width] = dot(lat_turned[0:half, :], value_grad).astype(BF)
        send_ref[:, 0:width] = dot(lat_turned[half:, :], value_grad).astype(BF)
        gain_turned[...] = jnp.broadcast_to(gain_sum[...], (128, width)).T
        reorder(gain_turned, placed, own, ORDER_B)
        keep_ref[:, width:] = placed[0:half, :]
        send_ref[:, width:] = placed[half:, :]
        gl_ref[...] = dot(value_grad, wv_ref[...], ((1,), (1,))).astype(BF)


def whole(shape):
    return pl.BlockSpec(shape, lambda j: (0,) * len(shape))


def params():
    return pltpu.CompilerParams(vmem_limit_bytes=VMEM, dimension_semantics=("arbitrary",))


def cost(flops, moved):
    return pl.CostEstimate(flops=flops, bytes_accessed=moved, transcendentals=0)


def forward(lat, wv, nb, cf, emb, gain, wh, ow):
    nodes, width = lat.shape
    points = emb.shape[0]
    hidden = wh.shape[1]
    tile = pl.BlockSpec((points, 256), lambda j: (0, j))
    return pl.pallas_call(
        forward_kernel,
        grid=(hidden // 256,),
        in_specs=[
            whole(lat.shape), whole(wv.shape), whole(nb.shape), whole(cf.shape), whole(emb.shape), whole(gain.shape),
            pl.BlockSpec((width, 256), lambda j: (0, j)),
            pl.BlockSpec((ow.shape[0], 256), lambda j: (0, j)),
        ],
        out_specs=[
            whole((8, 104, 128)), tile, tile, whole((width, points)), whole((width, points)),
            whole((points, width)), whole((points, 1)), whole((nodes, points)),
        ],
        out_shape=[
            jax.ShapeDtypeStruct((8, 104, 128), F32),
            jax.ShapeDtypeStruct((points, hidden), BF),
            jax.ShapeDtypeStruct((points, hidden), BF),
            jax.ShapeDtypeStruct((width, points), BF),
            jax.ShapeDtypeStruct((width, points), BF),
            jax.ShapeDtypeStruct((points, width), BF),
            jax.ShapeDtypeStruct((points, 1), F32),
            jax.ShapeDtypeStruct((nodes, points), BF),
        ],
        scratch_shapes=[
            pltpu.VMEM((points, width), BF),
            pltpu.VMEM((104, points), F32),
            pltpu.VMEM((width, points), F32),
        ],
        compiler_params=params(),
        cost_estimate=cost(6_400_000_000, 30_000_000),
        name="forward",
    )(lat, wv, nb, cf, emb, gain, wh, ow)


def slopes_of(vc, f, r0, r1, r2, targets, vw, area):
    vm = pl.BlockSpec(memory_space=pltpu.VMEM)
    return pl.pallas_call(
        slopes_kernel,
        in_specs=[pl.BlockSpec(memory_space=pltpu.SMEM)] + [vm] * 7,
        out_specs=[vm, vm],
        out_shape=[jax.ShapeDtypeStruct((4, 112, 128), BF)] * 2,
        scratch_shapes=[pltpu.VMEM((8, 112, 128), F32)],
        compiler_params=pltpu.CompilerParams(vmem_limit_bytes=VMEM),
        cost_estimate=cost(20_000_000, 3_000_000),
        name="slopes",
    )(vc, f, r0, r1, r2, targets, vw, area)


def upper(last_piece, parts, ow, dg, hid, nt, go_first=None):
    points = dg.shape[0]
    width = nt.shape[0]
    first = 4 if last_piece else 0
    tiles = 5 if last_piece else 4
    col = (lambda j: (0, jnp.minimum(j, 3) + first)) if last_piece else (lambda j: (0, j))
    pg_col = (lambda j: (0, jnp.minimum(j, 3))) if last_piece else (lambda j: (0, j))
    piece = pl.BlockSpec((width // 2, 256), lambda j: (0, j))
    in_specs = [whole(p.shape) for p in parts] + [
        pl.BlockSpec((ow.shape[0], 256), col),
        pl.BlockSpec((points, 256), col),
        pl.BlockSpec((points, 256), col),
        whole(nt.shape),
    ]
    out_specs = [pl.BlockSpec((points, 256), pg_col), piece, piece]
    out_shape = [
        jax.ShapeDtypeStruct((points, 1024), BF),
        jax.ShapeDtypeStruct((width // 2, 256 * tiles), BF),
        jax.ShapeDtypeStruct((width // 2, 256 * tiles), BF),
    ]
    scratch = [pltpu.VMEM((128, points), BF), pltpu.VMEM((points, 128), BF), pltpu.VMEM((128, 256), BF)]
    args = [*parts, ow, dg, hid, nt]
    if last_piece:
        in_specs.append(whole(go_first.shape))
        args.append(go_first)
        scratch += [pltpu.VMEM((128, 1024), F32), pltpu.VMEM((2048, 128), F32)]
    else:
        out_specs.append(whole((128, 1024)))
        out_shape.append(jax.ShapeDtypeStruct((128, 1024), F32))
    return pl.pallas_call(
        lambda *refs: upper_kernel(last_piece, *refs),
        grid=(tiles,),
        in_specs=in_specs,
        out_specs=out_specs,
        out_shape=out_shape,
        scratch_shapes=scratch,
        compiler_params=params(),
        cost_estimate=cost(2_700_000_000, 12_000_000),
        name="upper_second" if last_piece else "upper_first",
    )(*args)


def lower(pga, pgb, wh, unit, inv, gain, st, lat, wv):
    points, width = unit.shape
    nodes = lat.shape[0]
    step = 256
    rows = lambda n: pl.BlockSpec((step, n), lambda j: (j, 0))
    return pl.pallas_call(
        lower_kernel,
        grid=(points // step,),
        in_specs=[
            rows(1024), rows(1024), whole(wh.shape), rows(width), rows(1), whole(gain.shape),
            pl.BlockSpec((nodes, step), lambda j: (0, j)), whole(lat.shape), whole(wv.shape),
        ],
        out_specs=[whole((width // 2, width + 128)), whole((width // 2, width + 128)), whole((nodes, width))],
        out_shape=[
            jax.ShapeDtypeStruct((width // 2, width + 128), BF),
            jax.ShapeDtypeStruct((width // 2, width + 128), BF),
            jax.ShapeDtypeStruct((nodes, width), BF),
        ],
        scratch_shapes=[
            pltpu.VMEM((1, width), F32),
            pltpu.VMEM((nodes, width), F32),
            pltpu.VMEM((width, nodes), F32),
            pltpu.VMEM((width, nodes), BF),
            pltpu.VMEM((width, 128), F32),
            pltpu.VMEM((width, 128), BF),
        ],
        compiler_params=params(),
        cost_estimate=cost(6_700_000_000, 16_000_000),
        name="lower",
    )(pga, pgb, wh, unit, inv, gain, st, lat, wv)


def permute(value, pairs):
    return lax.ppermute(value, AXES, pairs)


def summed_shard(keep, send, order):
    parts = [keep, permute(send, core_pairs())]
    rows = keep.shape[0]
    for axis in order:
        for step in range(2):
            rows //= 2
            out = sum(part[rows : 2 * rows].astype(F32) for part in parts).astype(BF)
            parts = [part[:rows] for part in parts] + [permute(out, ring_pairs(axis, step))]
    return sum(part.astype(F32) for part in parts)


def per_device(
    latents, grid_embed, neighbours, edge_coef, w_value, gain, w_hidden, output_weight,
    targets, var_weight, area, valid_counts,
):
    lat = latents[0]
    gain_row = gain[None, :]
    f, hid, dg, nta, ntb, unit, inv, st = forward(
        lat, w_value, neighbours, edge_coef, grid_embed, gain_row, w_hidden, output_weight
    )
    r0 = permute(f[4:8], core_pairs())
    r1 = permute(jnp.concatenate([f[2:4], r0[2:4]]), ring_pairs("x", 0))
    r2 = permute(jnp.stack([f[1], r0[1], r1[1], r1[3]]), ring_pairs("x", 1))
    keep, send = slopes_of(valid_counts, f, r0, r1, r2, targets, var_weight[:, None], area[None, :])
    q2 = permute(send, ring_pairs("x", 1))
    q1 = permute(jnp.concatenate([keep[2:4], q2[2:4]]), ring_pairs("x", 0))
    q0 = permute(jnp.stack([keep[1], q2[1], q1[1], q1[3]]), core_pairs())
    parts = [keep, q2, q1, q0]
    pga, a1_keep, a1_send, go = upper(False, parts, output_weight, dg, hid, nta)
    pgb, a2_keep, a2_send = upper(True, parts, output_weight, dg, hid, ntb, go)
    b_keep, b_send, grad_latents = lower(pga, pgb, w_hidden, unit, inv, gain_row, st, lat, w_value)
    a1 = summed_shard(a1_keep, a1_send, ORDER_A1)
    a2 = summed_shard(a2_keep, a2_send, ORDER_A2)
    b = summed_shard(b_keep, b_send, ORDER_B)
    grad_hidden = jnp.concatenate([a1, a2[:, :1024]], axis=1)
    out = a2[:, 1024:].reshape(8, 2, 128).transpose(2, 1, 0).reshape(128, 16)[:100]
    return (b[:, :1024], b[:, 1024], grad_hidden, out, grad_latents[None])


def solution(mesh):
    in_specs = (
        P("member", "node", None),
        P("node", None),
        P(None, "node"),
        P(None, "node"),
        P(),
        P(),
        P(),
        P(),
        P(None, "node"),
        P(),
        P("node"),
        P(),
    )
    out_specs = (
        P(("member", "node"), None),
        P(("member", "node")),
        P(("member", "node"), None),
        P(None, ("member", "node")),
        P("member", "node", None),
    )
    return jax.shard_map(
        per_device, mesh=mesh, in_specs=in_specs, out_specs=out_specs, check_vma=False
    )
```

time: 2030 us -> 164 us (0.08)
  waiting for transfers between devices: 1820 us -> 48.9 us
  blocking collectives: 66.6 us -> 0 us
  Pallas kernels: 0 us -> 64.4 us
  matrix products: 54.3 us -> 0 us
  other arithmetic: 46.5 us -> 2.16 us
  starting transfers between devices: 0.83 us -> 38.3 us
    reduce_scatter x2 -> x0, waiting for transfers between devices: 1150 us -> none  [the longest x1 648 us: per_device(): lax.psum_scatter(grad_hidden, ('member', 'node'), scatter_dimension=0, ti...]
    unnamed x5 -> x0, waiting for transfers between devices: 642 us -> none
    unnamed x1 -> x0, blocking collectives: 66.6 us -> none
    pallas_call x0 -> x5, Pallas kernels: none -> 64.4 us  [the longest x1 24.9 us: forward(): pl.pallas_call(forward_kernel, grid=(hidden // 256,), in_specs=[whole(lat...]
    dot_general x9 -> x0, matrix products: 54.3 us -> none  [the longest x1 11.4 us: backward_upper(): lax.dot_general(normalized_rows, pre_grad, (((0,), (0,)), ((), ())), pref...]
    ppermute x0 -> x27, waiting for transfers between devices: none -> 48.9 us  [permute(): return lax.ppermute(value, AXES, pairs)]
    ppermute x0 -> x27, starting transfers between devices: none -> 38.3 us  [permute(): return lax.ppermute(value, AXES, pairs)]
    all_gather x1 -> x0, waiting for transfers between devices: 29.9 us -> none  [per_device(): lax.all_gather(member_prediction[None], 'member', axis=0, tiled=True)]
  transfers between devices with their start and end apart: 4 -> 27, of which waited for: 4 -> 18; matrix products, arithmetic and copies ran while one was open for 4% -> 4% of each run, Pallas kernels for 0% -> 18%
where the time goes in v1:
time: 164 us
  Pallas kernels  64.4 us (39%)
  waiting for transfers between devices  48.9 us (30%)
  starting transfers between devices  38.3 us (23%)
  local copies, waits for them, and re-layouts  8.84 us (5%)
  other arithmetic  2.16 us (1%)
    ppermute x27, waiting for transfers between devices, permute(): return lax.ppermute(value, AXES, pairs)  48.9 us
    ppermute x27, starting transfers between devices, permute(): return lax.ppermute(value, AXES, pairs)  38.3 us
    pallas_call x1, Pallas kernels, forward(): pl.pallas_call(forward_kernel, grid=(hidden // 256,), in_specs=[whole(lat...  24.9 us
    pallas_call x1, Pallas kernels, lower(): pl.pallas_call(lower_kernel, grid=(points // step,), in_specs=[rows(1024)...  19.1 us
    pallas_call x2, Pallas kernels, upper(): pl.pallas_call(lambda *refs: upper_kernel(last_piece, *refs), grid=(tiles...  17.7 us
  transfers between devices with their start and end apart: 27, of which 18 were waited for; matrix products, arithmetic and copies ran while one was open for 4% of the time, Pallas kernels for 18%

profile of v1, /device:TPU:0, one launch (start us, length us, event | category | flops | bytes accessed | tf_op | source)
XLA Modules:
  0.0 163.5 jit_solution(13426958673833479518)
XLA Ops:
  0.6 24.9 %forward.1 = (f32[8,104,128]{2,1,0:T(8,128)}, bf16[1024,2048]{1,0:T(8,128)(2,1)}, bf16[1024,2048]{1,0:T(8,128)(2,1)}, bf16[1024,1024]{1,0:T(8,128)(2,1)}, bf16[1...) custom-call(bf16[384,1024]{1,0:T(8,128)(2,1)} %bitcast.13, ...), custom_call_target="tpu_custom_call" | custom-call | flops 6400000000 | bytes 30000000 | tf_op jit(solution)/shard_map/forward/pallas_call | solution.py:279
  25.6 1.0 slice.543
  26.5 0.1 collective-permute-start
  26.6 0.9 slice.544
  27.5 0.5 collective-permute-done.r0_ref
  28.1 1.7 %collective-permute-start.1 = (f32[4,104,128]{2,1,0:T(8,128)S(1)}, f32[4,104,128]{2,1,0:T(8,128)S(1)}, u32[]{:S(2)}, u32[]{:S(2)}) collective-permute-start(f32[4,104,128]{2,1,0:T(8,128)S(1)} %pad_maximum_fusion), channel_id=1, source_target_pairs={{0,32},{1,33},{2,34},{3,35},{4,36},{5,37},{6,38},{7,39},{8,40},{9,... | collective-permute-start | bytes 638984 | tf_op jit(solution)/shard_map/ppermute | solution.py:401
  29.8 0.8 slice.546
  30.6 3.5 %collective-permute-done.1.r1_ref = f32[4,104,128]{2,1,0:T(8,128)S(1)} collective-permute-done((f32[4,104,128]{2,1,0:T(8,128)S(1)}, f32[4,104,128]{2,1,0:T(8,128)S(1)}, u32[]{:S(2)}, u32[]{:S(2)}) %collective-permute-start.1) | collective-permute-done | bytes 213024 | tf_op jit(solution)/shard_map/ppermute | solution.py:401
  34.1 2.9 %collective-permute-start.2 = (f32[4,104,128]{2,1,0:T(8,128)S(1)}, f32[4,104,128]{2,1,0:T(8,128)S(1)}, u32[]{:S(2)}, u32[]{:S(2)}) collective-permute-start(f32[4,104,128]{2,1,0:T(8,128)S(1)} %pad_maximum_fusion.1), channel_id=1, source_target_pairs={{0,96},{1,97},{2,98},{3,99},{4,100},{5,101},{6,102},{7,103},{8,104... | collective-permute-start | bytes 638984 | tf_op jit(solution)/shard_map/ppermute | solution.py:401
  37.0 0.7 copy.18.vw_ref
  37.7 3.5 %collective-permute-done.2.r2_ref = f32[4,104,128]{2,1,0:T(8,128)S(1)} collective-permute-done((f32[4,104,128]{2,1,0:T(8,128)S(1)}, f32[4,104,128]{2,1,0:T(8,128)S(1)}, u32[]{:S(2)}, u32[]{:S(2)}) %collective-permute-start.2) | collective-permute-done | bytes 213024 | tf_op jit(solution)/shard_map/ppermute | solution.py:401
  41.2 0.7 copy-done.8
  41.9 2.6 %slopes.1 = (bf16[4,112,128]{2,1,0:T(8,128)(2,1)}, bf16[4,112,128]{2,1,0:T(8,128)(2,1)}) custom-call(s32[16]{0:T(128)} %vc_ref.1, f32[8,104,128]{2,1,0:T(8,128)} %get-tuple-element.25.f_ref, f32[4,104,128]{2,1,0:T(8,128)} %copy-done.5, f32[4,104,128]{2,1,0:T(8,128)} %copy-done.6, f32[4,104,128]{2,1,0:T(8,128)} %copy-done.8, f32[100,1024]{1,0:T(8,128)} %tg_ref.1, ...), custom_call_target="tpu_custom_call" | custom-call | flops 20000000 | bytes 3000000 | tf_op jit(solution)/shard_map/slopes/pallas_call | solution.py:314
  44.5 2.8 %collective-permute-start.3 = (bf16[4,112,128]{2,1,0:T(8,128)(2,1)}, bf16[4,112,128]{2,1,0:T(8,128)(2,1)S(1)}, u32[]{:S(2)}, u32[]{:S(2)}) collective-permute-start(bf16[4,112,128]{2,1,0:T(8,128)(2,1)} %get-tuple-element.27), channel_id=1, source_target_pairs={{0,96},{1,97},{2,98},{3,99},{4,100},{5,101},{6,102},{7,103},{8,104... | collective-permute-start | bytes 344072 | tf_op jit(solution)/shard_map/ppermute | solution.py:401
  47.4 0.8 slice.550
  48.2 2.9 %collective-permute-done.3.refs_1_ = bf16[4,112,128]{2,1,0:T(8,128)(2,1)S(1)} collective-permute-done((bf16[4,112,128]{2,1,0:T(8,128)(2,1)}, bf16[4,112,128]{2,1,0:T(8,128)(2,1)S(1)}, u32[]{:S(2)}, u32[]{:S(2)}) %collective-permute-start.3) | collective-permute-done | bytes 114720 | tf_op jit(solution)/shard_map/ppermute | solution.py:401
  51.1 0.1 collective-permute-start.4
  51.2 0.8 slice.552
  52.0 4.0 %collective-permute-done.4.refs_2_ = bf16[4,112,128]{2,1,0:T(8,128)(2,1)S(1)} collective-permute-done((bf16[4,112,128]{2,1,0:T(8,128)(2,1)S(1)}, bf16[4,112,128]{2,1,0:T(8,128)(2,1)S(1)}, u32[]{:S(2)}, u32[]{:S(2)}) %collective-permute-start.4) | collective-permute-done | bytes 114720 | tf_op jit(solution)/shard_map/ppermute | solution.py:401
  56.1 1.3 collective-permute-done.5.refs_3_
  57.4 0.6 copy-done.7
  58.1 7.6 %upper_first.1 = (bf16[1024,1024]{1,0:T(8,128)(2,1)}, bf16[512,1024]{1,0:T(8,128)(2,1)}, bf16[512,1024]{1,0:T(8,128)(2,1)}, f32[128,1024]{1,0:T(8,128)}) custom-call(bf16[4,112,128]{2,1,0:T(8,128)(2,1)} %get-tuple-element.26.refs_0_, bf16[4,112,128]{2,1,0:T(8,128)(2,1)} %copy-done.3, bf16[4,112,128]{2,1,0:T(8,128)(2,1)} %copy-done.4, ...), custom_call_target="tpu_custom_call" | custom-call | flops 2700000000 | bytes 12000000 | tf_op jit(solution)/shard_map/upper_first/pallas_call | solution.py:355
  65.6 0.2 collective-permute-start.13
  65.8 10.1 %upper_second.1 = (bf16[1024,1024]{1,0:T(8,128)(2,1)}, bf16[512,1280]{1,0:T(8,128)(2,1)}, bf16[512,1280]{1,0:T(8,128)(2,1)}) custom-call(bf16[4,112,128]{2,1,0:T(8,128)(2,1)} %get-tuple-element.26.refs_0_, bf16[4,112,128]{2,1,0:T(8,128)(2,1)} %copy-done.3, bf16[4,112,128]{2,1,0:T(8,128)(2,1)} %copy-done.4, bf16[4,112,128]{2,1,0:T(8,128)(2,1)} %copy-done.7, ...), custom_call_target="tpu_custom_call" | custom-call | flops 2700000000 | bytes 12000000 | tf_op jit(solution)/shard_map/upper_second/pallas_call | solution.py:355
  75.9 19.1 %lower.1 = (bf16[512,1152]{1,0:T(8,128)(2,1)}, bf16[512,1152]{1,0:T(8,128)(2,1)}, bf16[384,1024]{1,0:T(8,128)(2,1)}) custom-call(bf16[1024,1024]{1,0:T(8,128)(2,1)} %get-tuple-element.31.pga_ref, bf16[1024,1024]{1,0:T(8,128)(2,1)} %get-tuple-element.34.pgb_ref, bf16[1024,2048]{1,0:T(8,128)(2,1)} %wh_ref.3, bf16[1024,1024]{1,0:T(8,128)(2,1)} %get-tuple-element.35.unit_ref, ...), custom_call_target="tpu_custom_call" | custom-call | flops 6700000256 | bytes 16000000 | tf_op jit(solution)/shard_map/lower/pallas_call | solution.py:373
  95.1 0.4 collective-permute-start.6
  95.4 0.2 add_convert_fusion.2
  95.7 0.6 copy-done.10
  96.4 2.1 %collective-permute-start.20 = (bf16[512,1280]{1,0:T(8,128)(2,1)S(1)}, bf16[512,1280]{1,0:T(8,128)(2,1)S(1)}, u32[]{:S(2)}, u32[]{:S(2)}) collective-permute-start(bf16[512,1280]{1,0:T(8,128)(2,1)S(1)} %copy-done.10), channel_id=1, source_target_pairs={{0,16},{1,17},{2,18},{3,19},{4,20},{5,21},{6,22},{7,23},{8,24},{9,... | collective-permute-start | bytes 3932168 | tf_op jit(solution)/shard_map/ppermute | solution.py:401
  98.4 6.5 %collective-permute-done.14 = bf16[256,1024]{1,0:T(8,128)(2,1)S(1)} collective-permute-done((bf16[256,1024]{1,0:T(8,128)(2,1)S(1)}, bf16[256,1024]{1,0:T(8,128)(2,1)S(1)}, u32[]{:S(2)}, u32[]{:S(2)}) %collective-permute-start.14) | collective-permute-done | bytes 524320 | tf_op jit(solution)/shard_map/ppermute | solution.py:401
  104.9 0.1 add_convert_fusion.5
  105.0 2.9 %collective-permute-start.15 = (bf16[128,1024]{1,0:T(8,128)(2,1)S(1)}, bf16[128,1024]{1,0:T(8,128)(2,1)S(1)}, u32[]{:S(2)}, u32[]{:S(2)}) collective-permute-start(bf16[128,1024]{1,0:T(8,128)(2,1)S(1)} %add_convert_fusion.5), channel_id=1, source_target_pairs={{0,96},{1,97},{2,98},{3,99},{4,100},{5,101},{6,102},{7,103},{8,104... | collective-permute-start | bytes 786440 | tf_op jit(solution)/shard_map/ppermute | solution.py:401
  108.0 0.1 add_convert_fusion.1
  108.1 1.7 %collective-permute-start.7 = (bf16[256,1152]{1,0:T(8,128)(2,1)S(1)}, bf16[256,1152]{1,0:T(8,128)(2,1)S(1)}, u32[]{:S(2)}, u32[]{:S(2)}) collective-permute-start(bf16[256,1152]{1,0:T(8,128)(2,1)S(1)} %add_convert_fusion.1), channel_id=1, source_target_pairs={{0,1},{1,0},{2,3},{3,2},{4,5},{5,4},{6,7},{7,6},{8,9},{9,8},{10,11... | collective-permute-start | bytes 1769480 | tf_op jit(solution)/shard_map/ppermute | solution.py:401
  109.8 2.9 %collective-permute-done.15 = bf16[128,1024]{1,0:T(8,128)(2,1)S(1)} collective-permute-done((bf16[128,1024]{1,0:T(8,128)(2,1)S(1)}, bf16[128,1024]{1,0:T(8,128)(2,1)S(1)}, u32[]{:S(2)}, u32[]{:S(2)}) %collective-permute-start.15) | collective-permute-done | bytes 262176 | tf_op jit(solution)/shard_map/ppermute | solution.py:401
  112.8 2.1 %collective-permute-start.16 = (bf16[64,1024]{1,0:T(8,128)(2,1)S(1)}, bf16[64,1024]{1,0:T(8,128)(2,1)S(1)}, u32[]{:S(2)}, u32[]{:S(2)}) collective-permute-start(bf16[64,1024]{1,0:T(8,128)(2,1)S(1)} %add_convert_fusion.8), channel_id=1, source_target_pairs={{0,4},{1,5},{2,6},{3,7},{4,0},{5,1},{6,2},{7,3},{8,12},{9,13},{10,... | collective-permute-start | bytes 393224 | tf_op jit(solution)/shard_map/ppermute | solution.py:401
  114.9 0.2 add_convert_fusion
  115.0 0.1 collective-permute-start.21
  115.1 2.7 %collective-permute-done.16 = bf16[64,1024]{1,0:T(8,128)(2,1)S(1)} collective-permute-done((bf16[64,1024]{1,0:T(8,128)(2,1)S(1)}, bf16[64,1024]{1,0:T(8,128)(2,1)S(1)}, u32[]{:S(2)}, u32[]{:S(2)}) %collective-permute-start.16) | collective-permute-done | bytes 131104 | tf_op jit(solution)/shard_map/ppermute | solution.py:401
  117.9 4.2 %collective-permute-start.17 = (bf16[32,1024]{1,0:T(8,128)(2,1)S(1)}, bf16[32,1024]{1,0:T(8,128)(2,1)S(1)}, u32[]{:S(2)}, u32[]{:S(2)}) collective-permute-start(bf16[32,1024]{1,0:T(8,128)(2,1)S(1)} %add_convert_fusion.11), channel_id=1, source_target_pairs={{0,12},{1,13},{2,14},{3,15},{4,8},{5,9},{6,10},{7,11},{8,4},{9,5},... | collective-permute-start | bytes 196616 | tf_op jit(solution)/shard_map/ppermute | solution.py:401
  122.1 0.1 add_convert_fusion.4
  122.2 3.1 %collective-permute-start.8 = (bf16[128,1152]{1,0:T(8,128)(2,1)S(1)}, bf16[128,1152]{1,0:T(8,128)(2,1)S(1)}, u32[]{:S(2)}, u32[]{:S(2)}) collective-permute-start(bf16[128,1152]{1,0:T(8,128)(2,1)S(1)} %add_convert_fusion.4), channel_id=1, source_target_pairs={{0,3},{1,2},{2,1},{3,0},{4,7},{5,6},{6,5},{7,4},{8,11},{9,10},{10,... | collective-permute-start | bytes 884744 | tf_op jit(solution)/shard_map/ppermute | solution.py:401
  125.3 1.4 collective-permute-start.18
  126.8 0.1 add_convert_fusion.3
  126.9 3.1 %collective-permute-start.22 = (bf16[128,1280]{1,0:T(8,128)(2,1)S(1)}, bf16[128,1280]{1,0:T(8,128)(2,1)S(1)}, u32[]{:S(2)}, u32[]{:S(2)}) collective-permute-start(bf16[128,1280]{1,0:T(8,128)(2,1)S(1)} %add_convert_fusion.3), channel_id=1, source_target_pairs={{0,12},{1,13},{2,14},{3,15},{4,8},{5,9},{6,10},{7,11},{8,4},{9,5},... | collective-permute-start | bytes 983048 | tf_op jit(solution)/shard_map/ppermute | solution.py:401
  130.0 3.0 %collective-permute-start.19 = (bf16[8,1024]{1,0:T(8,128)(2,1)S(1)}, bf16[8,1024]{1,0:T(8,128)(2,1)S(1)}, u32[]{:S(2)}, u32[]{:S(2)}) collective-permute-start(bf16[8,1024]{1,0:T(8,128)(2,1)S(1)} %add_convert_fusion.17), channel_id=1, source_target_pairs={{0,3},{1,2},{2,1},{3,0},{4,7},{5,6},{6,5},{7,4},{8,11},{9,10},{10,... | collective-permute-start | bytes 49160 | tf_op jit(solution)/shard_map/ppermute | solution.py:401
  133.2 1.8 %collective-permute-done.19 = bf16[8,1024]{1,0:T(8,128)(2,1)S(1)} collective-permute-done((bf16[8,1024]{1,0:T(8,128)(2,1)S(1)}, bf16[8,1024]{1,0:T(8,128)(2,1)S(1)}, u32[]{:S(2)}, u32[]{:S(2)}) %collective-permute-start.19) | collective-permute-done | bytes 16416 | tf_op jit(solution)/shard_map/ppermute | solution.py:401
  135.0 3.8 %collective-permute-done.9 = bf16[64,1152]{1,0:T(8,128)(2,1)S(1)} collective-permute-done((bf16[64,1152]{1,0:T(8,128)(2,1)S(1)}, bf16[64,1152]{1,0:T(8,128)(2,1)S(1)}, u32[]{:S(2)}, u32[]{:S(2)}) %collective-permute-start.9) | collective-permute-done | bytes 147488 | tf_op jit(solution)/shard_map/ppermute | solution.py:401
  138.9 2.8 %collective-permute-start.10 = (bf16[32,1152]{1,0:T(8,128)(2,1)S(1)}, bf16[32,1152]{1,0:T(8,128)(2,1)S(1)}, u32[]{:S(2)}, u32[]{:S(2)}) collective-permute-start(bf16[32,1152]{1,0:T(8,128)(2,1)S(1)} %add_convert_fusion.10), channel_id=1, source_target_pairs={{0,96},{1,97},{2,98},{3,99},{4,100},{5,101},{6,102},{7,103},{8,104... | collective-permute-start | bytes 221192 | tf_op jit(solution)/shard_map/ppermute | solution.py:401
  141.8 0.5 collective-permute-start.23
  142.3 2.2 %collective-permute-done.10 = bf16[32,1152]{1,0:T(8,128)(2,1)S(1)} collective-permute-done((bf16[32,1152]{1,0:T(8,128)(2,1)S(1)}, bf16[32,1152]{1,0:T(8,128)(2,1)S(1)}, u32[]{:S(2)}, u32[]{:S(2)}) %collective-permute-start.10) | collective-permute-done | bytes 73760 | tf_op jit(solution)/shard_map/ppermute | solution.py:401
  144.6 0.3 collective-permute-start.11
  144.9 2.3 %collective-permute-done.23 = bf16[64,1280]{1,0:T(8,128)(2,1)S(1)} collective-permute-done((bf16[64,1280]{1,0:T(8,128)(2,1)S(1)}, bf16[64,1280]{1,0:T(8,128)(2,1)S(1)}, u32[]{:S(2)}, u32[]{:S(2)}) %collective-permute-start.23) | collective-permute-done | bytes 163872 | tf_op jit(solution)/shard_map/ppermute | solution.py:401
  147.4 1.2 collective-permute-done.11
  148.6 1.9 %collective-permute-start.12 = (bf16[8,1152]{1,0:T(8,128)(2,1)S(1)}, bf16[8,1152]{1,0:T(8,128)(2,1)S(1)}, u32[]{:S(2)}, u32[]{:S(2)}) collective-permute-start(bf16[8,1152]{1,0:T(8,128)(2,1)S(1)} %add_convert_fusion.16), channel_id=1, source_target_pairs={{0,12},{1,13},{2,14},{3,15},{4,8},{5,9},{6,10},{7,11},{8,4},{9,5},... | collective-permute-start | bytes 55304 | tf_op jit(solution)/shard_map/ppermute | solution.py:401
  150.5 2.5 %collective-permute-done.24 = bf16[32,1280]{1,0:T(8,128)(2,1)S(1)} collective-permute-done((bf16[32,1280]{1,0:T(8,128)(2,1)S(1)}, bf16[32,1280]{1,0:T(8,128)(2,1)S(1)}, u32[]{:S(2)}, u32[]{:S(2)}) %collective-permute-start.24) | collective-permute-done | bytes 81952 | tf_op jit(solution)/shard_map/ppermute | solution.py:401
  153.1 0.6 collective-permute-done.12
  153.7 3.4 %collective-permute-done.25 = bf16[16,1280]{1,0:T(8,128)(2,1)S(1)} collective-permute-done((bf16[16,1280]{1,0:T(8,128)(2,1)S(1)}, bf16[16,1280]{1,0:T(8,128)(2,1)S(1)}, u32[]{:S(2)}, u32[]{:S(2)}) %collective-permute-start.25) | collective-permute-done | bytes 40992 | tf_op jit(solution)/shard_map/ppermute | solution.py:401
  157.1 0.6 collective-permute-start.26
  157.7 0.6 slice_reduce_fusion
  158.3 0.6 slice.699
  158.9 3.3 %collective-permute-done.26 = bf16[8,1280]{1,0:T(8,128)(2,1)S(1)} collective-permute-done((bf16[8,1280]{1,0:T(8,128)(2,1)S(1)}, bf16[8,1280]{1,0:T(8,128)(2,1)S(1)}, u32[]{:S(2)}, u32[]{:S(2)}) %collective-permute-start.26) | collective-permute-done | bytes 20512 | tf_op jit(solution)/shard_map/ppermute | solution.py:401
  162.3 0.6 slice_bitcast_fusion
  162.9 0.6 pad_maximum_fusion.4
  (60 shorter events, 1.2 us)
Async XLA Ops:
  25.6 11.4 %copy-start.9 = (f32[100]{0:T(128)S(1)}, f32[100]{0:T(128)}, u32[]{:S(2)}) copy-start(f32[100]{0:T(128)} %param.21) | copy-start | bytes 1204
  26.5 1.5 collective-permute-start
  28.1 13.1 %copy-start.5 = (f32[4,104,128]{2,1,0:T(8,128)}, f32[4,104,128]{2,1,0:T(8,128)S(1)}, u32[]{:S(2)}) copy-start(f32[4,104,128]{2,1,0:T(8,128)S(1)} %collective-permute-done.r0_ref) | copy-start | bytes 638980
  28.1 5.9 %collective-permute-start.1 = (f32[4,104,128]{2,1,0:T(8,128)S(1)}, f32[4,104,128]{2,1,0:T(8,128)S(1)}, u32[]{:S(2)}, u32[]{:S(2)}) collective-permute-start(f32[4,104,128]{2,1,0:T(8,128)S(1)} %pad_maximum_fusion), channel_id=1, source_target_pairs={{0,32},{1,33},{2,34},{3,35},{4,36},{5,37},{6,38},{7,39},{8,40},{9,... | collective-permute-start | bytes 638984 | tf_op jit(solution)/shard_map/ppermute | solution.py:401
  34.0 7.2 %copy-start.6 = (f32[4,104,128]{2,1,0:T(8,128)}, f32[4,104,128]{2,1,0:T(8,128)S(1)}, u32[]{:S(2)}) copy-start(f32[4,104,128]{2,1,0:T(8,128)S(1)} %collective-permute-done.1.r1_ref) | copy-start | bytes 638980
  34.1 7.1 %collective-permute-start.2 = (f32[4,104,128]{2,1,0:T(8,128)S(1)}, f32[4,104,128]{2,1,0:T(8,128)S(1)}, u32[]{:S(2)}, u32[]{:S(2)}) collective-permute-start(f32[4,104,128]{2,1,0:T(8,128)S(1)} %pad_maximum_fusion.1), channel_id=1, source_target_pairs={{0,96},{1,97},{2,98},{3,99},{4,100},{5,101},{6,102},{7,103},{8,104... | collective-permute-start | bytes 638984 | tf_op jit(solution)/shard_map/ppermute | solution.py:401
  41.2 0.7 copy-start.8
  44.5 6.5 %collective-permute-start.3 = (bf16[4,112,128]{2,1,0:T(8,128)(2,1)}, bf16[4,112,128]{2,1,0:T(8,128)(2,1)S(1)}, u32[]{:S(2)}, u32[]{:S(2)}) collective-permute-start(bf16[4,112,128]{2,1,0:T(8,128)(2,1)} %get-tuple-element.27), channel_id=1, source_target_pairs={{0,96},{1,97},{2,98},{3,99},{4,100},{5,101},{6,102},{7,103},{8,104... | collective-permute-start | bytes 344072 | tf_op jit(solution)/shard_map/ppermute | solution.py:401
  51.1 6.3 %copy-start.3 = (bf16[4,112,128]{2,1,0:T(8,128)(2,1)}, bf16[4,112,128]{2,1,0:T(8,128)(2,1)S(1)}, u32[]{:S(2)}) copy-start(bf16[4,112,128]{2,1,0:T(8,128)(2,1)S(1)} %collective-permute-done.3.refs_1_) | copy-start | bytes 344068
  51.1 4.9 %collective-permute-start.4 = (bf16[4,112,128]{2,1,0:T(8,128)(2,1)S(1)}, bf16[4,112,128]{2,1,0:T(8,128)(2,1)S(1)}, u32[]{:S(2)}, u32[]{:S(2)}) collective-permute-start(bf16[4,112,128]{2,1,0:T(8,128)(2,1)S(1)} %pad_maximum_fusion.2), channel_id=1, source_target_pairs={{0,32},{1,33},{2,34},{3,35},{4,36},{5,37},{6,38},{7,39},{8,40},{9,... | collective-permute-start | bytes 344072 | tf_op jit(solution)/shard_map/ppermute | solution.py:401
  56.0 1.4 copy-start.4
  56.0 1.4 collective-permute-start.5
  57.4 0.6 copy-start.7
  65.6 29.8 %collective-permute-start.13 = (bf16[512,1024]{1,0:T(8,128)(2,1)}, bf16[512,1024]{1,0:T(8,128)(2,1)S(1)}, u32[]{:S(2)}, u32[]{:S(2)}) collective-permute-start(bf16[512,1024]{1,0:T(8,128)(2,1)} %get-tuple-element.41), channel_id=1, source_target_pairs={{0,16},{1,17},{2,18},{3,19},{4,20},{5,21},{6,22},{7,23},{8,24},{9,... | collective-permute-start | bytes 3145736 | tf_op jit(solution)/shard_map/ppermute | solution.py:401
  75.9 19.5 %copy-start.2 = (bf16[512,1024]{1,0:T(8,128)(2,1)S(1)}, bf16[512,1024]{1,0:T(8,128)(2,1)}, u32[]{:S(2)}) copy-start(bf16[512,1024]{1,0:T(8,128)(2,1)} %get-tuple-element.40) | copy-start | bytes 3145732
  95.0 1.3 copy-start.10
  95.1 12.9 %collective-permute-start.6 = (bf16[512,1152]{1,0:T(8,128)(2,1)}, bf16[512,1152]{1,0:T(8,128)(2,1)S(1)}, u32[]{:S(2)}, u32[]{:S(2)}) collective-permute-start(bf16[512,1152]{1,0:T(8,128)(2,1)} %get-tuple-element.39), channel_id=1, source_target_pairs={{0,16},{1,17},{2,18},{3,19},{4,20},{5,21},{6,22},{7,23},{8,24},{9,... | collective-permute-start | bytes 3538952 | tf_op jit(solution)/shard_map/ppermute | solution.py:401
  95.4 12.5 %copy-start.1 = (bf16[512,1152]{1,0:T(8,128)(2,1)S(1)}, bf16[512,1152]{1,0:T(8,128)(2,1)}, u32[]{:S(2)}) copy-start(bf16[512,1152]{1,0:T(8,128)(2,1)} %get-tuple-element.38) | copy-start | bytes 3538948
  95.6 9.3 %collective-permute-start.14 = (bf16[256,1024]{1,0:T(8,128)(2,1)S(1)}, bf16[256,1024]{1,0:T(8,128)(2,1)S(1)}, u32[]{:S(2)}, u32[]{:S(2)}) collective-permute-start(bf16[256,1024]{1,0:T(8,128)(2,1)S(1)} %add_convert_fusion.2), channel_id=1, source_target_pairs={{0,32},{1,33},{2,34},{3,35},{4,36},{5,37},{6,38},{7,39},{8,40},{9,... | collective-permute-start | bytes 1572872 | tf_op jit(solution)/shard_map/ppermute | solution.py:401
  96.4 18.5 %collective-permute-start.20 = (bf16[512,1280]{1,0:T(8,128)(2,1)S(1)}, bf16[512,1280]{1,0:T(8,128)(2,1)S(1)}, u32[]{:S(2)}, u32[]{:S(2)}) collective-permute-start(bf16[512,1280]{1,0:T(8,128)(2,1)S(1)} %copy-done.10), channel_id=1, source_target_pairs={{0,16},{1,17},{2,18},{3,19},{4,20},{5,21},{6,22},{7,23},{8,24},{9,... | collective-permute-start | bytes 3932168 | tf_op jit(solution)/shard_map/ppermute | solution.py:401
  105.0 9.8 %copy-start = (bf16[512,1280]{1,0:T(8,128)(2,1)S(1)}, bf16[512,1280]{1,0:T(8,128)(2,1)}, u32[]{:S(2)}) copy-start(bf16[512,1280]{1,0:T(8,128)(2,1)} %get-tuple-element.42) | copy-start | bytes 3932164
  105.0 7.7 %collective-permute-start.15 = (bf16[128,1024]{1,0:T(8,128)(2,1)S(1)}, bf16[128,1024]{1,0:T(8,128)(2,1)S(1)}, u32[]{:S(2)}, u32[]{:S(2)}) collective-permute-start(bf16[128,1024]{1,0:T(8,128)(2,1)S(1)} %add_convert_fusion.5), channel_id=1, source_target_pairs={{0,96},{1,97},{2,98},{3,99},{4,100},{5,101},{6,102},{7,103},{8,104... | collective-permute-start | bytes 786440 | tf_op jit(solution)/shard_map/ppermute | solution.py:401
  108.1 14.0 %collective-permute-start.7 = (bf16[256,1152]{1,0:T(8,128)(2,1)S(1)}, bf16[256,1152]{1,0:T(8,128)(2,1)S(1)}, u32[]{:S(2)}, u32[]{:S(2)}) collective-permute-start(bf16[256,1152]{1,0:T(8,128)(2,1)S(1)} %add_convert_fusion.1), channel_id=1, source_target_pairs={{0,1},{1,0},{2,3},{3,2},{4,5},{5,4},{6,7},{7,6},{8,9},{9,8},{10,11... | collective-permute-start | bytes 1769480 | tf_op jit(solution)/shard_map/ppermute | solution.py:401
  112.8 5.0 %collective-permute-start.16 = (bf16[64,1024]{1,0:T(8,128)(2,1)S(1)}, bf16[64,1024]{1,0:T(8,128)(2,1)S(1)}, u32[]{:S(2)}, u32[]{:S(2)}) collective-permute-start(bf16[64,1024]{1,0:T(8,128)(2,1)S(1)} %add_convert_fusion.8), channel_id=1, source_target_pairs={{0,4},{1,5},{2,6},{3,7},{4,0},{5,1},{6,2},{7,3},{8,12},{9,13},{10,... | collective-permute-start | bytes 393224 | tf_op jit(solution)/shard_map/ppermute | solution.py:401
  115.0 11.8 %collective-permute-start.21 = (bf16[256,1280]{1,0:T(8,128)(2,1)S(1)}, bf16[256,1280]{1,0:T(8,128)(2,1)S(1)}, u32[]{:S(2)}, u32[]{:S(2)}) collective-permute-start(bf16[256,1280]{1,0:T(8,128)(2,1)S(1)} %add_convert_fusion), channel_id=1, source_target_pairs={{0,4},{1,5},{2,6},{3,7},{4,0},{5,1},{6,2},{7,3},{8,12},{9,13},{10,... | collective-permute-start | bytes 1966088 | tf_op jit(solution)/shard_map/ppermute | solution.py:401
  117.9 7.4 %collective-permute-start.17 = (bf16[32,1024]{1,0:T(8,128)(2,1)S(1)}, bf16[32,1024]{1,0:T(8,128)(2,1)S(1)}, u32[]{:S(2)}, u32[]{:S(2)}) collective-permute-start(bf16[32,1024]{1,0:T(8,128)(2,1)S(1)} %add_convert_fusion.11), channel_id=1, source_target_pairs={{0,12},{1,13},{2,14},{3,15},{4,8},{5,9},{6,10},{7,11},{8,4},{9,5},... | collective-permute-start | bytes 196616 | tf_op jit(solution)/shard_map/ppermute | solution.py:401
  122.2 10.8 %collective-permute-start.8 = (bf16[128,1152]{1,0:T(8,128)(2,1)S(1)}, bf16[128,1152]{1,0:T(8,128)(2,1)S(1)}, u32[]{:S(2)}, u32[]{:S(2)}) collective-permute-start(bf16[128,1152]{1,0:T(8,128)(2,1)S(1)} %add_convert_fusion.4), channel_id=1, source_target_pairs={{0,3},{1,2},{2,1},{3,0},{4,7},{5,6},{6,5},{7,4},{8,11},{9,10},{10,... | collective-permute-start | bytes 884744 | tf_op jit(solution)/shard_map/ppermute | solution.py:401
  125.3 4.6 %collective-permute-start.18 = (bf16[16,1024]{1,0:T(8,128)(2,1)S(1)}, bf16[16,1024]{1,0:T(8,128)(2,1)S(1)}, u32[]{:S(2)}, u32[]{:S(2)}) collective-permute-start(bf16[16,1024]{1,0:T(8,128)(2,1)S(1)} %add_convert_fusion.14), channel_id=1, source_target_pairs={{0,1},{1,0},{2,3},{3,2},{4,5},{5,4},{6,7},{7,6},{8,9},{9,8},{10,11... | collective-permute-start | bytes 98312 | tf_op jit(solution)/shard_map/ppermute | solution.py:401
  126.9 14.8 %collective-permute-start.22 = (bf16[128,1280]{1,0:T(8,128)(2,1)S(1)}, bf16[128,1280]{1,0:T(8,128)(2,1)S(1)}, u32[]{:S(2)}, u32[]{:S(2)}) collective-permute-start(bf16[128,1280]{1,0:T(8,128)(2,1)S(1)} %add_convert_fusion.3), channel_id=1, source_target_pairs={{0,12},{1,13},{2,14},{3,15},{4,8},{5,9},{6,10},{7,11},{8,4},{9,5},... | collective-permute-start | bytes 983048 | tf_op jit(solution)/shard_map/ppermute | solution.py:401
  130.0 5.0 %collective-permute-start.19 = (bf16[8,1024]{1,0:T(8,128)(2,1)S(1)}, bf16[8,1024]{1,0:T(8,128)(2,1)S(1)}, u32[]{:S(2)}, u32[]{:S(2)}) collective-permute-start(bf16[8,1024]{1,0:T(8,128)(2,1)S(1)} %add_convert_fusion.17), channel_id=1, source_target_pairs={{0,3},{1,2},{2,1},{3,0},{4,7},{5,6},{6,5},{7,4},{8,11},{9,10},{10,... | collective-permute-start | bytes 49160 | tf_op jit(solution)/shard_map/ppermute | solution.py:401
  133.1 5.8 %collective-permute-start.9 = (bf16[64,1152]{1,0:T(8,128)(2,1)S(1)}, bf16[64,1152]{1,0:T(8,128)(2,1)S(1)}, u32[]{:S(2)}, u32[]{:S(2)}) collective-permute-start(bf16[64,1152]{1,0:T(8,128)(2,1)S(1)} %add_convert_fusion.7), channel_id=1, source_target_pairs={{0,32},{1,33},{2,34},{3,35},{4,36},{5,37},{6,38},{7,39},{8,40},{9,... | collective-permute-start | bytes 442376 | tf_op jit(solution)/shard_map/ppermute | solution.py:401
  138.9 5.6 %collective-permute-start.10 = (bf16[32,1152]{1,0:T(8,128)(2,1)S(1)}, bf16[32,1152]{1,0:T(8,128)(2,1)S(1)}, u32[]{:S(2)}, u32[]{:S(2)}) collective-permute-start(bf16[32,1152]{1,0:T(8,128)(2,1)S(1)} %add_convert_fusion.10), channel_id=1, source_target_pairs={{0,96},{1,97},{2,98},{3,99},{4,100},{5,101},{6,102},{7,103},{8,104... | collective-permute-start | bytes 221192 | tf_op jit(solution)/shard_map/ppermute | solution.py:401
  141.8 5.4 %collective-permute-start.23 = (bf16[64,1280]{1,0:T(8,128)(2,1)S(1)}, bf16[64,1280]{1,0:T(8,128)(2,1)S(1)}, u32[]{:S(2)}, u32[]{:S(2)}) collective-permute-start(bf16[64,1280]{1,0:T(8,128)(2,1)S(1)} %add_convert_fusion.6), channel_id=1, source_target_pairs={{0,1},{1,0},{2,3},{3,2},{4,5},{5,4},{6,7},{7,6},{8,9},{9,8},{10,11... | collective-permute-start | bytes 491528 | tf_op jit(solution)/shard_map/ppermute | solution.py:401
  144.6 4.0 %collective-permute-start.11 = (bf16[16,1152]{1,0:T(8,128)(2,1)S(1)}, bf16[16,1152]{1,0:T(8,128)(2,1)S(1)}, u32[]{:S(2)}, u32[]{:S(2)}) collective-permute-start(bf16[16,1152]{1,0:T(8,128)(2,1)S(1)} %add_convert_fusion.13), channel_id=1, source_target_pairs={{0,4},{1,5},{2,6},{3,7},{4,0},{5,1},{6,2},{7,3},{8,12},{9,13},{10,... | collective-permute-start | bytes 110600 | tf_op jit(solution)/shard_map/ppermute | solution.py:401
  147.3 5.7 %collective-permute-start.24 = (bf16[32,1280]{1,0:T(8,128)(2,1)S(1)}, bf16[32,1280]{1,0:T(8,128)(2,1)S(1)}, u32[]{:S(2)}, u32[]{:S(2)}) collective-permute-start(bf16[32,1280]{1,0:T(8,128)(2,1)S(1)} %add_convert_fusion.9), channel_id=1, source_target_pairs={{0,3},{1,2},{2,1},{3,0},{4,7},{5,6},{6,5},{7,4},{8,11},{9,10},{10,... | collective-permute-start | bytes 245768 | tf_op jit(solution)/shard_map/ppermute | solution.py:401
  148.6 5.1 %collective-permute-start.12 = (bf16[8,1152]{1,0:T(8,128)(2,1)S(1)}, bf16[8,1152]{1,0:T(8,128)(2,1)S(1)}, u32[]{:S(2)}, u32[]{:S(2)}) collective-permute-start(bf16[8,1152]{1,0:T(8,128)(2,1)S(1)} %add_convert_fusion.16), channel_id=1, source_target_pairs={{0,12},{1,13},{2,14},{3,15},{4,8},{5,9},{6,10},{7,11},{8,4},{9,5},... | collective-permute-start | bytes 55304 | tf_op jit(solution)/shard_map/ppermute | solution.py:401
  153.0 4.1 %collective-permute-start.25 = (bf16[16,1280]{1,0:T(8,128)(2,1)S(1)}, bf16[16,1280]{1,0:T(8,128)(2,1)S(1)}, u32[]{:S(2)}, u32[]{:S(2)}) collective-permute-start(bf16[16,1280]{1,0:T(8,128)(2,1)S(1)} %add_convert_fusion.12), channel_id=1, source_target_pairs={{0,32},{1,33},{2,34},{3,35},{4,36},{5,37},{6,38},{7,39},{8,40},{9,... | collective-permute-start | bytes 122888 | tf_op jit(solution)/shard_map/ppermute | solution.py:401
  157.1 5.1 %collective-permute-start.26 = (bf16[8,1280]{1,0:T(8,128)(2,1)S(1)}, bf16[8,1280]{1,0:T(8,128)(2,1)S(1)}, u32[]{:S(2)}, u32[]{:S(2)}) collective-permute-start(bf16[8,1280]{1,0:T(8,128)(2,1)S(1)} %add_convert_fusion.15), channel_id=1, source_target_pairs={{0,96},{1,97},{2,98},{3,99},{4,100},{5,101},{6,102},{7,103},{8,104... | collective-permute-start | bytes 61448 | tf_op jit(solution)/shard_map/ppermute | solution.py:401

commit v2 on v0

v2 whole, which is shorter than its diff:
```python
import itertools

import jax
import jax.numpy as jnp
from jax import lax
from jax.experimental import pallas as pl
from jax.experimental.pallas import tpu as pltpu
from jax.sharding import PartitionSpec as P

BF = jnp.bfloat16
F32 = jnp.float32
kernel_width = 0.25
fair_alpha = 0.95
norm_eps = 1e-05
members = 8
GELU_C = 0.7978845608028654
VMEM = 56 * 1024 * 1024
CORE_AXES = ("x", "z", "y")
AXES = ("x", "core", "z", "y")


def flat(x, c, z, y):
    return ((x * 2 + c) * 4 + z) * 4 + y


def core_pairs():
    return [
        (flat(x, c, z, y), flat(x, 1 - c, z, y))
        for x, c, z, y in itertools.product(range(4), range(2), range(4), range(4))
    ]


def ring_pairs(axis):
    pairs = []
    for x, c, z, y in itertools.product(range(4), range(2), range(4), range(4)):
        to = {"x": x, "z": z, "y": y}
        to[axis] ^= (1, 3)[c]
        pairs.append((flat(x, c, z, y), flat(to["x"], c, to["z"], to["y"])))
    return pairs


def own_place():
    return {"x": lax.axis_index("x"), "c": lax.axis_index("core"), "z": lax.axis_index("z"), "y": lax.axis_index("y")}


def masks(core):
    first, second = 1 + 2 * core, 3 - 2 * core
    return (0, second, first, 2)


def x_pairs(position):
    pairs = []
    for x, c, z, y in itertools.product(range(4), range(2), range(4), range(4)):
        pairs.append((flat(x, c, z, y), flat(x ^ masks(c)[position], c, z, y)))
    return pairs


def dot(a, b, dims=((1,), (0,))):
    return lax.dot_general(a, b, (dims, ((), ())), preferred_element_type=F32)


def forward_kernel(
    lat_ref, wv_ref, nb_ref, cf_ref, emb_hbm, gain_ref, wh_ref, ow_ref,
    f0, f1, f2, f3, hid_ref, dg_ref, nrm_hbm, inv_ref, st_ref, lat_send,
    nrm, total, emb, sems,
):
    j = pl.program_id(0)
    nodes, points = st_ref.shape
    own = own_place()
    save = pltpu.make_async_copy(nrm, nrm_hbm, sems.at[1])

    @pl.when(j == 0)
    def _():
        load = pltpu.make_async_copy(emb_hbm, emb, sems.at[0])
        load.start()
        values = dot(lat_ref[...], wv_ref[...]).astype(BF)
        rows_of = lax.broadcasted_iota(jnp.int32, (nodes, 256), 0)
        for r in range(points // 256):
            rows = slice(256 * r, 256 * r + 256)
            st = jnp.zeros((nodes, 256), F32)
            for k in range(3):
                st = st + jnp.where(nb_ref[k : k + 1, rows] == rows_of, cf_ref[k : k + 1, rows], 0.0)
            st_ref[:, rows] = st.astype(BF)
        load.wait()
        for r in range(points // 256):
            rows = slice(256 * r, 256 * r + 256)
            summed = emb[rows, :].astype(F32) + dot(st_ref[:, rows], values, ((0,), (0,)))
            inv = lax.rsqrt(jnp.mean(summed * summed, axis=-1, keepdims=True) + norm_eps)
            inv_ref[rows, :] = inv
            nrm[rows, :] = (summed * inv * gain_ref[...]).astype(BF)
        save.start()
        total[...] = jnp.zeros_like(total)
        for x in range(4):
            columns = pl.ds(pl.multiple_of(x * 256 + (1 - own["c"]) * 128, 128), 128)
            lat_send[:, 128 * x : 128 * x + 128] = lat_ref[:, columns]

    step = 256
    for r in range(points // step):
        rows = slice(step * r, step * r + step)
        pre = dot(nrm[rows, :], wh_ref[...])
        square = pre * pre
        t = jnp.tanh(pre * (GELU_C + (GELU_C * 0.044715) * square))
        half = 0.5 * pre
        hid_ref[rows, :] = (half * t + half).astype(BF)
        slope = 0.5 + 0.5 * t + half * (1.0 - t * t) * (GELU_C + (3 * GELU_C * 0.044715) * square)
        dg_ref[rows, :] = slope.astype(BF)
    total[0:100, :] += dot(ow_ref[...], hid_ref[...], ((1,), (1,)))

    @pl.when(j == pl.num_programs(0) - 1)
    def _():
        for f, m in zip((f0, f1, f2, f3), masks(own["c"])):
            f[...] = total[:, pl.ds(pl.multiple_of((own["x"] ^ m) * 256, 256), 256)]
        save.wait()


def slopes_kernel(
    vc_ref, f0, f1, f2, f3, c0, c1, c2, c3, tg_ref, vw_ref, area_ref, s0, s1, s2, s3, held
):
    own = own_place()
    first = pl.multiple_of(own["x"] * 256, 256)
    spread = (1.0 - (1.0 - fair_alpha) / members) / (2.0 * members * (members - 1))
    held[:, 96:112, :] = jnp.zeros((4, 16, 256), F32)
    limit = vc_ref[own["z"] * 4 + own["y"]]
    for part in range(2):
        mine = pl.ds(pl.multiple_of(first + 128 * part, 128), 128)
        here = slice(128 * part, 128 * part + 128)
        place = first + 128 * part + lax.broadcasted_iota(jnp.int32, (1, 128), 1)
        live = jnp.where(place < limit, area_ref[:, mine], 0.0)
        for top in range(0, 100, 8):
            rows = slice(top, min(top + 8, 100))
            f = [field[rows, here] for field in (f0, f1, f2, f3, c0, c1, c2, c3)]
            sums = [jnp.zeros_like(f[0]) for _ in range(4)]
            for a in range(4):
                for b in range(a + 1, 8):
                    d = f[a] - f[b]
                    s = d * lax.rsqrt(d * d + kernel_width * kernel_width)
                    sums[a] = sums[a] + s
                    if b < 4:
                        sums[b] = sums[b] - s
            target = tg_ref[rows, mine]
            weight = vw_ref[rows, :] * live * 0.01
            for a in range(4):
                d = f[a] - target
                s = d * lax.rsqrt(d * d + kernel_width * kernel_width)
                held[a, rows, here] = weight * (s * (1.0 / members) - 2.0 * spread * sums[a])
    for a, s in enumerate((s0, s1, s2, s3)):
        s[...] = held[a].astype(BF)


def upper_kernel(
    s0, s1, s2, s3, ow_ref, dg_ref, hid_ref, nrm_ref,
    pg_ref, keep_ref, send_ref, go_keep, go_send,
    slopes, own_w, go, result,
):
    j = pl.program_id(0)
    points, wide = dg_ref.shape
    half = keep_ref.shape[0]
    own = own_place()

    @pl.when(j == 0)
    def _():
        for s, m in zip((s0, s1, s2, s3), masks(own["c"])):
            at = pl.ds(pl.multiple_of((own["x"] ^ m) * 256, 256), 256)
            slopes[0:112, at] = s[...]
        slopes[112:128, :] = jnp.zeros((16, points), BF)
        own_w[...] = jnp.zeros_like(own_w)

    own_w[0:100, :] = ow_ref[...]
    for r in range(points // 256):
        rows = slice(256 * r, 256 * r + 256)
        grad = dot(slopes[:, rows], own_w[...], ((0,), (0,)))
        pg_ref[rows, :] = (dg_ref[rows, :].astype(F32) * grad).astype(BF)
    result[...] = dot(nrm_ref[...], pg_ref[...], ((0,), (0,)))
    bit = jnp.where(j < 2, own["z"], own["x"]) & 1
    for k in range(2):
        columns = pl.ds(pl.multiple_of((bit ^ k) * 256, 256), 256)
        for ref, core in ((keep_ref, own["c"]), (send_ref, 1 - own["c"])):
            for x in range(4):
                rows = pl.ds(pl.multiple_of(x * 256 + core * 128, 128), 128)
                ref[128 * x : 128 * x + 128, 256 * k : 256 * k + 256] = result[rows, columns].astype(BF)
    go[:, pl.ds(pl.multiple_of(j * wide, wide), wide)] = dot(slopes[...], hid_ref[...])

    @pl.when(j == pl.num_programs(0) - 1)
    def _():
        for x in range(4):
            for ref, core in ((go_keep, own["c"]), (go_send, 1 - own["c"])):
                columns = pl.ds(pl.multiple_of(x * 512 + core * 256, 256), 256)
                ref[:, 256 * x : 256 * x + 256] = go[:, columns].astype(BF)


def lower_kernel(pg_ref, wh_ref, nrm_ref, inv_ref, gain_ref, st_ref, vg_ref, gain_sum, value_sum):
    j = pl.program_id(0)
    nodes = st_ref.shape[0]

    @pl.when(j == 0)
    def _():
        gain_sum[...] = jnp.zeros_like(gain_sum)
        value_sum[...] = jnp.zeros_like(value_sum)

    normed_grad = dot(pg_ref[...], wh_ref[...], ((1,), (1,)))
    normed = nrm_ref[...].astype(F32)
    product = normed_grad * normed
    gain_sum[...] += jnp.sum(product, axis=0, keepdims=True)
    mean = jnp.mean(product, axis=-1, keepdims=True)
    gain = gain_ref[...]
    summed_grad = inv_ref[...] * (normed_grad * gain - normed * (1.0 / gain) * mean)
    value_sum[...] += dot(st_ref[...], summed_grad.astype(BF))

    @pl.when(j == pl.num_programs(0) - 1)
    def _():
        vg_ref[0:nodes, :] = value_sum[...].astype(BF)
        vg_ref[nodes:, :] = jnp.broadcast_to(gain_sum[...] / gain_ref[...], (16, gain.shape[1])).astype(BF)


def latents_kernel(vg_ref, wv_ref, gl_ref):
    gl_ref[...] = dot(vg_ref[0 : gl_ref.shape[0], :], wv_ref[...], ((1,), (1,))).astype(BF)


def value_kernel(
    lat_ref, lat_recv, vg_ref, vg_recv, go_keep, go_recv, b_ref, own_lat, gain_turned
):
    nodes, width = lat_ref.shape
    core = lax.axis_index("core")
    gain = vg_ref[nodes:, :].astype(F32)[0:8] + vg_recv[nodes:, :].astype(F32)[0:8]
    gain = jnp.broadcast_to(gain[0:1], (128, width)).T
    gain_turned[...] = gain
    for x in range(4):
        columns = pl.ds(pl.multiple_of(x * 256 + core * 128, 128), 128)
        own_lat[:, 128 * x : 128 * x + 128] = lat_ref[:, columns]
    value = dot(own_lat[...], vg_ref[0:nodes, :], ((0,), (0,)))
    value = value + dot(lat_recv[...], vg_recv[0:nodes, :], ((0,), (0,)))
    b_ref[:, 0:width] = value.astype(BF)
    out = (go_keep[...].astype(F32) + go_recv[...].astype(F32)).T.reshape(64, 2, 8, 128)
    for k in range(2):
        b_ref[:, width + 128 * k : width + 128 * k + 128] = out[:, k].reshape(512, 128).astype(BF)
    for x in range(4):
        rows = pl.ds(pl.multiple_of(x * 256 + core * 128, 128), 128)
        b_ref[128 * x : 128 * x + 128, width + 256 :] = gain_turned[rows, :].astype(BF)


def whole(shape):
    return pl.BlockSpec(shape, lambda j: (0,) * len(shape))


def params():
    return pltpu.CompilerParams(vmem_limit_bytes=VMEM, dimension_semantics=("arbitrary",))


def cost(flops, moved):
    return pl.CostEstimate(flops=flops, bytes_accessed=moved, transcendentals=0)


def like(shape, dtype=BF):
    return jax.ShapeDtypeStruct(shape, dtype)


def forward(lat, wv, nb, cf, emb, gain, wh, ow):
    nodes, width = lat.shape
    points = emb.shape[0]
    hidden = wh.shape[1]
    wide = 512
    tile = pl.BlockSpec((points, wide), lambda j: (0, j))
    raw = pl.BlockSpec(memory_space=pl.ANY)
    return pl.pallas_call(
        forward_kernel,
        grid=(hidden // wide,),
        in_specs=[
            whole(lat.shape), whole(wv.shape), whole(nb.shape), whole(cf.shape), raw, whole(gain.shape),
            pl.BlockSpec((width, wide), lambda j: (0, j)),
            pl.BlockSpec((ow.shape[0], wide), lambda j: (0, j)),
        ],
        out_specs=[whole((104, 256))] * 4
        + [tile, tile, raw, whole((points, 1)), whole((nodes, points)), whole((nodes, width // 2))],
        out_shape=[like((104, 256), F32)] * 4
        + [
            like((points, hidden)), like((points, hidden)), like((points, width)),
            like((points, 1), F32), like((nodes, points)), like((nodes, width // 2)),
        ],
        scratch_shapes=[
            pltpu.VMEM((points, width), BF),
            pltpu.VMEM((104, points), F32),
            pltpu.VMEM((points, width), BF),
            pltpu.SemaphoreType.DMA((2,)),
        ],
        compiler_params=params(),
        cost_estimate=cost(6_400_000_000, 30_000_000),
        name="forward",
    )(lat, wv, nb, cf, emb, gain, wh, ow)


def in_vmem(kernel, name, out_shape, scratch, estimate, *args, scalars=0):
    vm = pl.BlockSpec(memory_space=pltpu.VMEM)
    many = isinstance(out_shape, list)
    return pl.pallas_call(
        kernel,
        in_specs=[pl.BlockSpec(memory_space=pltpu.SMEM)] * scalars + [vm] * (len(args) - scalars),
        out_specs=[vm] * len(out_shape) if many else vm,
        out_shape=out_shape,
        scratch_shapes=scratch,
        compiler_params=pltpu.CompilerParams(vmem_limit_bytes=VMEM),
        cost_estimate=estimate,
        name=name,
    )(*args)


def upper(parts, ow, dg, hid, nrm):
    points, hidden = dg.shape
    width = nrm.shape[1]
    wide = 512
    col = lambda n: pl.BlockSpec((n, wide), lambda j: (0, j))

    def place(j):
        bit = jnp.where(j < 2, lax.axis_index("x"), lax.axis_index("z")) & 1
        return (0, j ^ bit)

    piece = pl.BlockSpec((width // 2, wide), place)
    return pl.pallas_call(
        upper_kernel,
        grid=(hidden // wide,),
        in_specs=[whole(p.shape) for p in parts] + [col(ow.shape[0]), col(points), col(points), whole(nrm.shape)],
        out_specs=[col(points), piece, piece, whole((128, hidden // 2)), whole((128, hidden // 2))],
        out_shape=[
            like((points, hidden)), like((width // 2, hidden)), like((width // 2, hidden)),
            like((128, hidden // 2)), like((128, hidden // 2)),
        ],
        scratch_shapes=[
            pltpu.VMEM((128, points), BF), pltpu.VMEM((128, wide), BF),
            pltpu.VMEM((128, hidden), F32), pltpu.VMEM((width, wide), F32),
        ],
        compiler_params=params(),
        cost_estimate=cost(5_400_000_000, 24_000_000),
        name="upper",
    )(*parts, ow, dg, hid, nrm)


def lower(pg, wh, nrm, inv, gain, st):
    points, width = nrm.shape
    nodes = st.shape[0]
    step = 256
    rows = lambda n: pl.BlockSpec((step, n), lambda j: (j, 0))
    return pl.pallas_call(
        lower_kernel,
        grid=(points // step,),
        in_specs=[
            rows(pg.shape[1]), whole(wh.shape), rows(width), rows(1), whole(gain.shape),
            pl.BlockSpec((nodes, step), lambda j: (0, j)),
        ],
        out_specs=whole((nodes + 16, width)),
        out_shape=like((nodes + 16, width)),
        scratch_shapes=[pltpu.VMEM((1, width), F32), pltpu.VMEM((nodes, width), F32)],
        compiler_params=params(),
        cost_estimate=cost(5_100_000_000, 16_000_000),
        name="lower",
    )(pg, wh, nrm, inv, gain, st)


def permute(value, pairs):
    return lax.ppermute(value, AXES, pairs)


def total_of(parts, tile):
    return sum(part[:, 512 * tile : 512 * tile + 512].astype(F32) for part in parts)


def per_device(
    latents, grid_embed, neighbours, edge_coef, w_value, gain, w_hidden, output_weight,
    targets, var_weight, area, valid_counts,
):
    lat = latents[0]
    gain_row = gain[None, :]
    f0, f1, f2, f3, hid, dg, nrm, inv, st, lat_send = forward(
        lat, w_value, neighbours, edge_coef, grid_embed, gain_row, w_hidden, output_weight
    )
    core = core_pairs()
    r3 = permute(f3, x_pairs(3))
    r1 = permute(f1, x_pairs(1))
    r2 = permute(f2, x_pairs(2))
    c0, c1, c2, c3 = (permute(f, core) for f in (f0, r1, r2, r3))
    s0, s1, s2, s3 = in_vmem(
        slopes_kernel, "slopes", [like((112, 256))] * 4, [pltpu.VMEM((4, 112, 256), F32)],
        cost(20_000_000, 3_000_000),
        valid_counts, f0, r1, r2, r3, c0, c1, c2, c3, targets, var_weight[:, None], area[None, :], scalars=1,
    )
    q3 = permute(s3, x_pairs(3))
    q1 = permute(s1, x_pairs(1))
    q2 = permute(s2, x_pairs(2))
    lat_recv = permute(lat_send, core)
    pg, a_keep, a_send, go_keep, go_send = upper([s0, q1, q2, q3], output_weight, dg, hid, nrm)
    a = [a_keep, permute(a_send, core)]
    go_recv = permute(go_send, core)
    vg = lower(pg, w_hidden, nrm, inv, gain_row, st)
    width = vg.shape[1]
    first = [permute(total_of(a, k).astype(BF), ring_pairs(axis)) for k, axis in ((1, "x"), (3, "z"))]
    vg_recv = permute(vg, core)
    grad_latents = in_vmem(latents_kernel, "grad_latents", like(lat.shape), [], cost(800_000_000, 4_000_000), vg, w_value)
    b = in_vmem(
        value_kernel, "grad_value", like((width // 2, width + 384)),
        [pltpu.VMEM((lat.shape[0], width // 2), BF), pltpu.VMEM((width, 128), F32)],
        cost(800_000_000, 6_000_000),
        lat, lat_recv, vg, vg_recv, go_keep, go_recv,
    )
    quarters = []
    for k, axis, half in ((0, "z", first[0]), (2, "x", first[1])):
        kept = total_of(a, k) + half.astype(F32)
        quarters.append(kept[:, :256] + permute(kept[:, 256:].astype(BF), ring_pairs(axis)).astype(F32))
    mine = jnp.concatenate([quarters[0].astype(BF), quarters[1].astype(BF), b], axis=1)
    sent = mine.reshape(64, 8, mine.shape[1])
    met = lax.all_to_all(sent, CORE_AXES, 0, 0, tiled=True)
    met = met.reshape(2, 2, 2, 2, 4, 8, met.shape[2])
    a_sum = jnp.sum(met[..., :512].astype(F32), axis=(0, 2, 4))
    b_sum = jnp.sum(met[..., 512:].astype(F32), axis=(0, 1, 2, 3, 4))
    a_first = a_sum[..., :256].transpose(2, 0, 1, 3).reshape(8, 1024)
    a_second = a_sum[..., 256:].transpose(2, 1, 0, 3).reshape(8, 1024)
    grad_hidden = jnp.concatenate([a_first, a_second], axis=1)
    out = b_sum[:, width : width + 256].reshape(8, 2, 128).transpose(2, 1, 0).reshape(128, 16)[:100]
    return (b_sum[:, :width], b_sum[:, width + 256], grad_hidden, out, grad_latents[None])


def solution(mesh):
    mesh = jax.sharding.Mesh(mesh.devices.reshape(4, 2, 4, 4), AXES)
    member, node = ("x", "core"), ("z", "y")
    in_specs = (
        P(member, node, None),
        P(node, None),
        P(None, node),
        P(None, node),
        P(),
        P(),
        P(),
        P(),
        P(None, node),
        P(),
        P(node),
        P(),
    )
    out_specs = (
        P(AXES, None),
        P(AXES),
        P(AXES, None),
        P(None, AXES),
        P(member, node, None),
    )
    return jax.shard_map(
        per_device, mesh=mesh, in_specs=in_specs, out_specs=out_specs, check_vma=False
    )
```

time: 2030 us -> 137 us (0.07)
  waiting for transfers between devices: 1820 us -> 44 us
  blocking collectives: 66.6 us -> 0 us
  matrix products: 54.3 us -> 0 us
  Pallas kernels: 0 us -> 53.7 us
  other arithmetic: 46.5 us -> 4.36 us
  starting transfers between devices: 0.83 us -> 27.3 us
    reduce_scatter x2 -> x0, waiting for transfers between devices: 1150 us -> none  [the longest x1 648 us: per_device(): lax.psum_scatter(grad_hidden, ('member', 'node'), scatter_dimension=0, ti...]
    unnamed x5 -> x0, waiting for transfers between devices: 642 us -> none
    unnamed x1 -> x0, blocking collectives: 66.6 us -> none
    dot_general x9 -> x0, matrix products: 54.3 us -> none  [the longest x1 11.4 us: backward_upper(): lax.dot_general(normalized_rows, pre_grad, (((0,), (0,)), ((), ())), pref...]
    pallas_call x0 -> x6, Pallas kernels: none -> 53.7 us  [the longest x1 18.4 us: forward(): pl.pallas_call(forward_kernel, grid=(hidden // wide,), in_specs=[whole(la...]
    all_gather x1 -> x0, waiting for transfers between devices: 29.9 us -> none  [per_device(): lax.all_gather(member_prediction[None], 'member', axis=0, tiled=True)]
    scatter-add x1 -> x0, other arithmetic: 28.9 us -> none  [backward_lower(): jax.ops.segment_sum(edge_grads.reshape(-1, width), neighbour_rows.reshape...]
    all_to_all x0 -> x1, waiting for transfers between devices: none -> 25.3 us  [per_device(): met = lax.all_to_all(sent, CORE_AXES, 0, 0, tiled=True)]
  transfers between devices with their start and end apart: 4 -> 19, of which waited for: 4 -> 11; matrix products, arithmetic and copies ran while one was open for 4% -> 1% of each run, Pallas kernels for 0% -> 15%
where the time goes in v2:
time: 137 us; the launch traced here: 136 us
  Pallas kernels  53.7 us (39%)
  waiting for transfers between devices  44 us (32%)
  starting transfers between devices  27.3 us (20%)
  local copies, waits for them, and re-layouts  5.87 us (4%)
  other arithmetic  4.36 us (3%)
    all_to_all x1, waiting for transfers between devices, per_device(): met = lax.all_to_all(sent, CORE_AXES, 0, 0, tiled=True)  25.3 us
    ppermute x18, waiting for transfers between devices, permute(): return lax.ppermute(value, AXES, pairs)  18.7 us
    pallas_call x1, Pallas kernels, forward(): pl.pallas_call(forward_kernel, grid=(hidden // wide,), in_specs=[whole(la...  18.4 us
    ppermute x18, starting transfers between devices, permute(): return lax.ppermute(value, AXES, pairs)  16.6 us
    pallas_call x1, Pallas kernels, upper(): pl.pallas_call(upper_kernel, grid=(hidden // wide,), in_specs=[whole(p.sh...  12.6 us
    pallas_call x1, Pallas kernels, lower(): pl.pallas_call(lower_kernel, grid=(points // step,), in_specs=[rows(pg.sh...  11.7 us
    pallas_call x3, Pallas kernels, in_vmem(): pl.pallas_call(kernel, in_specs=[pl.BlockSpec(memory_space=pltpu.SMEM)] *...  10.9 us
    all_to_all x1, starting transfers between devices, per_device(): met = lax.all_to_all(sent, CORE_AXES, 0, 0, tiled=True)  10.7 us
  transfers between devices with their start and end apart: 19, of which 11 were waited for; matrix products, arithmetic and copies ran while one was open for 1% of the time, Pallas kernels for 15%

profile of v2, /device:TPU:0, one launch (start us, length us, event | category | flops | bytes accessed | tf_op | source)
XLA Modules:
  0.0 136.0 jit_solution(10949275944884611524)
XLA Ops:
  0.6 18.4 %forward.1 = (f32[104,256]{1,0:T(8,128)}, f32[104,256]{1,0:T(8,128)}, f32[104,256]{1,0:T(8,128)}, f32[104,256]{1,0:T(8,128)}, bf16[1024,2048]{1,0:T(8,128)(2,1)}...) custom-call(bf16[384,1024]{1,0:T(8,128)(2,1)} %bitcast.21, ...), custom_call_target="tpu_custom_call" | custom-call | flops 6400000000 | bytes 30000000 | tf_op jit(solution)/shard_map/forward/pallas_call | solution.py:264
  19.1 2.9 %collective-permute-start = (f32[104,256]{1,0:T(8,128)}, f32[104,256]{1,0:T(8,128)S(1)}, u32[]{:S(2)}, u32[]{:S(2)}) collective-permute-start(f32[104,256]{1,0:T(8,128)} %get-tuple-element.25), channel_id=1, source_target_pairs={{0,96},{1,97},{2,98},{3,99},{4,100},{5,101},{6,102},{7,103},{8,104... | collective-permute-start | bytes 319496 | tf_op jit(solution)/shard_map/ppermute | solution.py:358
  22.0 0.2 collective-permute-start.1
  22.2 1.6 %collective-permute-start.2 = (f32[104,256]{1,0:T(8,128)}, f32[104,256]{1,0:T(8,128)S(1)}, u32[]{:S(2)}, u32[]{:S(2)}) collective-permute-start(f32[104,256]{1,0:T(8,128)} %get-tuple-element.27), channel_id=1, source_target_pairs={{0,64},{1,65},{2,66},{3,67},{4,68},{5,69},{6,70},{7,71},{8,72},{9,... | collective-permute-start | bytes 319496 | tf_op jit(solution)/shard_map/ppermute | solution.py:358
  23.8 0.0 collective-permute-start.3
  23.9 2.4 %collective-permute-done.f1 = f32[104,256]{1,0:T(8,128)S(1)} collective-permute-done((f32[104,256]{1,0:T(8,128)}, f32[104,256]{1,0:T(8,128)S(1)}, u32[]{:S(2)}, u32[]{:S(2)}) %collective-permute-start) | collective-permute-done | bytes 106528 | tf_op jit(solution)/shard_map/ppermute | solution.py:358
  26.3 0.0 collective-permute-start.4
  26.3 0.9 collective-permute-done.1.f2
  27.2 0.0 collective-permute-start.5
  27.2 1.9 %collective-permute-done.2.f3 = f32[104,256]{1,0:T(8,128)S(1)} collective-permute-done((f32[104,256]{1,0:T(8,128)}, f32[104,256]{1,0:T(8,128)S(1)}, u32[]{:S(2)}, u32[]{:S(2)}) %collective-permute-start.2) | collective-permute-done | bytes 106528 | tf_op jit(solution)/shard_map/ppermute | solution.py:358
  29.0 0.0 collective-permute-start.6
  29.0 0.7 copy.20.vw_ref
  29.8 0.0 collective-permute-done.3.c0
  29.8 0.0 collective-permute-done.4.c1
  29.8 0.0 collective-permute-done.5.c2
  29.8 0.5 collective-permute-done.6.c3
  30.3 0.1 copy-done.8
  30.4 0.1 copy-done.9
  30.5 0.0 copy-done.10
  30.5 0.5 copy-done.11
  31.0 2.7 %slopes.1 = (bf16[112,256]{1,0:T(8,128)(2,1)}, bf16[112,256]{1,0:T(8,128)(2,1)}, bf16[112,256]{1,0:T(8,128)(2,1)}, bf16[112,256]{1,0:T(8,128)(2,1)}) custom-call(s32[16]{0:T(128)} %vc_ref.1, f32[104,256]{1,0:T(8,128)} %get-tuple-element.24.f0, f32[104,256]{1,0:T(8,128)} %copy-done.5, f32[104,256]{1,0:T(8,128)} %copy-done.6, f32[104,256]{1,0:T(8,128)} %copy-done.7, ...), custom_call_target="tpu_custom_call" | custom-call | flops 20000000 | bytes 3000000 | tf_op jit(solution)/shard_map/slopes/pallas_call | solution.py:294
  33.7 2.0 %collective-permute-start.7 = (bf16[112,256]{1,0:T(8,128)(2,1)}, bf16[112,256]{1,0:T(8,128)(2,1)S(1)}, u32[]{:S(2)}, u32[]{:S(2)}) collective-permute-start(bf16[112,256]{1,0:T(8,128)(2,1)} %get-tuple-element.29), channel_id=1, source_target_pairs={{0,96},{1,97},{2,98},{3,99},{4,100},{5,101},{6,102},{7,103},{8,104... | collective-permute-start | bytes 172040 | tf_op jit(solution)/shard_map/ppermute | solution.py:358
  35.6 0.0 collective-permute-start.8
  35.6 2.7 %collective-permute-start.9 = (bf16[112,256]{1,0:T(8,128)(2,1)}, bf16[112,256]{1,0:T(8,128)(2,1)S(1)}, u32[]{:S(2)}, u32[]{:S(2)}) collective-permute-start(bf16[112,256]{1,0:T(8,128)(2,1)} %get-tuple-element.31), channel_id=1, source_target_pairs={{0,64},{1,65},{2,66},{3,67},{4,68},{5,69},{6,70},{7,71},{8,72},{9,... | collective-permute-start | bytes 172040 | tf_op jit(solution)/shard_map/ppermute | solution.py:358
  38.4 1.3 collective-permute-done.7.s1
  39.6 0.8 collective-permute-done.8.s2
  40.5 1.3 collective-permute-done.9.s3
  41.7 0.6 copy-done.17
  42.4 12.6 %upper.1 = (bf16[1024,2048]{1,0:T(8,128)(2,1)}, bf16[512,2048]{1,0:T(8,128)(2,1)}, bf16[512,2048]{1,0:T(8,128)(2,1)}, bf16[128,1024]{1,0:T(8,128)(2,1)}, bf16[128,1024]{1,0:T(8,128)(2,1)}) custom-call(bf16[112,256]{1,0:T(8,128)(2,1)} %get-tuple-element.28.s0, bf16[112,256]{1,0:T(8,128)(2,1)} %copy-done.15, bf16[112,256]{1,0:T(8,128)(2,1)} %copy-done.16, ...), custom_call_target="tpu_custom_call" | custom-call | flops 5400000000 | bytes 24000000 | tf_op jit(solution)/shard_map/upper/pallas_call | solution.py:317
  55.0 4.4 %collective-permute-done.10 = bf16[512,2048]{1,0:T(8,128)(2,1)S(1)} collective-permute-done((bf16[512,2048]{1,0:T(8,128)(2,1)}, bf16[512,2048]{1,0:T(8,128)(2,1)S(1)}, u32[]{:S(2)}, u32[]{:S(2)}) %collective-permute-start.10) | collective-permute-done | bytes 2097184 | tf_op jit(solution)/shard_map/ppermute | solution.py:358
  59.3 1.2 add_convert_fusion.1
  60.5 2.1 %collective-permute-start.11 = (bf16[512,512]{1,0:T(8,128)(2,1)S(1)}, bf16[512,512]{1,0:T(8,128)(2,1)S(1)}, u32[]{:S(2)}, u32[]{:S(2)}) collective-permute-start(bf16[512,512]{1,0:T(8,128)(2,1)S(1)} %add_convert_fusion.1), channel_id=1, source_target_pairs={{0,32},{1,33},{2,34},{3,35},{4,36},{5,37},{6,38},{7,39},{8,40},{9,... | collective-permute-start | bytes 1572872 | tf_op jit(solution)/shard_map/ppermute | solution.py:358
  62.6 11.7 %lower.1.vg_ref = bf16[400,1024]{1,0:T(8,128)(2,1)} custom-call(bf16[1024,2048]{1,0:T(8,128)(2,1)} %get-tuple-element.38.pg_ref, bf16[1024,2048]{1,0:T(8,128)(2,1)} %wh_ref.3, bf16[1024,1024]{1,0:T(8,128)(2,1)} %get-tuple-element.34.nrm_ref, f32[1024,1]{1,0:T(8,128)} %get-tuple-element.39.inv_ref, f32[1,1024]{1,0:T(1,128)} %bitcast.28, ...), custom_call_target="tpu_custom_call" | custom-call | flops 5100000256 | bytes 16000000 | tf_op jit(solution)/shard_map/lower/pallas_call | solution.py:341
  74.4 0.3 collective-permute-start.16
  74.7 0.0 collective-permute-done.11
  74.7 0.4 convert_add_fusion.1
  75.0 2.0 %collective-permute-start.13 = (bf16[512,512]{1,0:T(8,128)(2,1)S(1)}, bf16[512,512]{1,0:T(8,128)(2,1)S(1)}, u32[]{:S(2)}, u32[]{:S(2)}) collective-permute-start(bf16[512,512]{1,0:T(8,128)(2,1)S(1)} %get-tuple-element.44), channel_id=1, source_target_pairs={{0,4},{1,5},{2,6},{3,7},{4,0},{5,1},{6,2},{7,3},{8,12},{9,13},{10,... | collective-permute-start | bytes 1572872 | tf_op jit(solution)/shard_map/ppermute | solution.py:358
  77.0 2.1 %collective-permute-start.15 = (bf16[384,512]{1,0:T(8,128)(2,1)S(1)}, bf16[384,512]{1,0:T(8,128)(2,1)S(1)}, u32[]{:S(2)}, u32[]{:S(2)}) collective-permute-start(bf16[384,512]{1,0:T(8,128)(2,1)S(1)} %copy-done.13), channel_id=1, source_target_pairs={{0,16},{1,17},{2,18},{3,19},{4,20},{5,21},{6,22},{7,23},{8,24},{9,... | collective-permute-start | bytes 1179656 | tf_op jit(solution)/shard_map/ppermute | solution.py:358
  79.2 0.1 collective-permute-start.17
  79.3 0.1 collective-permute-start.12
  79.4 4.9 %collective-permute-done.13 = bf16[512,512]{1,0:T(8,128)(2,1)S(1)} collective-permute-done((bf16[512,512]{1,0:T(8,128)(2,1)S(1)}, bf16[512,512]{1,0:T(8,128)(2,1)S(1)}, u32[]{:S(2)}, u32[]{:S(2)}) %collective-permute-start.13) | collective-permute-done | bytes 524320 | tf_op jit(solution)/shard_map/ppermute | solution.py:358
  84.3 0.3 convert_add_fusion
  84.6 0.4 collective-permute-start.14
  85.0 0.0 collective-permute-done.15.lat_recv
  85.0 0.0 collective-permute-done.17.go_recv
  85.0 0.7 copy-done.3
  85.7 0.1 copy-done.4
  85.9 0.3 copy-done.2
  86.1 4.5 %grad_value.1 = bf16[512,1408]{1,0:T(8,128)(2,1)} custom-call(bf16[384,1024]{1,0:T(8,128)(2,1)} %bitcast.22, bf16[384,512]{1,0:T(8,128)(2,1)} %copy-done.3, bf16[400,1024]{1,0:T(8,128)(2,1)} %lower.1.vg_ref, bf16[400,1024]{1,0:T(8,128)(2,1)} %copy-done.2, bf16[128,1024]{1,0:T(8,128)(2,1)} %get-tuple-element.41.go_keep, bf16[128,1024]{1,0:T(8,128)(2,1)} %copy-done.4), custom_call_target="tpu_custom_call" | custom-call | flops 800000000 | bytes 6000000 | tf_op jit(solution)/shard_map/grad_value/pallas_call | solution.py:294
  90.6 0.0 collective-permute-done.12
  90.6 0.1 fusion.1
  90.7 0.4 collective-permute-done.14
  91.1 0.1 fusion
  91.1 0.8 copy-done
  91.9 1.4 %maximum_bitcast_fusion = bf16[64,8,1920]{2,1,0:T(8,128)(2,1)} fusion(bf16[512,1408]{1,0:T(8,128)(2,1)S(1)} %copy-done, bf16[512,256]{1,0:T(8,128)(2,1)S(1)} %fusion, bf16[512,256]{1,0:T(8,128)(2,1)S(1)} %fusion.1), kind=kLoop, calls=%fused_computation.1 | loop fusion | flops 5898240 | bytes 3932160 | tf_op jit(solution)/shard_map/reshape | solution.py:407
  93.4 10.7 %all-to-all-start = ((bf16[64,8,1920]{2,1,0:T(8,128)(2,1)}), bf16[64,8,1920]{2,1,0:T(8,128)(2,1)S(1)}, u32[]{:S(2)}, u32[]{:S(2)}) async-start(bf16[64,8,1920]{2,1,0:T(8,128)(2,1)} %maximum_bitcast_fusion), calls=%async_computation | async-start | bytes 3932160 | tf_op jit(solution)/shard_map/all_to_all | solution.py:408
  104.1 3.7 %grad_latents.1 = bf16[384,1024]{1,0:T(8,128)(2,1)} custom-call(bf16[400,1024]{1,0:T(8,128)(2,1)} %lower.1.vg_ref, bf16[1024,1024]{1,0:T(8,128)(2,1)} %wv_ref.3), custom_call_target="tpu_custom_call" | custom-call | flops 800000000 | bytes 4000000 | tf_op jit(solution)/shard_map/grad_latents/pallas_call | solution.py:294
  107.9 25.3 %all-to-all-done = bf16[64,8,1920]{2,1,0:T(8,128)(2,1)S(1)} async-done(((bf16[64,8,1920]{2,1,0:T(8,128)(2,1)}), bf16[64,8,1920]{2,1,0:T(8,128)(2,1)S(1)}, u32[]{:S(2)}, u32[]{:S(2)}) %all-to-all-start) | async-done | bytes 1966112 | tf_op jit(solution)/shard_map/all_to_all | solution.py:408
  133.2 0.2 convert_reduce_fusion
  133.4 0.1 convert_reduce_fusion.1
  133.5 0.6 slice_reduce_fusion
  134.1 0.6 slice.95
  134.7 0.6 slice_bitcast_fusion.1
  135.4 0.6 pad_maximum_fusion
  (35 shorter events, 0.2 us)
Async XLA Ops:
  0.6 28.4 %copy-start.12 = (f32[100]{0:T(128)S(1)}, f32[100]{0:T(128)}, u32[]{:S(2)}) copy-start(f32[100]{0:T(128)} %param.21) | copy-start | bytes 1204
  19.1 7.2 %collective-permute-start = (f32[104,256]{1,0:T(8,128)}, f32[104,256]{1,0:T(8,128)S(1)}, u32[]{:S(2)}, u32[]{:S(2)}) collective-permute-start(f32[104,256]{1,0:T(8,128)} %get-tuple-element.25), channel_id=1, source_target_pairs={{0,96},{1,97},{2,98},{3,99},{4,100},{5,101},{6,102},{7,103},{8,104... | collective-permute-start | bytes 319496 | tf_op jit(solution)/shard_map/ppermute | solution.py:358
  22.0 5.1 %collective-permute-start.1 = (f32[104,256]{1,0:T(8,128)}, f32[104,256]{1,0:T(8,128)S(1)}, u32[]{:S(2)}, u32[]{:S(2)}) collective-permute-start(f32[104,256]{1,0:T(8,128)} %get-tuple-element.26), channel_id=1, source_target_pairs={{0,32},{1,33},{2,34},{3,35},{4,36},{5,37},{6,38},{7,39},{8,40},{9,... | collective-permute-start | bytes 319496 | tf_op jit(solution)/shard_map/ppermute | solution.py:358
  22.2 6.8 %collective-permute-start.2 = (f32[104,256]{1,0:T(8,128)}, f32[104,256]{1,0:T(8,128)S(1)}, u32[]{:S(2)}, u32[]{:S(2)}) collective-permute-start(f32[104,256]{1,0:T(8,128)} %get-tuple-element.27), channel_id=1, source_target_pairs={{0,64},{1,65},{2,66},{3,67},{4,68},{5,69},{6,70},{7,71},{8,72},{9,... | collective-permute-start | bytes 319496 | tf_op jit(solution)/shard_map/ppermute | solution.py:358
  23.8 5.9 %collective-permute-start.3 = (f32[104,256]{1,0:T(8,128)}, f32[104,256]{1,0:T(8,128)S(1)}, u32[]{:S(2)}, u32[]{:S(2)}) collective-permute-start(f32[104,256]{1,0:T(8,128)} %get-tuple-element.24.f0), channel_id=1, source_target_pairs={{0,16},{1,17},{2,18},{3,19},{4,20},{5,21},{6,22},{7,23},{8,24},{9,... | collective-permute-start | bytes 319496 | tf_op jit(solution)/shard_map/ppermute | solution.py:358
  26.3 4.1 %copy-start.5 = (f32[104,256]{1,0:T(8,128)}, f32[104,256]{1,0:T(8,128)S(1)}, u32[]{:S(2)}) copy-start(f32[104,256]{1,0:T(8,128)S(1)} %collective-permute-done.f1) | copy-start | bytes 319492
  26.3 3.5 %collective-permute-start.4 = (f32[104,256]{1,0:T(8,128)S(1)}, f32[104,256]{1,0:T(8,128)S(1)}, u32[]{:S(2)}, u32[]{:S(2)}) collective-permute-start(f32[104,256]{1,0:T(8,128)S(1)} %collective-permute-done.f1), channel_id=1, source_target_pairs={{0,16},{1,17},{2,18},{3,19},{4,20},{5,21},{6,22},{7,23},{8,24},{9,... | collective-permute-start | bytes 319496 | tf_op jit(solution)/shard_map/ppermute | solution.py:358
  27.2 3.2 %copy-start.6 = (f32[104,256]{1,0:T(8,128)}, f32[104,256]{1,0:T(8,128)S(1)}, u32[]{:S(2)}) copy-start(f32[104,256]{1,0:T(8,128)S(1)} %collective-permute-done.1.f2) | copy-start | bytes 319492
  27.2 2.6 %collective-permute-start.5 = (f32[104,256]{1,0:T(8,128)S(1)}, f32[104,256]{1,0:T(8,128)S(1)}, u32[]{:S(2)}, u32[]{:S(2)}) collective-permute-start(f32[104,256]{1,0:T(8,128)S(1)} %collective-permute-done.1.f2), channel_id=1, source_target_pairs={{0,16},{1,17},{2,18},{3,19},{4,20},{5,21},{6,22},{7,23},{8,24},{9,... | collective-permute-start | bytes 319496 | tf_op jit(solution)/shard_map/ppermute | solution.py:358
  29.0 1.3 copy-start.7
  29.0 1.3 collective-permute-start.6
  29.8 0.6 copy-start.8
  29.8 0.7 copy-start.9
  29.8 0.7 copy-start.10
  30.3 0.6 copy-start.11
  33.7 6.0 %collective-permute-start.7 = (bf16[112,256]{1,0:T(8,128)(2,1)}, bf16[112,256]{1,0:T(8,128)(2,1)S(1)}, u32[]{:S(2)}, u32[]{:S(2)}) collective-permute-start(bf16[112,256]{1,0:T(8,128)(2,1)} %get-tuple-element.29), channel_id=1, source_target_pairs={{0,96},{1,97},{2,98},{3,99},{4,100},{5,101},{6,102},{7,103},{8,104... | collective-permute-start | bytes 172040 | tf_op jit(solution)/shard_map/ppermute | solution.py:358
  35.6 4.8 %collective-permute-start.8 = (bf16[112,256]{1,0:T(8,128)(2,1)}, bf16[112,256]{1,0:T(8,128)(2,1)S(1)}, u32[]{:S(2)}, u32[]{:S(2)}) collective-permute-start(bf16[112,256]{1,0:T(8,128)(2,1)} %get-tuple-element.30), channel_id=1, source_target_pairs={{0,32},{1,33},{2,34},{3,35},{4,36},{5,37},{6,38},{7,39},{8,40},{9,... | collective-permute-start | bytes 172040 | tf_op jit(solution)/shard_map/ppermute | solution.py:358
  35.6 6.1 %collective-permute-start.9 = (bf16[112,256]{1,0:T(8,128)(2,1)}, bf16[112,256]{1,0:T(8,128)(2,1)S(1)}, u32[]{:S(2)}, u32[]{:S(2)}) collective-permute-start(bf16[112,256]{1,0:T(8,128)(2,1)} %get-tuple-element.31), channel_id=1, source_target_pairs={{0,64},{1,65},{2,66},{3,67},{4,68},{5,69},{6,70},{7,71},{8,72},{9,... | collective-permute-start | bytes 172040 | tf_op jit(solution)/shard_map/ppermute | solution.py:358
  39.6 2.1 %copy-start.15 = (bf16[112,256]{1,0:T(8,128)(2,1)}, bf16[112,256]{1,0:T(8,128)(2,1)S(1)}, u32[]{:S(2)}) copy-start(bf16[112,256]{1,0:T(8,128)(2,1)S(1)} %collective-permute-done.7.s1) | copy-start | bytes 172036
  40.5 1.3 copy-start.16
  41.7 0.6 copy-start.17
  55.0 4.4 %collective-permute-start.10 = (bf16[512,2048]{1,0:T(8,128)(2,1)}, bf16[512,2048]{1,0:T(8,128)(2,1)S(1)}, u32[]{:S(2)}, u32[]{:S(2)}) collective-permute-start(bf16[512,2048]{1,0:T(8,128)(2,1)} %get-tuple-element.36), channel_id=1, source_target_pairs={{0,16},{1,17},{2,18},{3,19},{4,20},{5,21},{6,22},{7,23},{8,24},{9,... | collective-permute-start | bytes 6291464 | tf_op jit(solution)/shard_map/ppermute | solution.py:358
  60.5 14.1 %collective-permute-start.11 = (bf16[512,512]{1,0:T(8,128)(2,1)S(1)}, bf16[512,512]{1,0:T(8,128)(2,1)S(1)}, u32[]{:S(2)}, u32[]{:S(2)}) collective-permute-start(bf16[512,512]{1,0:T(8,128)(2,1)S(1)} %add_convert_fusion.1), channel_id=1, source_target_pairs={{0,32},{1,33},{2,34},{3,35},{4,36},{5,37},{6,38},{7,39},{8,40},{9,... | collective-permute-start | bytes 1572872 | tf_op jit(solution)/shard_map/ppermute | solution.py:358
  62.6 12.0 %copy-start.1 = (bf16[512,2048]{1,0:T(8,128)(2,1)S(1)}, bf16[512,2048]{1,0:T(8,128)(2,1)}, u32[]{:S(2)}) copy-start(bf16[512,2048]{1,0:T(8,128)(2,1)} %get-tuple-element.35) | copy-start | bytes 6291460
  74.3 2.7 %copy-start.13 = (bf16[384,512]{1,0:T(8,128)(2,1)S(1)}, bf16[384,512]{1,0:T(8,128)(2,1)}, u32[]{:S(2)}) copy-start(bf16[384,512]{1,0:T(8,128)(2,1)} %get-tuple-element.37) | copy-start | bytes 1179652
  74.3 4.8 %copy-start.14 = (bf16[128,1024]{1,0:T(8,128)(2,1)S(1)}, bf16[128,1024]{1,0:T(8,128)(2,1)}, u32[]{:S(2)}) copy-start(bf16[128,1024]{1,0:T(8,128)(2,1)} %get-tuple-element.42) | copy-start | bytes 786436
  74.4 10.7 %collective-permute-start.16 = (bf16[400,1024]{1,0:T(8,128)(2,1)}, bf16[400,1024]{1,0:T(8,128)(2,1)S(1)}, u32[]{:S(2)}, u32[]{:S(2)}) collective-permute-start(bf16[400,1024]{1,0:T(8,128)(2,1)} %lower.1.vg_ref), channel_id=1, source_target_pairs={{0,16},{1,17},{2,18},{3,19},{4,20},{5,21},{6,22},{7,23},{8,24},{9,... | collective-permute-start | bytes 2457608 | tf_op jit(solution)/shard_map/ppermute | solution.py:358
  75.0 9.3 %collective-permute-start.13 = (bf16[512,512]{1,0:T(8,128)(2,1)S(1)}, bf16[512,512]{1,0:T(8,128)(2,1)S(1)}, u32[]{:S(2)}, u32[]{:S(2)}) collective-permute-start(bf16[512,512]{1,0:T(8,128)(2,1)S(1)} %get-tuple-element.44), channel_id=1, source_target_pairs={{0,4},{1,5},{2,6},{3,7},{4,0},{5,1},{6,2},{7,3},{8,12},{9,13},{10,... | collective-permute-start | bytes 1572872 | tf_op jit(solution)/shard_map/ppermute | solution.py:358
  77.0 8.0 %collective-permute-start.15 = (bf16[384,512]{1,0:T(8,128)(2,1)S(1)}, bf16[384,512]{1,0:T(8,128)(2,1)S(1)}, u32[]{:S(2)}, u32[]{:S(2)}) collective-permute-start(bf16[384,512]{1,0:T(8,128)(2,1)S(1)} %copy-done.13), channel_id=1, source_target_pairs={{0,16},{1,17},{2,18},{3,19},{4,20},{5,21},{6,22},{7,23},{8,24},{9,... | collective-permute-start | bytes 1179656 | tf_op jit(solution)/shard_map/ppermute | solution.py:358
  79.2 5.8 %collective-permute-start.17 = (bf16[128,1024]{1,0:T(8,128)(2,1)S(1)}, bf16[128,1024]{1,0:T(8,128)(2,1)S(1)}, u32[]{:S(2)}, u32[]{:S(2)}) collective-permute-start(bf16[128,1024]{1,0:T(8,128)(2,1)S(1)} %copy-done.14), channel_id=1, source_target_pairs={{0,16},{1,17},{2,18},{3,19},{4,20},{5,21},{6,22},{7,23},{8,24},{9,... | collective-permute-start | bytes 786440 | tf_op jit(solution)/shard_map/ppermute | solution.py:358
  79.3 11.3 %collective-permute-start.12 = (bf16[512,256]{1,0:T(8,128)(2,1)S(1)}, bf16[512,256]{1,0:T(8,128)(2,1)S(1)}, u32[]{:S(2)}, u32[]{:S(2)}) collective-permute-start(bf16[512,256]{1,0:T(8,128)(2,1)S(1)} %slice.125), channel_id=1, source_target_pairs={{0,4},{1,5},{2,6},{3,7},{4,0},{5,1},{6,2},{7,3},{8,12},{9,13},{10,... | collective-permute-start | bytes 786440 | tf_op jit(solution)/shard_map/ppermute | solution.py:358
  84.6 6.5 %collective-permute-start.14 = (bf16[512,256]{1,0:T(8,128)(2,1)S(1)}, bf16[512,256]{1,0:T(8,128)(2,1)S(1)}, u32[]{:S(2)}, u32[]{:S(2)}) collective-permute-start(bf16[512,256]{1,0:T(8,128)(2,1)S(1)} %slice.124), channel_id=1, source_target_pairs={{0,32},{1,33},{2,34},{3,35},{4,36},{5,37},{6,38},{7,39},{8,40},{9,... | collective-permute-start | bytes 786440 | tf_op jit(solution)/shard_map/ppermute | solution.py:358
  85.0 0.7 copy-start.3
  85.0 0.8 copy-start.4
  85.0 1.1 copy-start.2
  90.6 1.4 %copy-start = (bf16[512,1408]{1,0:T(8,128)(2,1)S(1)}, bf16[512,1408]{1,0:T(8,128)(2,1)}, u32[]{:S(2)}) copy-start(bf16[512,1408]{1,0:T(8,128)(2,1)} %grad_value.1) | copy-start | bytes 4325380
  93.4 39.8 %all-to-all-start = ((bf16[64,8,1920]{2,1,0:T(8,128)(2,1)}), bf16[64,8,1920]{2,1,0:T(8,128)(2,1)S(1)}, u32[]{:S(2)}, u32[]{:S(2)}) async-start(bf16[64,8,1920]{2,1,0:T(8,128)(2,1)} %maximum_bitcast_fusion), calls=%async_computation | async-start | bytes 3932160 | tf_op jit(solution)/shard_map/all_to_all | solution.py:408

commit v3 on v2

v3 whole, which is shorter than its diff:
```python
import itertools

import jax
import jax.numpy as jnp
from jax import lax
from jax.experimental import pallas as pl
from jax.experimental.pallas import tpu as pltpu
from jax.sharding import PartitionSpec as P

BF = jnp.bfloat16
F32 = jnp.float32
kernel_width = 0.25
fair_alpha = 0.95
norm_eps = 1e-05
members = 8
GELU_C = 0.7978845608028654
MIB = 1024 * 1024
CORE_AXES = ("x", "z", "y")
AXES = ("x", "core", "z", "y")


def flat(x, c, z, y):
    return ((x * 2 + c) * 4 + z) * 4 + y


def core_pairs():
    return [
        (flat(x, c, z, y), flat(x, 1 - c, z, y))
        for x, c, z, y in itertools.product(range(4), range(2), range(4), range(4))
    ]


def ring_pairs(axis):
    pairs = []
    for x, c, z, y in itertools.product(range(4), range(2), range(4), range(4)):
        to = {"x": x, "z": z, "y": y}
        to[axis] ^= (1, 3)[c]
        pairs.append((flat(x, c, z, y), flat(to["x"], c, to["z"], to["y"])))
    return pairs


def own_place():
    return {"x": lax.axis_index("x"), "c": lax.axis_index("core"), "z": lax.axis_index("z"), "y": lax.axis_index("y")}


def masks(core):
    first, second = 1 + 2 * core, 3 - 2 * core
    return (0, second, first, 2)


def x_pairs(position):
    pairs = []
    for x, c, z, y in itertools.product(range(4), range(2), range(4), range(4)):
        pairs.append((flat(x, c, z, y), flat(x ^ masks(c)[position], c, z, y)))
    return pairs


def dot(a, b, dims=((1,), (0,))):
    return lax.dot_general(a, b, (dims, ((), ())), preferred_element_type=F32)


def forward_kernel(
    lat_hbm, wv_hbm, nb_hbm, cf_hbm, emb_hbm, gain_hbm, wh_hbm, ow_hbm,
    f0, f1, f2, f3, hid_ref, dg_ref, nrm, inv_ref, st_ref, lat_send,
    total, lat, wv, emb, wh, ow, nb_ref, cf_ref, gain_ref, sems,
):
    nodes, points = st_ref.shape
    hidden = wh.shape[1]
    wide = 512
    own = own_place()
    pairs = [(lat_hbm, lat), (wv_hbm, wv), (emb_hbm, emb)]
    for first in range(0, hidden, wide):
        pairs.append((wh_hbm.at[:, first : first + wide], wh.at[:, first : first + wide]))
    pairs += [(ow_hbm, ow), (nb_hbm, nb_ref), (cf_hbm, cf_ref), (gain_hbm, gain_ref)]
    small = len(pairs) - 4
    copies = [pltpu.make_async_copy(source, target, sems.at[k]) for k, (source, target) in enumerate(pairs)]
    for k in (*range(small + 1, small + 4), *range(small + 1)):
        copies[k].start()
    for copy in copies[small + 1 :]:
        copy.wait()
    rows_of = lax.broadcasted_iota(jnp.int32, (nodes, 256), 0)
    for r in range(points // 256):
        rows = slice(256 * r, 256 * r + 256)
        st = jnp.zeros((nodes, 256), F32)
        for k in range(3):
            st = st + jnp.where(nb_ref[k : k + 1, rows] == rows_of, cf_ref[k : k + 1, rows], 0.0)
        st_ref[:, rows] = st.astype(BF)
    total[...] = jnp.zeros_like(total)
    copies[0].wait()
    copies[1].wait()
    values = dot(lat[...], wv[...]).astype(BF)
    for x in range(4):
        columns = pl.ds(pl.multiple_of(x * 256 + (1 - own["c"]) * 128, 128), 128)
        lat_send[:, 128 * x : 128 * x + 128] = lat[:, columns]
    copies[2].wait()
    for r in range(points // 256):
        rows = slice(256 * r, 256 * r + 256)
        summed = emb[rows, :].astype(F32) + dot(st_ref[:, rows], values, ((0,), (0,)))
        inv = lax.rsqrt(jnp.mean(summed * summed, axis=-1, keepdims=True) + norm_eps)
        inv_ref[rows, :] = inv
        nrm[rows, :] = (summed * inv * gain_ref[...]).astype(BF)
    copies[small].wait()
    for tile in range(hidden // wide):
        here = slice(wide * tile, wide * tile + wide)
        copies[3 + tile].wait()
        for r in range(points // 256):
            rows = slice(256 * r, 256 * r + 256)
            pre = dot(nrm[rows, :], wh[:, here])
            square = pre * pre
            t = jnp.tanh(pre * (GELU_C + (GELU_C * 0.044715) * square))
            cdf = 0.5 + 0.5 * t
            hid_ref[rows, here] = (pre * cdf).astype(BF)
            inner = pre * (GELU_C + (3 * GELU_C * 0.044715) * square)
            dg_ref[rows, here] = (cdf * (1.0 + (1.0 - t) * inner)).astype(BF)
        total[0:100, :] += dot(ow[:, here], hid_ref[:, here], ((1,), (1,)))
    for f, m in zip((f0, f1, f2, f3), masks(own["c"])):
        f[...] = total[:, pl.ds(pl.multiple_of((own["x"] ^ m) * 256, 256), 256)]


def slopes_kernel(
    vc_ref, f0, f1, f2, f3, c0, c1, c2, c3, tg_ref, vw_ref, area_ref, s0, s1, s2, s3, held
):
    own = own_place()
    first = pl.multiple_of(own["x"] * 256, 256)
    spread = (1.0 - (1.0 - fair_alpha) / members) / (2.0 * members * (members - 1))
    held[:, 96:112, :] = jnp.zeros((4, 16, 256), F32)
    limit = vc_ref[own["z"] * 4 + own["y"]]
    across = lax.broadcasted_iota(jnp.int32, (104, 100), 1)
    down = lax.broadcasted_iota(jnp.int32, (104, 100), 0)
    weights = jnp.sum(jnp.where(across == down, vw_ref[...], 0.0), axis=1, keepdims=True) * 0.01
    for part in range(2):
        mine = pl.ds(pl.multiple_of(first + 128 * part, 128), 128)
        here = slice(128 * part, 128 * part + 128)
        place = first + 128 * part + lax.broadcasted_iota(jnp.int32, (1, 128), 1)
        live = jnp.where(place < limit, area_ref[:, mine], 0.0)
        for top in range(0, 100, 8):
            rows = slice(top, min(top + 8, 100))
            f = [field[rows, here] for field in (f0, f1, f2, f3, c0, c1, c2, c3)]
            sums = [jnp.zeros_like(f[0]) for _ in range(4)]
            for a in range(4):
                for b in range(a + 1, 8):
                    d = f[a] - f[b]
                    s = d * lax.rsqrt(d * d + kernel_width * kernel_width)
                    sums[a] = sums[a] + s
                    if b < 4:
                        sums[b] = sums[b] - s
            target = tg_ref[rows, mine]
            weight = weights[rows, :] * live
            for a in range(4):
                d = f[a] - target
                s = d * lax.rsqrt(d * d + kernel_width * kernel_width)
                held[a, rows, here] = weight * (s * (1.0 / members) - 2.0 * spread * sums[a])
    for a, s in enumerate((s0, s1, s2, s3)):
        s[...] = held[a].astype(BF)


def upper_kernel(
    axis, s0, s1, s2, s3, ow_ref, dg_ref, nrm_ref, *rest
):
    if axis == "z":
        hid_ref, pg_ref, keep_ref, send_ref, go_keep, go_send, slopes, own_w, result, go = rest
    else:
        pg_ref, keep_ref, send_ref, slopes, own_w, result = rest
    points = nrm_ref.shape[0]
    offset = 1024 if axis == "z" else 0
    own = own_place()
    for s, m in zip((s0, s1, s2, s3), masks(own["c"])):
        at = pl.ds(pl.multiple_of((own["x"] ^ m) * 256, 256), 256)
        slopes[0:112, at] = s[...]
    slopes[112:128, :] = jnp.zeros((16, points), BF)
    own_w[96:128, :] = jnp.zeros((32, 1024), BF)
    own_w[0:100, :] = ow_ref[:, offset : offset + 1024]
    for r in range(points // 256):
        rows = slice(256 * r, 256 * r + 256)
        grad = dot(slopes[:, rows], own_w[...], ((0,), (0,)))
        pg_ref[rows, :] = (dg_ref[rows, offset : offset + 1024].astype(F32) * grad).astype(BF)
    for tile in range(2):
        result[...] = dot(nrm_ref[...], pg_ref[:, 512 * tile : 512 * tile + 512], ((0,), (0,)))
        columns = pl.ds(pl.multiple_of((tile ^ (own[axis] & 1)) * 512, 512), 512)
        for ref, core in ((keep_ref, own["c"]), (send_ref, 1 - own["c"])):
            for x in range(4):
                rows = pl.ds(pl.multiple_of(x * 256 + core * 128, 128), 128)
                ref[128 * x : 128 * x + 128, columns] = result[rows, :].astype(BF)
    if axis == "z":
        go[...] = dot(slopes[...], hid_ref[...])
        for x in range(4):
            for ref, core in ((go_keep, own["c"]), (go_send, 1 - own["c"])):
                columns = pl.ds(pl.multiple_of(x * 512 + core * 256, 256), 256)
                ref[:, 256 * x : 256 * x + 256] = go[:, columns].astype(BF)


def lower_kernel(pga_ref, pgb_ref, wh_ref, nrm_ref, inv_ref, gain_ref, st_ref, top_ref, rest_ref, value_sum):
    nodes, points = st_ref.shape
    top = top_ref.shape[0]
    gain = gain_ref[...]
    over_gain = 1.0 / gain
    gain_sum = jnp.zeros_like(gain)
    for r in range(points // 256):
        rows = slice(256 * r, 256 * r + 256)
        normed_grad = dot(pga_ref[rows, :], wh_ref[:, 0:1024], ((1,), (1,)))
        normed_grad = normed_grad + dot(pgb_ref[rows, :], wh_ref[:, 1024:2048], ((1,), (1,)))
        normed = nrm_ref[rows, :].astype(F32)
        product = normed_grad * normed
        gain_sum = gain_sum + jnp.sum(product, axis=0, keepdims=True)
        mean = jnp.mean(product, axis=-1, keepdims=True)
        summed_grad = inv_ref[rows, :] * (normed_grad * gain - normed * over_gain * mean)
        part = dot(st_ref[:, rows], summed_grad.astype(BF))
        value_sum[...] = part if r == 0 else value_sum[...] + part
    top_ref[...] = value_sum[0:top, :].astype(BF)
    rest_ref[0 : nodes - top, :] = value_sum[top:nodes, :].astype(BF)
    rest_ref[nodes - top :, :] = jnp.broadcast_to(gain_sum * over_gain, (16, gain.shape[1])).astype(BF)


def latents_kernel(top_ref, rest_ref, wv_ref, gl_ref):
    top = top_ref.shape[0]
    gl_ref[0:top, :] = dot(top_ref[...], wv_ref[...], ((1,), (1,))).astype(BF)
    gl_ref[top:, :] = dot(rest_ref[0 : gl_ref.shape[0] - top, :], wv_ref[...], ((1,), (1,))).astype(BF)


def value_kernel(
    lat_ref, lat_recv, top_ref, rest_ref, top_recv, rest_recv, go_keep, go_recv, first_ref, second_ref,
    out_hbm, own_lat, gain_turned, block, sems,
):
    nodes, width = lat_ref.shape
    variables = 100
    core = lax.axis_index("core")
    copies = [
        pltpu.make_async_copy(first_ref, out_hbm.at[:, 0:512], sems.at[0]),
        pltpu.make_async_copy(second_ref, out_hbm.at[:, 512:1024], sems.at[1]),
        pltpu.make_async_copy(block, out_hbm.at[:, 1024:], sems.at[2]),
    ]
    copies[0].start()
    copies[1].start()
    top = top_ref.shape[0]
    bottom = nodes - top
    gain = rest_ref[bottom:, :].astype(F32)[0:8] + rest_recv[bottom:, :].astype(F32)[0:8]
    gain_turned[...] = jnp.broadcast_to(gain[0:1], (128, width)).T
    for x in range(4):
        columns = pl.ds(pl.multiple_of(x * 256 + core * 128, 128), 128)
        own_lat[:, 128 * x : 128 * x + 128] = lat_ref[:, columns]
    value = dot(own_lat[0:top, :], top_ref[...], ((0,), (0,)))
    value = value + dot(own_lat[top:, :], rest_ref[0:bottom, :], ((0,), (0,)))
    value = value + dot(lat_recv[0:top, :], top_recv[...], ((0,), (0,)))
    value = value + dot(lat_recv[top:, :], rest_recv[0:bottom, :], ((0,), (0,)))
    block[:, 0:width] = value.astype(BF)
    out = (go_keep[...].astype(F32) + go_recv[...].astype(F32)).T.reshape(64, 2, 8, 128)
    lane = lax.broadcasted_iota(jnp.int32, (128, 128), 1)
    for x in range(4):
        rows = slice(128 * x, 128 * x + 128)
        own_gain = gain_turned[pl.ds(pl.multiple_of(x * 256 + core * 128, 128), 128), :]
        first = out[16 * x : 16 * x + 16, 0].reshape(128, 128)
        block[rows, width : width + 128] = jnp.where(lane == variables, own_gain, first).astype(BF)
        block[rows, width + 128 :] = out[16 * x : 16 * x + 16, 1].reshape(128, 128).astype(BF)
    copies[2].start()
    for copy in copies:
        copy.wait()


def final_kernel(met_ref, value_ref, gain_ref, hidden_ref, out_ref):
    width = value_ref.shape[1]
    first, second = [None, None], [None, None]
    rest = None
    for x in range(4):
        for z in range(4):
            for y in range(4):
                block = met_ref[x * 16 + z * 4 + y].astype(F32)
                for sums, k, columns in ((first, x & 1, slice(0, 512)), (second, z & 1, slice(512, 1024))):
                    sums[k] = block[:, columns] if sums[k] is None else sums[k] + block[:, columns]
                rest = block[:, 1024:] if rest is None else rest + block[:, 1024:]
    for k, part in enumerate(first + second):
        hidden_ref[:, 512 * k : 512 * k + 512] = part
    value_ref[...] = rest[:, :width]
    variables = out_ref.shape[1]
    out_ref[0:8, :] = rest[:, width : width + variables]
    out_ref[8:16, :] = rest[:, width + 128 : width + 128 + variables]
    gain_ref[...] = rest[:, width : width + 128].T[variables : variables + 1]


def cost(flops, moved):
    return pl.CostEstimate(flops=flops, bytes_accessed=moved, transcendentals=0)


def like(shape, dtype=BF):
    return jax.ShapeDtypeStruct(shape, dtype)


def held(*arrays):
    return [pltpu.with_memory_space_constraint(array, pltpu.VMEM) for array in arrays]


def forward(lat, wv, nb, cf, emb, gain, wh, ow):
    nodes, width = lat.shape
    points = emb.shape[0]
    hidden = wh.shape[1]
    vm = pl.BlockSpec(memory_space=pltpu.VMEM)
    raw = pl.BlockSpec(memory_space=pl.ANY)
    args = [pltpu.with_memory_space_constraint(array, pltpu.HBM) for array in (lat, wv, nb, cf, emb, gain, wh, ow)]
    return pl.pallas_call(
        forward_kernel,
        in_specs=[raw] * 8,
        out_specs=[vm] * 10,
        out_shape=[like((104, 256), F32)] * 4
        + [
            pltpu.VMEM((points, hidden), BF), pltpu.VMEM((points, hidden), BF), pltpu.VMEM((points, width), BF),
            pltpu.VMEM((points, 1), F32), pltpu.VMEM((nodes, points), BF), like((nodes, width // 2)),
        ],
        scratch_shapes=[
            pltpu.VMEM((104, points), F32), pltpu.VMEM((nodes, width), BF), pltpu.VMEM((width, width), BF),
            pltpu.VMEM((points, width), BF), pltpu.VMEM((width, hidden), BF), pltpu.VMEM(ow.shape, BF),
            pltpu.VMEM(nb.shape, jnp.int32), pltpu.VMEM(cf.shape, F32), pltpu.VMEM(gain.shape, F32),
            pltpu.SemaphoreType.DMA((7 + hidden // 512,)),
        ],
        compiler_params=pltpu.CompilerParams(vmem_limit_bytes=24 * MIB),
        cost_estimate=cost(6_400_000_000, 12_000_000),
        name="forward",
    )(*args)


def in_vmem(kernel, name, out_shape, scratch, estimate, limit, *args, scalars=0, in_hbm=False):
    vm = pl.BlockSpec(memory_space=pltpu.VMEM)
    many = isinstance(out_shape, list)
    return pl.pallas_call(
        kernel,
        in_specs=[pl.BlockSpec(memory_space=pltpu.SMEM)] * scalars + [vm] * (len(args) - scalars),
        out_specs=[vm] * len(out_shape) if many else pl.BlockSpec(memory_space=pl.ANY) if in_hbm else vm,
        out_shape=out_shape,
        scratch_shapes=scratch,
        compiler_params=pltpu.CompilerParams(vmem_limit_bytes=limit * MIB),
        cost_estimate=estimate,
        name=name,
    )(*args)


def upper(axis, parts, ow, dg, nrm, *hid):
    points, width = nrm.shape
    half = like((width // 2, 1024))
    out_shape = [pltpu.VMEM((points, 1024), BF), half, half]
    scratch = [pltpu.VMEM((128, points), BF), pltpu.VMEM((128, 1024), BF), pltpu.VMEM((width, 512), F32)]
    if axis == "z":
        out_shape += [like((128, 1024)), like((128, 1024))]
        scratch.append(pltpu.VMEM((128, 2048), F32))
    return in_vmem(
        lambda *refs: upper_kernel(axis, *refs), "upper_" + axis, out_shape, scratch, cost(2_700_000_000, 2_000_000), 20,
        *parts, ow, *held(dg, nrm, *hid),
    )


def permute(value, pairs):
    return lax.ppermute(value, AXES, pairs)


def total_of(parts, tile):
    return sum(part[:, 512 * tile : 512 * tile + 512].astype(F32) for part in parts)


def per_device(
    latents, grid_embed, neighbours, edge_coef, w_value, gain, w_hidden, output_weight,
    targets, var_weight, area, valid_counts,
):
    lat = latents[0]
    gain_row = gain[None, :]
    f0, f1, f2, f3, hid, dg, nrm, inv, st, lat_send = forward(
        lat, w_value, neighbours, edge_coef, grid_embed, gain_row, w_hidden, output_weight
    )
    core = core_pairs()
    r3 = permute(f3, x_pairs(3))
    r1 = permute(f1, x_pairs(1))
    r2 = permute(f2, x_pairs(2))
    c0, c1, c2, c3 = (permute(f, core) for f in (f0, r1, r2, r3))
    s0, s1, s2, s3 = in_vmem(
        slopes_kernel, "slopes", [like((112, 256))] * 4, [pltpu.VMEM((4, 112, 256), F32)],
        cost(20_000_000, 3_000_000), 16,
        valid_counts, f0, r1, r2, r3, c0, c1, c2, c3, targets, var_weight[None, :], area[None, :], scalars=1,
    )
    q3 = permute(s3, x_pairs(3))
    q1 = permute(s1, x_pairs(1))
    q2 = permute(s2, x_pairs(2))
    lat_recv = permute(lat_send, core)
    parts = [s0, q1, q2, q3]
    pga, *first = upper("x", parts, output_weight, dg, nrm)
    first[1] = permute(first[1], core)
    pgb, keep, send, go_keep, go_send = upper("z", parts, output_weight, dg, nrm, hid)
    second = [keep, permute(send, core)]
    go_recv = permute(go_send, core)
    sent, pgb = lax.optimization_barrier((total_of(first, 1).astype(BF), pgb))
    first.append(permute(sent, ring_pairs("x")))
    nodes, width = lat.shape
    top, rest = in_vmem(
        lower_kernel, "lower", [like((192, width)), like((nodes - 192 + 16, width))], [pltpu.VMEM((nodes, width), F32)],
        cost(5_100_000_000, 8_000_000), 24,
        *held(pga, pgb), w_hidden, *held(nrm, inv), gain_row, *held(st),
    )
    second.append(permute(total_of(second, 1).astype(BF), ring_pairs("z")))
    halves = [total_of(part, 0).astype(BF) for part in (first, second)]
    *halves, top, rest = lax.optimization_barrier((*halves, top, rest))
    top_recv, rest_recv = permute(top, core), permute(rest, core)
    grad_latents = in_vmem(
        latents_kernel, "grad_latents", like(lat.shape), [], cost(800_000_000, 4_000_000), 16, top, rest, w_value
    )
    mine = in_vmem(
        value_kernel, "grad_value", pltpu.HBM((width // 2, 1024 + width + 256), BF),
        [
            pltpu.VMEM((nodes, width // 2), BF), pltpu.VMEM((width, 128), F32),
            pltpu.VMEM((width // 2, width + 256), BF), pltpu.SemaphoreType.DMA((3,)),
        ],
        cost(800_000_000, 6_000_000), 16,
        lat, lat_recv, top, rest, top_recv, rest_recv, go_keep, go_recv, *halves, in_hbm=True,
    )
    sent = mine.reshape(64, 8, mine.shape[1])
    met = lax.all_to_all(sent, CORE_AXES, 0, 0, tiled=True)
    grad_value, grad_gain, grad_hidden, grad_out = in_vmem(
        final_kernel, "final", [like((8, width), F32), like((1, 8), F32), like((8, 2048), F32), like((16, 100), F32)],
        [], cost(2_000_000, 2_600_000), 16, met,
    )
    return (grad_value, grad_gain.reshape(8), grad_hidden, grad_out.T, grad_latents[None])


def solution(mesh):
    mesh = jax.sharding.Mesh(mesh.devices.reshape(4, 2, 4, 4), AXES)
    member, node = ("x", "core"), ("z", "y")
    in_specs = (
        P(member, node, None),
        P(node, None),
        P(None, node),
        P(None, node),
        P(),
        P(),
        P(),
        P(),
        P(None, node),
        P(),
        P(node),
        P(),
    )
    out_specs = (
        P(AXES, None),
        P(AXES),
        P(AXES, None),
        P(None, AXES),
        P(member, node, None),
    )
    return jax.shard_map(
        per_device, mesh=mesh, in_specs=in_specs, out_specs=out_specs, check_vma=False
    )
```

time: 137 us -> 107 us (0.78)
  Pallas kernels: 53.7 us -> 36 us
  local copies, waits for them, and re-layouts: 5.87 us -> 1.63 us
  waiting for transfers between devices: 44 us -> 40.6 us
  other arithmetic: 4.36 us -> 0.97 us
    pallas_call x3 -> x1, Pallas kernels: 42.7 us -> 14.2 us  [forward(): pl.pallas_call(forward_kernel, in_specs=[raw] * 8, out_specs=[vm] * 10, o...]
    pallas_call x3 -> x7, Pallas kernels: 10.9 us -> 21.8 us  [in_vmem(): pl.pallas_call(kernel, in_specs=[pl.BlockSpec(memory_space=pltpu.SMEM)] *...]
    ppermute x18, waiting for transfers between devices: 18.7 us -> 12 us  [permute(): return lax.ppermute(value, AXES, pairs)]
    all_to_all x1, waiting for transfers between devices: 25.3 us -> 28.6 us  [per_device(): met = lax.all_to_all(sent, CORE_AXES, 0, 0, tiled=True)]
    slice x6 -> x0, local copies, waits for them, and re-layouts: 1.92 us -> none  [the longest x1 0.63 us: per_device(): b_sum[:, width + 256]]
    unnamed x36 -> x18, local copies, waits for them, and re-layouts: 3.17 us -> 1.63 us
    reshape x1 -> x0, other arithmetic: 1.43 us -> none  [per_device(): sent = mine.reshape(64, 8, mine.shape[1])]
  transfers between devices with their start and end apart: 19 -> 19, of which waited for: 11 -> 11; matrix products, arithmetic and copies ran while one was open for 1% -> 1% of each run, Pallas kernels for 15% -> 12%
where the time goes in v3:
time: 107 us
  waiting for transfers between devices  40.6 us (38%)
  Pallas kernels  36 us (34%)
  starting transfers between devices  26.5 us (25%)
  local copies, waits for them, and re-layouts  1.63 us (2%)
    all_to_all x1, waiting for transfers between devices, per_device(): met = lax.all_to_all(sent, CORE_AXES, 0, 0, tiled=True)  28.6 us
    pallas_call x7, Pallas kernels, in_vmem(): pl.pallas_call(kernel, in_specs=[pl.BlockSpec(memory_space=pltpu.SMEM)] *...  21.8 us
    ppermute x18, starting transfers between devices, permute(): return lax.ppermute(value, AXES, pairs)  17 us
    pallas_call x1, Pallas kernels, forward(): pl.pallas_call(forward_kernel, in_specs=[raw] * 8, out_specs=[vm] * 10, o...  14.2 us
    ppermute x18, waiting for transfers between devices, permute(): return lax.ppermute(value, AXES, pairs)  12 us
    all_to_all x1, starting transfers between devices, per_device(): met = lax.all_to_all(sent, CORE_AXES, 0, 0, tiled=True)  9.52 us
  transfers between devices with their start and end apart: 19, of which 11 were waited for; matrix products, arithmetic and copies ran while one was open for 1% of the time, Pallas kernels for 12%

profile of v3, /device:TPU:0, one launch (start us, length us, event | category | flops | bytes accessed | tf_op | source)
XLA Modules:
  0.0 106.5 jit_solution(3804211228710074059)
XLA Ops:
  0.6 0.0 copy-start.2
  0.6 0.0 copy-start.4
  0.7 0.0 copy-start.5
  0.7 0.0 copy-start.6
  0.7 0.0 copy-start.3
  0.7 14.2 %forward.1 = (f32[104,256]{1,0:T(8,128)S(1)}, f32[104,256]{1,0:T(8,128)S(1)}, f32[104,256]{1,0:T(8,128)S(1)}, f32[104,256]{1,0:T(8,128)S(1)}, bf16[1024,2048]{1,...) custom-call(bf16[384,1024]{1,0:T(8,128)(2,1)} %bitcast.8, ...), custom_call_target="tpu_custom_call" | custom-call | flops 6400000000 | bytes 12000000 | tf_op jit(solution)/shard_map/forward/pallas_call | solution.py:298
  14.9 3.0 %collective-permute-start.1 = (f32[104,256]{1,0:T(8,128)S(1)}, f32[104,256]{1,0:T(8,128)S(1)}, u32[]{:S(2)}, u32[]{:S(2)}) collective-permute-start(f32[104,256]{1,0:T(8,128)S(1)} %get-tuple-element.41), channel_id=1, source_target_pairs={{0,96},{1,97},{2,98},{3,99},{4,100},{5,101},{6,102},{7,103},{8,104... | collective-permute-start | bytes 319496 | tf_op jit(solution)/shard_map/ppermute | solution.py:349
  17.9 0.2 collective-permute-start.2
  18.1 1.6 %collective-permute-start.3 = (f32[104,256]{1,0:T(8,128)S(1)}, f32[104,256]{1,0:T(8,128)S(1)}, u32[]{:S(2)}, u32[]{:S(2)}) collective-permute-start(f32[104,256]{1,0:T(8,128)S(1)} %get-tuple-element.43), channel_id=1, source_target_pairs={{0,64},{1,65},{2,66},{3,67},{4,68},{5,69},{6,70},{7,71},{8,72},{9,... | collective-permute-start | bytes 319496 | tf_op jit(solution)/shard_map/ppermute | solution.py:349
  19.7 0.0 collective-permute-start.4
  19.7 2.2 %collective-permute-done.1.f1 = f32[104,256]{1,0:T(8,128)S(1)} collective-permute-done((f32[104,256]{1,0:T(8,128)S(1)}, f32[104,256]{1,0:T(8,128)S(1)}, u32[]{:S(2)}, u32[]{:S(2)}) %collective-permute-start.1) | collective-permute-done | bytes 106528 | tf_op jit(solution)/shard_map/ppermute | solution.py:349
  21.9 0.0 collective-permute-start.5
  21.9 0.9 collective-permute-done.2.f2
  22.8 0.0 collective-permute-start.6
  22.8 1.9 %collective-permute-done.3.f3 = f32[104,256]{1,0:T(8,128)S(1)} collective-permute-done((f32[104,256]{1,0:T(8,128)S(1)}, f32[104,256]{1,0:T(8,128)S(1)}, u32[]{:S(2)}, u32[]{:S(2)}) %collective-permute-start.3) | collective-permute-done | bytes 106528 | tf_op jit(solution)/shard_map/ppermute | solution.py:349
  24.7 0.0 collective-permute-start.7
  24.7 0.0 collective-permute-done.4.c0
  24.7 0.0 collective-permute-done.5.c1
  24.7 0.0 collective-permute-done.6.c2
  24.7 1.3 %collective-permute-done.7.c3 = f32[104,256]{1,0:T(8,128)S(1)} collective-permute-done((f32[104,256]{1,0:T(8,128)S(1)}, f32[104,256]{1,0:T(8,128)S(1)}, u32[]{:S(2)}, u32[]{:S(2)}) %collective-permute-start.7) | collective-permute-done | bytes 106528 | tf_op jit(solution)/shard_map/ppermute | solution.py:349
  26.0 0.0 copy-done.2
  26.0 0.0 copy-done.5
  26.0 1.2 %slopes.1 = (bf16[112,256]{1,0:T(8,128)(2,1)S(1)}, bf16[112,256]{1,0:T(8,128)(2,1)S(1)}, bf16[112,256]{1,0:T(8,128)(2,1)S(1)}, bf16[112,256]{1,0:T(8,128)(2,1)S(1)}) custom-call(s32[16]{0:T(128)S(1)} %copy-done.5, f32[104,256]{1,0:T(8,128)S(1)} %get-tuple-element.40.f0, f32[104,256]{1,0:T(8,128)S(1)} %collective-permute-done.1.f1, ...), custom_call_target="tpu_custom_call" | custom-call | flops 20000000 | bytes 3000000 | tf_op jit(solution)/shard_map/slopes/pallas_call | solution.py:322
  27.2 2.0 %collective-permute-start.8 = (bf16[112,256]{1,0:T(8,128)(2,1)S(1)}, bf16[112,256]{1,0:T(8,128)(2,1)S(1)}, u32[]{:S(2)}, u32[]{:S(2)}) collective-permute-start(bf16[112,256]{1,0:T(8,128)(2,1)S(1)} %get-tuple-element.45), channel_id=1, source_target_pairs={{0,96},{1,97},{2,98},{3,99},{4,100},{5,101},{6,102},{7,103},{8,104... | collective-permute-start | bytes 172040 | tf_op jit(solution)/shard_map/ppermute | solution.py:349
  29.2 0.0 collective-permute-start.9
  29.2 2.7 %collective-permute-start.10 = (bf16[112,256]{1,0:T(8,128)(2,1)S(1)}, bf16[112,256]{1,0:T(8,128)(2,1)S(1)}, u32[]{:S(2)}, u32[]{:S(2)}) collective-permute-start(bf16[112,256]{1,0:T(8,128)(2,1)S(1)} %get-tuple-element.47), channel_id=1, source_target_pairs={{0,64},{1,65},{2,66},{3,67},{4,68},{5,69},{6,70},{7,71},{8,72},{9,... | collective-permute-start | bytes 172040 | tf_op jit(solution)/shard_map/ppermute | solution.py:349
  32.0 1.0 collective-permute-done.8.refs_1_
  33.0 0.8 collective-permute-done.9.refs_2_
  33.8 1.3 %collective-permute-done.10.refs_3_ = bf16[112,256]{1,0:T(8,128)(2,1)S(1)} collective-permute-done((bf16[112,256]{1,0:T(8,128)(2,1)S(1)}, bf16[112,256]{1,0:T(8,128)(2,1)S(1)}, u32[]{:S(2)}, u32[]{:S(2)}) %collective-permute-start.10) | collective-permute-done | bytes 57376 | tf_op jit(solution)/shard_map/ppermute | solution.py:349
  35.1 0.0 copy-done.3
  35.1 4.3 %upper_z.1 = (bf16[1024,1024]{1,0:T(8,128)(2,1)S(1)}, bf16[512,1024]{1,0:T(8,128)(2,1)S(1)}, bf16[512,1024]{1,0:T(8,128)(2,1)S(1)}, bf16[128,1024]{1,0:T(8,128)(2,1)S(1)}, bf16[128,1024]{1,0:T(8,128)(2,1)S(1)}) custom-call(bf16[112,256]{1,0:T(8,128)(2,1)S(1)} %get-tuple-element.44.refs_0_, bf16[112,256]{1,0:T(8,128)(2,1)S(1)} %collective-permute-done.8.refs_1_, ...), custom_call_target="tpu_custom_call" | custom-call | flops 2700000000 | bytes 2000000 | tf_op jit(solution)/shard_map/upper_z/pallas_call | solution.py:322
  39.4 0.1 collective-permute-start.13
  39.5 0.0 copy-start.7
  39.5 3.4 %upper_x.1 = (bf16[1024,1024]{1,0:T(8,128)(2,1)S(1)}, bf16[512,1024]{1,0:T(8,128)(2,1)S(1)}, bf16[512,1024]{1,0:T(8,128)(2,1)S(1)}) custom-call(bf16[112,256]{1,0:T(8,128)(2,1)S(1)} %get-tuple-element.44.refs_0_, bf16[112,256]{1,0:T(8,128)(2,1)S(1)} %collective-permute-done.8.refs_1_, bf16[112,256]{1,0:T(8,128)(2,1)S(1)} %collective-permute-done.9.refs_2_, ...), custom_call_target="tpu_custom_call" | custom-call | flops 2700000000 | bytes 2000000 | tf_op jit(solution)/shard_map/upper_x/pallas_call | solution.py:322
  42.9 0.0 copy-start.8
  43.0 0.6 collective-permute-start.11
  43.6 0.0 collective-permute-done.13
  43.6 0.2 add_convert_fusion.1
  43.8 2.0 %collective-permute-start.14 = (bf16[512,512]{1,0:T(8,128)(2,1)S(1)}, bf16[512,512]{1,0:T(8,128)(2,1)S(1)}, u32[]{:S(2)}, u32[]{:S(2)}) collective-permute-start(bf16[512,512]{1,0:T(8,128)(2,1)S(1)} %add_convert_fusion.1), channel_id=1, source_target_pairs={{0,4},{1,5},{2,6},{3,7},{4,0},{5,1},{6,2},{7,3},{8,12},{9,13},{10,... | collective-permute-start | bytes 1572872 | tf_op jit(solution)/shard_map/ppermute | solution.py:349
  45.8 0.1 collective-permute-done.11
  45.9 0.2 add_convert_fusion.3
  46.1 2.1 %collective-permute-start.12 = (bf16[512,512]{1,0:T(8,128)(2,1)S(1)}, bf16[512,512]{1,0:T(8,128)(2,1)S(1)}, u32[]{:S(2)}, u32[]{:S(2)}) collective-permute-start(bf16[512,512]{1,0:T(8,128)(2,1)S(1)} %add_convert_fusion.3), channel_id=1, source_target_pairs={{0,32},{1,33},{2,34},{3,35},{4,36},{5,37},{6,38},{7,39},{8,40},{9,... | collective-permute-start | bytes 1572872 | tf_op jit(solution)/shard_map/ppermute | solution.py:349
  48.2 6.8 %lower.1 = (bf16[192,1024]{1,0:T(8,128)(2,1)S(1)}, bf16[208,1024]{1,0:T(8,128)(2,1)S(1)}) custom-call(bf16[1024,1024]{1,0:T(8,128)(2,1)S(1)} %get-tuple-element.57.pga_ref, bf16[1024,1024]{1,0:T(8,128)(2,1)S(1)} %get-tuple-element.58.pgb_ref, bf16[1024,2048]{1,0:T(8,128)(2,1)S(1)} %copy-done.7, bf16[1024,1024]{1,0:T(8,128)(2,1)S(1)} %get-tuple-element.49.refs_6_.nrm_ref, ...), custom_call_target="tpu_custom_call" | custom-call | flops 5100000256 | bytes 8000000 | tf_op jit(solution)/shard_map/lower/pallas_call | solution.py:322
  55.0 0.0 copy-start.1
  55.0 0.0 collective-permute-done.14
  55.0 0.3 add_convert_fusion.second_ref
  55.3 0.2 collective-permute-done.12
  55.5 0.3 add_convert_fusion.2.first_ref
  55.8 2.0 %collective-permute-start.16 = (bf16[208,1024]{1,0:T(8,128)(2,1)S(1)}, bf16[208,1024]{1,0:T(8,128)(2,1)S(1)}, u32[]{:S(2)}, u32[]{:S(2)}) collective-permute-start(bf16[208,1024]{1,0:T(8,128)(2,1)S(1)} %get-tuple-element.64.rest_ref), channel_id=1, source_target_pairs={{0,16},{1,17},{2,18},{3,19},{4,20},{5,21},{6,22},{7,23},{8,24},{9,... | collective-permute-start | bytes 1277960 | tf_op jit(solution)/shard_map/ppermute | solution.py:349
  57.8 0.1 collective-permute-start
  57.9 0.4 collective-permute-start.15
  58.3 0.1 collective-permute-start.17
  58.4 1.4 %collective-permute-done.lat_recv = bf16[384,512]{1,0:T(8,128)(2,1)S(1)} collective-permute-done((bf16[384,512]{1,0:T(8,128)(2,1)S(1)}, bf16[384,512]{1,0:T(8,128)(2,1)S(1)}, u32[]{:S(2)}, u32[]{:S(2)}) %collective-permute-start) | collective-permute-done | bytes 393248 | tf_op jit(solution)/shard_map/ppermute | solution.py:349
  59.7 0.9 collective-permute-done.17.go_recv
  60.7 0.0 collective-permute-done.15.top_recv
  60.7 0.0 collective-permute-done.16.rest_recv
  60.7 0.0 copy-done.1
  60.7 2.7 %grad_value.1 = bf16[512,2304]{1,0:T(8,128)(2,1)} custom-call(bf16[384,1024]{1,0:T(8,128)(2,1)S(1)} %bitcast.9, bf16[384,512]{1,0:T(8,128)(2,1)S(1)} %collective-permute-done.lat_recv, bf16[192,1024]{1,0:T(8,128)(2,1)S(1)} %get-tuple-element.63.top_ref, bf16[208,1024]{1,0:T(8,128)(2,1)S(1)} %get-tuple-element.64.rest_ref, ...), custom_call_target="tpu_custom_call" | custom-call | flops 800000000 | bytes 6000000 | tf_op jit(solution)/shard_map/grad_value/pallas_call | solution.py:322
  63.4 9.5 %all-to-all-start = ((bf16[64,8,2304]{2,1,0:T(8,128)(2,1)}), bf16[64,8,2304]{2,1,0:T(8,128)(2,1)S(1)}, u32[]{:S(2)}, u32[]{:S(2)}) async-start(bf16[64,8,2304]{2,1,0:T(8,128)(2,1)} %bitcast.14), calls=%async_computation | async-start | bytes 4718592 | tf_op jit(solution)/shard_map/all_to_all | solution.py:410
  72.9 0.0 copy-start
  72.9 1.6 %copy-done = bf16[1024,1024]{1,0:T(8,128)(2,1)S(1)} copy-done((bf16[1024,1024]{1,0:T(8,128)(2,1)S(1)}, bf16[1024,1024]{1,0:T(8,128)(2,1)}, u32[]{:S(2)}) %copy-start) | copy-done | bytes 2097176
  74.5 2.4 %grad_latents.1 = bf16[384,1024]{1,0:T(8,128)(2,1)} custom-call(bf16[192,1024]{1,0:T(8,128)(2,1)S(1)} %get-tuple-element.63.top_ref, bf16[208,1024]{1,0:T(8,128)(2,1)S(1)} %get-tuple-element.64.rest_ref, bf16[1024,1024]{1,0:T(8,128)(2,1)S(1)} %copy-done), custom_call_target="tpu_custom_call" | custom-call | flops 800000000 | bytes 4000000 | tf_op jit(solution)/shard_map/grad_latents/pallas_call | solution.py:322
  76.9 28.6 %all-to-all-done.met_ref = bf16[64,8,2304]{2,1,0:T(8,128)(2,1)S(1)} async-done(((bf16[64,8,2304]{2,1,0:T(8,128)(2,1)}), bf16[64,8,2304]{2,1,0:T(8,128)(2,1)S(1)}, u32[]{:S(2)}, u32[]{:S(2)}) %all-to-all-start) | async-done | bytes 2359328 | tf_op jit(solution)/shard_map/all_to_all | solution.py:410
  105.5 1.0 final.1
  (4 shorter events, 0.0 us)
Async XLA Ops:
  0.6 25.4 %copy-start.2 = (f32[100,1024]{1,0:T(8,128)S(1)}, f32[100,1024]{1,0:T(8,128)}, u32[]{:S(2)}) copy-start(f32[100,1024]{1,0:T(8,128)} %tg_ref.1) | copy-start | bytes 1228804
  0.6 25.4 %copy-start.4 = (f32[1024]{0:T(1024)S(1)}, f32[1024]{0:T(1024)}, u32[]{:S(2)}) copy-start(f32[1024]{0:T(1024)} %param.22) | copy-start | bytes 12292
  0.7 25.3 %copy-start.5 = (s32[16]{0:T(128)S(1)}, s32[16]{0:T(128)}, u32[]{:S(2)}) copy-start(s32[16]{0:T(128)} %vc_ref.1) | copy-start | bytes 196
  0.7 25.3 %copy-start.6 = (f32[100]{0:T(128)S(1)}, f32[100]{0:T(128)}, u32[]{:S(2)}) copy-start(f32[100]{0:T(128)} %param.21) | copy-start | bytes 1204
  0.7 34.5 %copy-start.3 = (bf16[100,2048]{1,0:T(8,128)(2,1)S(1)}, bf16[100,2048]{1,0:T(8,128)(2,1)}, u32[]{:S(2)}) copy-start(bf16[100,2048]{1,0:T(8,128)(2,1)} %refs_4_.3) | copy-start | bytes 1228804
  14.9 7.0 %collective-permute-start.1 = (f32[104,256]{1,0:T(8,128)S(1)}, f32[104,256]{1,0:T(8,128)S(1)}, u32[]{:S(2)}, u32[]{:S(2)}) collective-permute-start(f32[104,256]{1,0:T(8,128)S(1)} %get-tuple-element.41), channel_id=1, source_target_pairs={{0,96},{1,97},{2,98},{3,99},{4,100},{5,101},{6,102},{7,103},{8,104... | collective-permute-start | bytes 319496 | tf_op jit(solution)/shard_map/ppermute | solution.py:349
  17.9 4.9 %collective-permute-start.2 = (f32[104,256]{1,0:T(8,128)S(1)}, f32[104,256]{1,0:T(8,128)S(1)}, u32[]{:S(2)}, u32[]{:S(2)}) collective-permute-start(f32[104,256]{1,0:T(8,128)S(1)} %get-tuple-element.42), channel_id=1, source_target_pairs={{0,32},{1,33},{2,34},{3,35},{4,36},{5,37},{6,38},{7,39},{8,40},{9,... | collective-permute-start | bytes 319496 | tf_op jit(solution)/shard_map/ppermute | solution.py:349
  18.1 6.6 %collective-permute-start.3 = (f32[104,256]{1,0:T(8,128)S(1)}, f32[104,256]{1,0:T(8,128)S(1)}, u32[]{:S(2)}, u32[]{:S(2)}) collective-permute-start(f32[104,256]{1,0:T(8,128)S(1)} %get-tuple-element.43), channel_id=1, source_target_pairs={{0,64},{1,65},{2,66},{3,67},{4,68},{5,69},{6,70},{7,71},{8,72},{9,... | collective-permute-start | bytes 319496 | tf_op jit(solution)/shard_map/ppermute | solution.py:349
  19.7 5.0 %collective-permute-start.4 = (f32[104,256]{1,0:T(8,128)S(1)}, f32[104,256]{1,0:T(8,128)S(1)}, u32[]{:S(2)}, u32[]{:S(2)}) collective-permute-start(f32[104,256]{1,0:T(8,128)S(1)} %get-tuple-element.40.f0), channel_id=1, source_target_pairs={{0,16},{1,17},{2,18},{3,19},{4,20},{5,21},{6,22},{7,23},{8,24},{9,... | collective-permute-start | bytes 319496 | tf_op jit(solution)/shard_map/ppermute | solution.py:349
  21.9 2.8 %collective-permute-start.5 = (f32[104,256]{1,0:T(8,128)S(1)}, f32[104,256]{1,0:T(8,128)S(1)}, u32[]{:S(2)}, u32[]{:S(2)}) collective-permute-start(f32[104,256]{1,0:T(8,128)S(1)} %collective-permute-done.1.f1), channel_id=1, source_target_pairs={{0,16},{1,17},{2,18},{3,19},{4,20},{5,21},{6,22},{7,23},{8,24},{9,... | collective-permute-start | bytes 319496 | tf_op jit(solution)/shard_map/ppermute | solution.py:349
  22.8 1.9 %collective-permute-start.6 = (f32[104,256]{1,0:T(8,128)S(1)}, f32[104,256]{1,0:T(8,128)S(1)}, u32[]{:S(2)}, u32[]{:S(2)}) collective-permute-start(f32[104,256]{1,0:T(8,128)S(1)} %collective-permute-done.2.f2), channel_id=1, source_target_pairs={{0,16},{1,17},{2,18},{3,19},{4,20},{5,21},{6,22},{7,23},{8,24},{9,... | collective-permute-start | bytes 319496 | tf_op jit(solution)/shard_map/ppermute | solution.py:349
  24.7 1.3 %collective-permute-start.7 = (f32[104,256]{1,0:T(8,128)S(1)}, f32[104,256]{1,0:T(8,128)S(1)}, u32[]{:S(2)}, u32[]{:S(2)}) collective-permute-start(f32[104,256]{1,0:T(8,128)S(1)} %collective-permute-done.3.f3), channel_id=1, source_target_pairs={{0,16},{1,17},{2,18},{3,19},{4,20},{5,21},{6,22},{7,23},{8,24},{9,... | collective-permute-start | bytes 319496 | tf_op jit(solution)/shard_map/ppermute | solution.py:349
  27.2 5.8 %collective-permute-start.8 = (bf16[112,256]{1,0:T(8,128)(2,1)S(1)}, bf16[112,256]{1,0:T(8,128)(2,1)S(1)}, u32[]{:S(2)}, u32[]{:S(2)}) collective-permute-start(bf16[112,256]{1,0:T(8,128)(2,1)S(1)} %get-tuple-element.45), channel_id=1, source_target_pairs={{0,96},{1,97},{2,98},{3,99},{4,100},{5,101},{6,102},{7,103},{8,104... | collective-permute-start | bytes 172040 | tf_op jit(solution)/shard_map/ppermute | solution.py:349
  29.2 4.6 %collective-permute-start.9 = (bf16[112,256]{1,0:T(8,128)(2,1)S(1)}, bf16[112,256]{1,0:T(8,128)(2,1)S(1)}, u32[]{:S(2)}, u32[]{:S(2)}) collective-permute-start(bf16[112,256]{1,0:T(8,128)(2,1)S(1)} %get-tuple-element.46), channel_id=1, source_target_pairs={{0,32},{1,33},{2,34},{3,35},{4,36},{5,37},{6,38},{7,39},{8,40},{9,... | collective-permute-start | bytes 172040 | tf_op jit(solution)/shard_map/ppermute | solution.py:349
  29.2 5.9 %collective-permute-start.10 = (bf16[112,256]{1,0:T(8,128)(2,1)S(1)}, bf16[112,256]{1,0:T(8,128)(2,1)S(1)}, u32[]{:S(2)}, u32[]{:S(2)}) collective-permute-start(bf16[112,256]{1,0:T(8,128)(2,1)S(1)} %get-tuple-element.47), channel_id=1, source_target_pairs={{0,64},{1,65},{2,66},{3,67},{4,68},{5,69},{6,70},{7,71},{8,72},{9,... | collective-permute-start | bytes 172040 | tf_op jit(solution)/shard_map/ppermute | solution.py:349
  39.4 4.2 %collective-permute-start.13 = (bf16[512,1024]{1,0:T(8,128)(2,1)S(1)}, bf16[512,1024]{1,0:T(8,128)(2,1)S(1)}, u32[]{:S(2)}, u32[]{:S(2)}) collective-permute-start(bf16[512,1024]{1,0:T(8,128)(2,1)S(1)} %get-tuple-element.56), channel_id=1, source_target_pairs={{0,16},{1,17},{2,18},{3,19},{4,20},{5,21},{6,22},{7,23},{8,24},{9,... | collective-permute-start | bytes 3145736 | tf_op jit(solution)/shard_map/ppermute | solution.py:349
  39.5 8.7 %copy-start.7 = (bf16[1024,2048]{1,0:T(8,128)(2,1)S(1)}, bf16[1024,2048]{1,0:T(8,128)(2,1)}, u32[]{:S(2)}) copy-start(bf16[1024,2048]{1,0:T(8,128)(2,1)} %wh_ref.1) | copy-start | bytes 12582916
  42.9 5.2 %copy-start.8 = (f32[1024]{0:T(1024)S(1)}, f32[1024]{0:T(1024)}, u32[]{:S(2)}) copy-start(f32[1024]{0:T(1024)} %param.17) | copy-start | bytes 12292
  43.0 2.9 %collective-permute-start.11 = (bf16[512,1024]{1,0:T(8,128)(2,1)S(1)}, bf16[512,1024]{1,0:T(8,128)(2,1)S(1)}, u32[]{:S(2)}, u32[]{:S(2)}) collective-permute-start(bf16[512,1024]{1,0:T(8,128)(2,1)S(1)} %get-tuple-element.51), channel_id=1, source_target_pairs={{0,16},{1,17},{2,18},{3,19},{4,20},{5,21},{6,22},{7,23},{8,24},{9,... | collective-permute-start | bytes 3145736 | tf_op jit(solution)/shard_map/ppermute | solution.py:349
  43.8 11.2 %collective-permute-start.14 = (bf16[512,512]{1,0:T(8,128)(2,1)S(1)}, bf16[512,512]{1,0:T(8,128)(2,1)S(1)}, u32[]{:S(2)}, u32[]{:S(2)}) collective-permute-start(bf16[512,512]{1,0:T(8,128)(2,1)S(1)} %add_convert_fusion.1), channel_id=1, source_target_pairs={{0,4},{1,5},{2,6},{3,7},{4,0},{5,1},{6,2},{7,3},{8,12},{9,13},{10,... | collective-permute-start | bytes 1572872 | tf_op jit(solution)/shard_map/ppermute | solution.py:349
  46.1 9.5 %collective-permute-start.12 = (bf16[512,512]{1,0:T(8,128)(2,1)S(1)}, bf16[512,512]{1,0:T(8,128)(2,1)S(1)}, u32[]{:S(2)}, u32[]{:S(2)}) collective-permute-start(bf16[512,512]{1,0:T(8,128)(2,1)S(1)} %add_convert_fusion.3), channel_id=1, source_target_pairs={{0,32},{1,33},{2,34},{3,35},{4,36},{5,37},{6,38},{7,39},{8,40},{9,... | collective-permute-start | bytes 1572872 | tf_op jit(solution)/shard_map/ppermute | solution.py:349
  55.0 5.7 %copy-start.1 = (bf16[1,384,1024]{2,1,0:T(8,128)(2,1)S(1)}, bf16[1,384,1024]{2,1,0:T(8,128)(2,1)}, u32[]{:S(2)}) copy-start(bf16[1,384,1024]{2,1,0:T(8,128)(2,1)} %param.12) | copy-start | bytes 2359300
  55.8 4.9 %collective-permute-start.16 = (bf16[208,1024]{1,0:T(8,128)(2,1)S(1)}, bf16[208,1024]{1,0:T(8,128)(2,1)S(1)}, u32[]{:S(2)}, u32[]{:S(2)}) collective-permute-start(bf16[208,1024]{1,0:T(8,128)(2,1)S(1)} %get-tuple-element.64.rest_ref), channel_id=1, source_target_pairs={{0,16},{1,17},{2,18},{3,19},{4,20},{5,21},{6,22},{7,23},{8,24},{9,... | collective-permute-start | bytes 1277960 | tf_op jit(solution)/shard_map/ppermute | solution.py:349
  57.8 2.0 %collective-permute-start = (bf16[384,512]{1,0:T(8,128)(2,1)S(1)}, bf16[384,512]{1,0:T(8,128)(2,1)S(1)}, u32[]{:S(2)}, u32[]{:S(2)}) collective-permute-start(bf16[384,512]{1,0:T(8,128)(2,1)S(1)} %get-tuple-element.39), channel_id=1, source_target_pairs={{0,16},{1,17},{2,18},{3,19},{4,20},{5,21},{6,22},{7,23},{8,24},{9,... | collective-permute-start | bytes 1179656 | tf_op jit(solution)/shard_map/ppermute | solution.py:349
  57.9 2.8 %collective-permute-start.15 = (bf16[192,1024]{1,0:T(8,128)(2,1)S(1)}, bf16[192,1024]{1,0:T(8,128)(2,1)S(1)}, u32[]{:S(2)}, u32[]{:S(2)}) collective-permute-start(bf16[192,1024]{1,0:T(8,128)(2,1)S(1)} %get-tuple-element.63.top_ref), channel_id=1, source_target_pairs={{0,16},{1,17},{2,18},{3,19},{4,20},{5,21},{6,22},{7,23},{8,24},{9,... | collective-permute-start | bytes 1179656 | tf_op jit(solution)/shard_map/ppermute | solution.py:349
  58.3 2.4 %collective-permute-start.17 = (bf16[128,1024]{1,0:T(8,128)(2,1)S(1)}, bf16[128,1024]{1,0:T(8,128)(2,1)S(1)}, u32[]{:S(2)}, u32[]{:S(2)}) collective-permute-start(bf16[128,1024]{1,0:T(8,128)(2,1)S(1)} %get-tuple-element.66), channel_id=1, source_target_pairs={{0,16},{1,17},{2,18},{3,19},{4,20},{5,21},{6,22},{7,23},{8,24},{9,... | collective-permute-start | bytes 786440 | tf_op jit(solution)/shard_map/ppermute | solution.py:349
  63.4 42.1 %all-to-all-start = ((bf16[64,8,2304]{2,1,0:T(8,128)(2,1)}), bf16[64,8,2304]{2,1,0:T(8,128)(2,1)S(1)}, u32[]{:S(2)}, u32[]{:S(2)}) async-start(bf16[64,8,2304]{2,1,0:T(8,128)(2,1)} %bitcast.14), calls=%async_computation | async-start | bytes 4718592 | tf_op jit(solution)/shard_map/all_to_all | solution.py:410
  72.9 1.6 %copy-start = (bf16[1024,1024]{1,0:T(8,128)(2,1)S(1)}, bf16[1024,1024]{1,0:T(8,128)(2,1)}, u32[]{:S(2)}) copy-start(bf16[1024,1024]{1,0:T(8,128)(2,1)} %wv_ref.1) | copy-start | bytes 6291460

commit v4 on v3

--- a/solution.py
+++ b/solution.py
@@ -59,9 +59,27 @@
     return lax.dot_general(a, b, (dims, ((), ())), preferred_element_type=F32)
 
 
+def cdf_of(pre):
+    return 0.5 + 0.5 * jnp.tanh(pre * (GELU_C + (GELU_C * 0.044715) * (pre * pre)))
+
+
+def gelu_slope_kernel(pre_ref, dg_ref):
+    def body(q, carry):
+        for part in range(4):
+            rows = pl.ds(pl.multiple_of(q * 64 + 16 * part, 16), 16)
+            pre = pre_ref[rows, :].astype(F32)
+            square = pre * pre
+            t = jnp.tanh(pre * (GELU_C + (GELU_C * 0.044715) * square))
+            inner = pre * (GELU_C + (3 * GELU_C * 0.044715) * square)
+            dg_ref[rows, :] = ((0.5 + 0.5 * t) * (1.0 + (1.0 - t) * inner)).astype(BF)
+        return carry
+
+    lax.fori_loop(0, pre_ref.shape[0] // 64, body, 0)
+
+
 def forward_kernel(
     lat_hbm, wv_hbm, nb_hbm, cf_hbm, emb_hbm, gain_hbm, wh_hbm, ow_hbm,
-    f0, f1, f2, f3, hid_ref, dg_ref, nrm, inv_ref, st_ref, lat_send,
+    f0, f1, f2, f3, hid_ref, pre_ref, nrm, inv_ref, st_ref, lat_send,
     total, lat, wv, emb, wh, ow, nb_ref, cf_ref, gain_ref, sems,
 ):
     nodes, points = st_ref.shape
@@ -101,17 +119,15 @@
         nrm[rows, :] = (summed * inv * gain_ref[...]).astype(BF)
     copies[small].wait()
     for tile in range(hidden // wide):
-        here = slice(wide * tile, wide * tile + wide)
         copies[3 + tile].wait()
         for r in range(points // 256):
             rows = slice(256 * r, 256 * r + 256)
-            pre = dot(nrm[rows, :], wh[:, here])
-            square = pre * pre
-            t = jnp.tanh(pre * (GELU_C + (GELU_C * 0.044715) * square))
-            cdf = 0.5 + 0.5 * t
-            hid_ref[rows, here] = (pre * cdf).astype(BF)
-            inner = pre * (GELU_C + (3 * GELU_C * 0.044715) * square)
-            dg_ref[rows, here] = (cdf * (1.0 + (1.0 - t) * inner)).astype(BF)
+            for first in range(wide * tile, wide * tile + wide, 256):
+                here = slice(first, first + 256)
+                pre = dot(nrm[rows, :], wh[:, here])
+                pre_ref[rows, here] = pre.astype(BF)
+                hid_ref[rows, here] = (pre * cdf_of(pre)).astype(BF)
+        here = slice(wide * tile, wide * tile + wide)
         total[0:100, :] += dot(ow[:, here], hid_ref[:, here], ((1,), (1,)))
     for f, m in zip((f0, f1, f2, f3), masks(own["c"])):
         f[...] = total[:, pl.ds(pl.multiple_of((own["x"] ^ m) * 256, 256), 256)]
@@ -154,44 +170,48 @@
         s[...] = held[a].astype(BF)
 
 
+def gather_slopes(parts, slopes):
+    own = own_place()
+    for s, m in zip(parts, masks(own["c"])):
+        at = pl.ds(pl.multiple_of((own["x"] ^ m) * 256, 256), 256)
+        slopes[0:112, at] = s[...]
+    slopes[112:128, :] = jnp.zeros((16, slopes.shape[1]), BF)
+
+
+def out_kernel(s0, s1, s2, s3, hid_ref, go_keep, go_send, slopes, go):
+    core = lax.axis_index("core")
+    gather_slopes((s0, s1, s2, s3), slopes)
+    go[...] = dot(slopes[...], hid_ref[...])
+    for x in range(4):
+        for ref, c in ((go_keep, core), (go_send, 1 - core)):
+            columns = pl.ds(pl.multiple_of(x * 512 + c * 256, 256), 256)
+            ref[:, 256 * x : 256 * x + 256] = go[:, columns].astype(BF)
+
+
 def upper_kernel(
-    axis, s0, s1, s2, s3, ow_ref, dg_ref, nrm_ref, *rest
+    axis, s0, s1, s2, s3, ow_ref, dg_ref, nrm_ref, pg_ref, keep_ref, send_ref, slopes, own_w, result_0, result_1
 ):
-    if axis == "z":
-        hid_ref, pg_ref, keep_ref, send_ref, go_keep, go_send, slopes, own_w, result, go = rest
-    else:
-        pg_ref, keep_ref, send_ref, slopes, own_w, result = rest
     points = nrm_ref.shape[0]
     offset = 1024 if axis == "z" else 0
     own = own_place()
-    for s, m in zip((s0, s1, s2, s3), masks(own["c"])):
-        at = pl.ds(pl.multiple_of((own["x"] ^ m) * 256, 256), 256)
-        slopes[0:112, at] = s[...]
-    slopes[112:128, :] = jnp.zeros((16, points), BF)
+    gather_slopes((s0, s1, s2, s3), slopes)
     own_w[96:128, :] = jnp.zeros((32, 1024), BF)
     own_w[0:100, :] = ow_ref[:, offset : offset + 1024]
     for r in range(points // 256):
         rows = slice(256 * r, 256 * r + 256)
         grad = dot(slopes[:, rows], own_w[...], ((0,), (0,)))
         pg_ref[rows, :] = (dg_ref[rows, offset : offset + 1024].astype(F32) * grad).astype(BF)
-    for tile in range(2):
+    for tile, result in enumerate((result_0, result_1)):
         result[...] = dot(nrm_ref[...], pg_ref[:, 512 * tile : 512 * tile + 512], ((0,), (0,)))
         columns = pl.ds(pl.multiple_of((tile ^ (own[axis] & 1)) * 512, 512), 512)
         for ref, core in ((keep_ref, own["c"]), (send_ref, 1 - own["c"])):
             for x in range(4):
                 rows = pl.ds(pl.multiple_of(x * 256 + core * 128, 128), 128)
                 ref[128 * x : 128 * x + 128, columns] = result[rows, :].astype(BF)
-    if axis == "z":
-        go[...] = dot(slopes[...], hid_ref[...])
-        for x in range(4):
-            for ref, core in ((go_keep, own["c"]), (go_send, 1 - own["c"])):
-                columns = pl.ds(pl.multiple_of(x * 512 + core * 256, 256), 256)
-                ref[:, 256 * x : 256 * x + 256] = go[:, columns].astype(BF)
-
-
-def lower_kernel(pga_ref, pgb_ref, wh_ref, nrm_ref, inv_ref, gain_ref, st_ref, top_ref, rest_ref, value_sum):
+
+
+def lower_kernel(pga_ref, pgb_ref, wh_ref, nrm_ref, inv_ref, gain_ref, st_ref, vg_ref, summed):
     nodes, points = st_ref.shape
-    top = top_ref.shape[0]
     gain = gain_ref[...]
     over_gain = 1.0 / gain
     gain_sum = jnp.zeros_like(gain)
@@ -204,54 +224,55 @@
         gain_sum = gain_sum + jnp.sum(product, axis=0, keepdims=True)
         mean = jnp.mean(product, axis=-1, keepdims=True)
         summed_grad = inv_ref[rows, :] * (normed_grad * gain - normed * over_gain * mean)
-        part = dot(st_ref[:, rows], summed_grad.astype(BF))
-        value_sum[...] = part if r == 0 else value_sum[...] + part
-    top_ref[...] = value_sum[0:top, :].astype(BF)
-    rest_ref[0 : nodes - top, :] = value_sum[top:nodes, :].astype(BF)
-    rest_ref[nodes - top :, :] = jnp.broadcast_to(gain_sum * over_gain, (16, gain.shape[1])).astype(BF)
-
-
-def latents_kernel(top_ref, rest_ref, wv_ref, gl_ref):
-    top = top_ref.shape[0]
-    gl_ref[0:top, :] = dot(top_ref[...], wv_ref[...], ((1,), (1,))).astype(BF)
-    gl_ref[top:, :] = dot(rest_ref[0 : gl_ref.shape[0] - top, :], wv_ref[...], ((1,), (1,))).astype(BF)
+        summed[rows, :] = summed_grad.astype(BF)
+    vg_ref[0:nodes, :] = dot(st_ref[...], summed[...]).astype(BF)
+    vg_ref[nodes:, :] = jnp.broadcast_to(gain_sum * over_gain, (16, gain.shape[1])).astype(BF)
+
+
+def latents_kernel(vg_ref, wv_ref, gl_ref):
+    gl_ref[...] = dot(vg_ref[0 : gl_ref.shape[0], :], wv_ref[...], ((1,), (1,))).astype(BF)
+
+
+def prepare_kernel(lat_ref, go_keep, go_recv, own_lat, out_ref):
+    core = lax.axis_index("core")
+    for x in range(4):
+        columns = pl.ds(pl.multiple_of(x * 256 + core * 128, 128), 128)
+        own_lat[:, 128 * x : 128 * x + 128] = lat_ref[:, columns]
+    out = (go_keep[...].astype(F32) + go_recv[...].astype(F32)).T.reshape(64, 2, 8, 128)
+    for k in range(2):
+        out_ref[:, 128 * k : 128 * k + 128] = out[:, k].reshape(512, 128).astype(BF)
 
 
 def value_kernel(
-    lat_ref, lat_recv, top_ref, rest_ref, top_recv, rest_recv, go_keep, go_recv, first_ref, second_ref,
-    out_hbm, own_lat, gain_turned, block, sems,
+    own_lat, lat_recv, vg_ref, vg_recv, out_ref, first_ref, second_ref,
+    out_hbm, gain_turned, block, sems,
 ):
-    nodes, width = lat_ref.shape
+    nodes, width = own_lat.shape[0], vg_ref.shape[1]
     variables = 100
     core = lax.axis_index("core")
     copies = [
         pltpu.make_async_copy(first_ref, out_hbm.at[:, 0:512], sems.at[0]),
         pltpu.make_async_copy(second_ref, out_hbm.at[:, 512:1024], sems.at[1]),
-        pltpu.make_async_copy(block, out_hbm.at[:, 1024:], sems.at[2]),
+        pltpu.make_async_copy(block.at[0:256, :], out_hbm.at[0:256, 1024:], sems.at[2]),
+        pltpu.make_async_copy(block.at[256:512, :], out_hbm.at[256:512, 1024:], sems.at[3]),
     ]
     copies[0].start()
     copies[1].start()
-    top = top_ref.shape[0]
-    bottom = nodes - top
-    gain = rest_ref[bottom:, :].astype(F32)[0:8] + rest_recv[bottom:, :].astype(F32)[0:8]
+    gain = vg_ref[nodes:, :].astype(F32)[0:8] + vg_recv[nodes:, :].astype(F32)[0:8]
     gain_turned[...] = jnp.broadcast_to(gain[0:1], (128, width)).T
-    for x in range(4):
-        columns = pl.ds(pl.multiple_of(x * 256 + core * 128, 128), 128)
-        own_lat[:, 128 * x : 128 * x + 128] = lat_ref[:, columns]
-    value = dot(own_lat[0:top, :], top_ref[...], ((0,), (0,)))
-    value = value + dot(own_lat[top:, :], rest_ref[0:bottom, :], ((0,), (0,)))
-    value = value + dot(lat_recv[0:top, :], top_recv[...], ((0,), (0,)))
-    value = value + dot(lat_recv[top:, :], rest_recv[0:bottom, :], ((0,), (0,)))
-    block[:, 0:width] = value.astype(BF)
-    out = (go_keep[...].astype(F32) + go_recv[...].astype(F32)).T.reshape(64, 2, 8, 128)
     lane = lax.broadcasted_iota(jnp.int32, (128, 128), 1)
-    for x in range(4):
-        rows = slice(128 * x, 128 * x + 128)
-        own_gain = gain_turned[pl.ds(pl.multiple_of(x * 256 + core * 128, 128), 128), :]
-        first = out[16 * x : 16 * x + 16, 0].reshape(128, 128)
-        block[rows, width : width + 128] = jnp.where(lane == variables, own_gain, first).astype(BF)
-        block[rows, width + 128 :] = out[16 * x : 16 * x + 16, 1].reshape(128, 128).astype(BF)
-    copies[2].start()
+    for part in range(2):
+        here = slice(256 * part, 256 * part + 256)
+        value = dot(own_lat[:, here], vg_ref[0:nodes, :], ((0,), (0,)))
+        value = value + dot(lat_recv[:, here], vg_recv[0:nodes, :], ((0,), (0,)))
+        block[here, 0:width] = value.astype(BF)
+        for x in (2 * part, 2 * part + 1):
+            rows = slice(128 * x, 128 * x + 128)
+            own_gain = gain_turned[pl.ds(pl.multiple_of(x * 256 + core * 128, 128), 128), :]
+            first = out_ref[rows, 0:128].astype(F32)
+            block[rows, width : width + 128] = jnp.where(lane == variables, own_gain, first).astype(BF)
+        block[here, width + 128 :] = out_ref[here, 128:]
+        copies[2 + part].start()
     for copy in copies:
         copy.wait()
 
@@ -331,17 +352,14 @@
     )(*args)
 
 
-def upper(axis, parts, ow, dg, nrm, *hid):
+def upper(axis, parts, ow, dg, nrm):
     points, width = nrm.shape
     half = like((width // 2, 1024))
     out_shape = [pltpu.VMEM((points, 1024), BF), half, half]
-    scratch = [pltpu.VMEM((128, points), BF), pltpu.VMEM((128, 1024), BF), pltpu.VMEM((width, 512), F32)]
-    if axis == "z":
-        out_shape += [like((128, 1024)), like((128, 1024))]
-        scratch.append(pltpu.VMEM((128, 2048), F32))
+    scratch = [pltpu.VMEM((128, points), BF), pltpu.VMEM((128, 1024), BF)] + [pltpu.VMEM((width, 512), F32)] * 2
     return in_vmem(
         lambda *refs: upper_kernel(axis, *refs), "upper_" + axis, out_shape, scratch, cost(2_700_000_000, 2_000_000), 20,
-        *parts, ow, *held(dg, nrm, *hid),
+        *parts, ow, *held(dg, nrm),
     )
 
 
@@ -359,14 +377,20 @@
 ):
     lat = latents[0]
     gain_row = gain[None, :]
-    f0, f1, f2, f3, hid, dg, nrm, inv, st, lat_send = forward(
+    f0, f1, f2, f3, hid, pre, nrm, inv, st, lat_send = forward(
         lat, w_value, neighbours, edge_coef, grid_embed, gain_row, w_hidden, output_weight
     )
     core = core_pairs()
     r3 = permute(f3, x_pairs(3))
     r1 = permute(f1, x_pairs(1))
     r2 = permute(f2, x_pairs(2))
+    lat_recv = permute(lat_send, core)
+    dg = in_vmem(
+        gelu_slope_kernel, "gelu_slope", pltpu.VMEM(pre.shape, BF), [], cost(40_000_000, 8_000_000), 16, *held(pre)
+    )
+    r1, r2, r3, dg = lax.optimization_barrier((r1, r2, r3, dg))
     c0, c1, c2, c3 = (permute(f, core) for f in (f0, r1, r2, r3))
+    lat_recv, c0 = lax.optimization_barrier((lat_recv, c0))
     s0, s1, s2, s3 = in_vmem(
         slopes_kernel, "slopes", [like((112, 256))] * 4, [pltpu.VMEM((4, 112, 256), F32)],
         cost(20_000_000, 3_000_000), 16,
@@ -375,36 +399,46 @@
     q3 = permute(s3, x_pairs(3))
     q1 = permute(s1, x_pairs(1))
     q2 = permute(s2, x_pairs(2))
-    lat_recv = permute(lat_send, core)
     parts = [s0, q1, q2, q3]
     pga, *first = upper("x", parts, output_weight, dg, nrm)
     first[1] = permute(first[1], core)
-    pgb, keep, send, go_keep, go_send = upper("z", parts, output_weight, dg, nrm, hid)
+    pga, parts[0] = lax.optimization_barrier((pga, s0))
+    pgb, keep, send = upper("z", parts, output_weight, dg, nrm)
     second = [keep, permute(send, core)]
+    sent = total_of(first, 1).astype(BF)
+    sent_z, s0 = lax.optimization_barrier((total_of(second, 1).astype(BF), s0))
+    go_keep, go_send = in_vmem(
+        out_kernel, "grad_out", [like((128, 1024)), like((128, 1024))],
+        [pltpu.VMEM((128, 1024), BF), pltpu.VMEM((128, 2048), F32)], cost(550_000_000, 1_000_000), 16,
+        s0, q1, q2, q3, *held(hid),
+    )
+    go_send, pgb = lax.optimization_barrier((go_send, pgb))
     go_recv = permute(go_send, core)
-    sent, pgb = lax.optimization_barrier((total_of(first, 1).astype(BF), pgb))
     first.append(permute(sent, ring_pairs("x")))
     nodes, width = lat.shape
-    top, rest = in_vmem(
-        lower_kernel, "lower", [like((192, width)), like((nodes - 192 + 16, width))], [pltpu.VMEM((nodes, width), F32)],
+    vg = in_vmem(
+        lower_kernel, "lower", like((nodes + 16, width)), [pltpu.VMEM(nrm.shape, BF)],
         cost(5_100_000_000, 8_000_000), 24,
         *held(pga, pgb), w_hidden, *held(nrm, inv), gain_row, *held(st),
     )
-    second.append(permute(total_of(second, 1).astype(BF), ring_pairs("z")))
+    second.append(permute(sent_z, ring_pairs("z")))
     halves = [total_of(part, 0).astype(BF) for part in (first, second)]
-    *halves, top, rest = lax.optimization_barrier((*halves, top, rest))
-    top_recv, rest_recv = permute(top, core), permute(rest, core)
+    *halves, vg, go_keep = lax.optimization_barrier((*halves, vg, go_keep))
+    own_lat, out = in_vmem(
+        prepare_kernel, "prepare", [like((nodes, width // 2)), like((width // 2, 256))], [], cost(1_000_000, 2_000_000), 16,
+        lat, go_keep, go_recv,
+    )
+    vg_recv = permute(vg, core)
     grad_latents = in_vmem(
-        latents_kernel, "grad_latents", like(lat.shape), [], cost(800_000_000, 4_000_000), 16, top, rest, w_value
+        latents_kernel, "grad_latents", like(lat.shape), [], cost(800_000_000, 4_000_000), 16, vg, w_value
     )
     mine = in_vmem(
         value_kernel, "grad_value", pltpu.HBM((width // 2, 1024 + width + 256), BF),
         [
-            pltpu.VMEM((nodes, width // 2), BF), pltpu.VMEM((width, 128), F32),
-            pltpu.VMEM((width // 2, width + 256), BF), pltpu.SemaphoreType.DMA((3,)),
+            pltpu.VMEM((width, 128), F32), pltpu.VMEM((width // 2, width + 256), BF), pltpu.SemaphoreType.DMA((4,)),
         ],
         cost(800_000_000, 6_000_000), 16,
-        lat, lat_recv, top, rest, top_recv, rest_recv, go_keep, go_recv, *halves, in_hbm=True,
+        own_lat, lat_recv, vg, vg_recv, out, *halves, in_hbm=True,
     )
     sent = mine.reshape(64, 8, mine.shape[1])
     met = lax.all_to_all(sent, CORE_AXES, 0, 0, tiled=True)

time: 107 us -> 105 us (0.981)
  waiting for transfers between devices: 40.6 us -> 36.4 us
  Pallas kernels: 36 us -> 37.6 us
    ppermute x18 -> x17, waiting for transfers between devices: 12 us -> 7.15 us  [permute(): return lax.ppermute(value, AXES, pairs)]
    pallas_call x7 -> x10, Pallas kernels: 21.8 us -> 25.4 us  [in_vmem(): pl.pallas_call(kernel, in_specs=[pl.BlockSpec(memory_space=pltpu.SMEM)] *...]
    pallas_call x1, Pallas kernels: 14.2 us -> 12.2 us  [forward(): pl.pallas_call(forward_kernel, in_specs=[raw] * 8, out_specs=[vm] * 10, o...]
    ppermute x18 -> x17, starting transfers between devices: 17 us -> 18.1 us  [permute(): return lax.ppermute(value, AXES, pairs)]
    all_to_all x1, starting transfers between devices: 9.52 us -> 8.43 us  [per_device(): met = lax.all_to_all(sent, CORE_AXES, 0, 0, tiled=True)]
  transfers between devices with their start and end apart: 19 -> 18, of which waited for: 11 -> 9; matrix products, arithmetic and copies ran while one was open for 1% -> 1% of each run, Pallas kernels for 12% -> 17%
where the time goes in v4:
time: 105 us; the launch traced here: 104 us
  Pallas kernels  37.6 us (36%)
  waiting for transfers between devices  36.4 us (35%)
  starting transfers between devices  26.5 us (25%)
  local copies, waits for them, and re-layouts  1.63 us (2%)
    all_to_all x1, waiting for transfers between devices, per_device(): met = lax.all_to_all(sent, CORE_AXES, 0, 0, tiled=True)  29.3 us
    pallas_call x10, Pallas kernels, in_vmem(): pl.pallas_call(kernel, in_specs=[pl.BlockSpec(memory_space=pltpu.SMEM)] *...  25.4 us
    ppermute x17, starting transfers between devices, permute(): return lax.ppermute(value, AXES, pairs)  18.1 us
    pallas_call x1, Pallas kernels, forward(): pl.pallas_call(forward_kernel, in_specs=[raw] * 8, out_specs=[vm] * 10, o...  12.2 us
    all_to_all x1, starting transfers between devices, per_device(): met = lax.all_to_all(sent, CORE_AXES, 0, 0, tiled=True)  8.43 us
    ppermute x17, waiting for transfers between devices, permute(): return lax.ppermute(value, AXES, pairs)  7.15 us
  transfers between devices with their start and end apart: 18, of which 9 were waited for; matrix products, arithmetic and copies ran while one was open for 1% of the time, Pallas kernels for 17%

profile of v4, /device:TPU:0, one launch (start us, length us, event | category | flops | bytes accessed | tf_op | source)
XLA Modules:
  0.0 104.0 jit_solution(10617961941472329962)
XLA Ops:
  0.6 12.2 %forward.1 = (f32[104,256]{1,0:T(8,128)S(1)}, f32[104,256]{1,0:T(8,128)S(1)}, f32[104,256]{1,0:T(8,128)S(1)}, f32[104,256]{1,0:T(8,128)S(1)}, bf16[1024,2048]{1,...) custom-call(bf16[384,1024]{1,0:T(8,128)(2,1)} %bitcast.8, ...), custom_call_target="tpu_custom_call" | custom-call | flops 6400000000 | bytes 12000000 | tf_op jit(solution)/shard_map/forward/pallas_call | solution.py:319
  12.8 0.1 collective-permute-start.3
  12.9 2.9 %collective-permute-start = (f32[104,256]{1,0:T(8,128)S(1)}, f32[104,256]{1,0:T(8,128)S(1)}, u32[]{:S(2)}, u32[]{:S(2)}) collective-permute-start(f32[104,256]{1,0:T(8,128)S(1)} %get-tuple-element.50), channel_id=1, source_target_pairs={{0,96},{1,97},{2,98},{3,99},{4,100},{5,101},{6,102},{7,103},{8,104... | collective-permute-start | bytes 319496 | tf_op jit(solution)/shard_map/ppermute | solution.py:367
  15.9 0.2 collective-permute-start.1
  16.1 1.6 %collective-permute-start.2 = (f32[104,256]{1,0:T(8,128)S(1)}, f32[104,256]{1,0:T(8,128)S(1)}, u32[]{:S(2)}, u32[]{:S(2)}) collective-permute-start(f32[104,256]{1,0:T(8,128)S(1)} %get-tuple-element.52), channel_id=1, source_target_pairs={{0,64},{1,65},{2,66},{3,67},{4,68},{5,69},{6,70},{7,71},{8,72},{9,... | collective-permute-start | bytes 319496 | tf_op jit(solution)/shard_map/ppermute | solution.py:367
  17.7 0.0 collective-permute-start.4
  17.7 0.0 copy-start.5
  17.7 0.0 copy-start.7
  17.7 5.0 %gelu_slope.1.refs_5_ = bf16[1024,2048]{1,0:T(8,128)(2,1)S(1)} custom-call(bf16[1024,2048]{1,0:T(8,128)(2,1)S(1)} %get-tuple-element.53.pre_ref), custom_call_target="tpu_custom_call" | custom-call | flops 40000000 | bytes 8000000 | tf_op jit(solution)/shard_map/gelu_slope/pallas_call | solution.py:343
  22.8 0.0 collective-permute-done.f1
  22.8 0.0 collective-permute-done.1.f2
  22.8 0.1 collective-permute-done.2.f3
  22.9 0.5 collective-permute-start.5
  23.4 0.1 collective-permute-start.6
  23.5 0.4 collective-permute-start.7
  23.9 0.0 collective-permute-done.4.c0
  23.9 0.0 collective-permute-done.3.lat_recv
  23.9 0.4 collective-permute-done.5.c1
  24.4 0.4 collective-permute-done.6.c2
  24.7 0.2 collective-permute-done.7.c3
  24.9 0.0 copy-done.2
  24.9 0.0 copy-done.3
  24.9 0.0 copy-done.4
  24.9 0.0 copy-done.5
  24.9 1.2 %slopes.1 = (bf16[112,256]{1,0:T(8,128)(2,1)S(1)}, bf16[112,256]{1,0:T(8,128)(2,1)S(1)}, bf16[112,256]{1,0:T(8,128)(2,1)S(1)}, bf16[112,256]{1,0:T(8,128)(2,1)S(1)}) custom-call(s32[16]{0:T(128)S(1)} %copy-done.4, f32[104,256]{1,0:T(8,128)S(1)} %get-tuple-element.49.f0, f32[104,256]{1,0:T(8,128)S(1)} %collective-permute-done.f1, ...), custom_call_target="tpu_custom_call" | custom-call | flops 20000000 | bytes 3000000 | tf_op jit(solution)/shard_map/slopes/pallas_call | solution.py:343
  26.1 2.9 %collective-permute-start.8 = (bf16[112,256]{1,0:T(8,128)(2,1)S(1)}, bf16[112,256]{1,0:T(8,128)(2,1)S(1)}, u32[]{:S(2)}, u32[]{:S(2)}) collective-permute-start(bf16[112,256]{1,0:T(8,128)(2,1)S(1)} %get-tuple-element.60), channel_id=1, source_target_pairs={{0,96},{1,97},{2,98},{3,99},{4,100},{5,101},{6,102},{7,103},{8,104... | collective-permute-start | bytes 172040 | tf_op jit(solution)/shard_map/ppermute | solution.py:367
  29.0 0.0 collective-permute-start.9
  29.0 1.8 %collective-permute-start.10 = (bf16[112,256]{1,0:T(8,128)(2,1)S(1)}, bf16[112,256]{1,0:T(8,128)(2,1)S(1)}, u32[]{:S(2)}, u32[]{:S(2)}) collective-permute-start(bf16[112,256]{1,0:T(8,128)(2,1)S(1)} %get-tuple-element.62), channel_id=1, source_target_pairs={{0,64},{1,65},{2,66},{3,67},{4,68},{5,69},{6,70},{7,71},{8,72},{9,... | collective-permute-start | bytes 172040 | tf_op jit(solution)/shard_map/ppermute | solution.py:367
  30.8 1.3 %collective-permute-done.8.refs_1_.s1 = bf16[112,256]{1,0:T(8,128)(2,1)S(1)} collective-permute-done((bf16[112,256]{1,0:T(8,128)(2,1)S(1)}, bf16[112,256]{1,0:T(8,128)(2,1)S(1)}, u32[]{:S(2)}, u32[]{:S(2)}) %collective-permute-start.8) | collective-permute-done | bytes 57376 | tf_op jit(solution)/shard_map/ppermute | solution.py:367
  32.1 1.1 %collective-permute-done.9.refs_2_.s2 = bf16[112,256]{1,0:T(8,128)(2,1)S(1)} collective-permute-done((bf16[112,256]{1,0:T(8,128)(2,1)S(1)}, bf16[112,256]{1,0:T(8,128)(2,1)S(1)}, u32[]{:S(2)}, u32[]{:S(2)}) %collective-permute-start.9) | collective-permute-done | bytes 57376 | tf_op jit(solution)/shard_map/ppermute | solution.py:367
  33.2 1.5 %collective-permute-done.10.refs_3_.s3 = bf16[112,256]{1,0:T(8,128)(2,1)S(1)} collective-permute-done((bf16[112,256]{1,0:T(8,128)(2,1)S(1)}, bf16[112,256]{1,0:T(8,128)(2,1)S(1)}, u32[]{:S(2)}, u32[]{:S(2)}) %collective-permute-start.10) | collective-permute-done | bytes 57376 | tf_op jit(solution)/shard_map/ppermute | solution.py:367
  34.7 0.0 copy-done.7
  34.7 3.4 %upper_x.1 = (bf16[1024,1024]{1,0:T(8,128)(2,1)S(1)}, bf16[512,1024]{1,0:T(8,128)(2,1)S(1)}, bf16[512,1024]{1,0:T(8,128)(2,1)S(1)}) custom-call(bf16[112,256]{1,0:T(8,128)(2,1)S(1)} %get-tuple-element.73.refs_0_.s0, bf16[112,256]{1,0:T(8,128)(2,1)S(1)} %collective-permute-done.8.refs_1_.s1, bf16[112,256]{1,0:T(8,128)(2,1)S(1)} %collective-permute-done.9.refs_2_.s2, ...), custom_call_target="tpu_custom_call" | custom-call | flops 2700000000 | bytes 2000000 | tf_op jit(solution)/shard_map/upper_x/pallas_call | solution.py:343
  38.0 0.1 collective-permute-start.11
  38.1 3.4 %upper_z.1 = (bf16[1024,1024]{1,0:T(8,128)(2,1)S(1)}, bf16[512,1024]{1,0:T(8,128)(2,1)S(1)}, bf16[512,1024]{1,0:T(8,128)(2,1)S(1)}) custom-call(bf16[112,256]{1,0:T(8,128)(2,1)S(1)} %get-tuple-element.73.refs_0_.s0, bf16[112,256]{1,0:T(8,128)(2,1)S(1)} %collective-permute-done.8.refs_1_.s1, bf16[112,256]{1,0:T(8,128)(2,1)S(1)} %collective-permute-done.9.refs_2_.s2, ...), custom_call_target="tpu_custom_call" | custom-call | flops 2700000000 | bytes 2000000 | tf_op jit(solution)/shard_map/upper_z/pallas_call | solution.py:343
  41.5 0.7 collective-permute-start.13
  42.2 0.0 collective-permute-done.11
  42.2 0.2 add_convert_fusion.3
  42.4 2.1 %collective-permute-start.12 = (bf16[512,512]{1,0:T(8,128)(2,1)S(1)}, bf16[512,512]{1,0:T(8,128)(2,1)S(1)}, u32[]{:S(2)}, u32[]{:S(2)}) collective-permute-start(bf16[512,512]{1,0:T(8,128)(2,1)S(1)} %add_convert_fusion.3), channel_id=1, source_target_pairs={{0,32},{1,33},{2,34},{3,35},{4,36},{5,37},{6,38},{7,39},{8,40},{9,... | collective-permute-start | bytes 1572872 | tf_op jit(solution)/shard_map/ppermute | solution.py:367
  44.5 0.0 collective-permute-done.13
  44.5 0.2 add_convert_fusion.1
  44.7 0.0 copy-start.6
  44.7 0.0 copy-start.8
  44.7 2.2 %collective-permute-start.14 = (bf16[512,512]{1,0:T(8,128)(2,1)S(1)}, bf16[512,512]{1,0:T(8,128)(2,1)S(1)}, u32[]{:S(2)}, u32[]{:S(2)}) collective-permute-start(bf16[512,512]{1,0:T(8,128)(2,1)S(1)} %add_convert_fusion.1), channel_id=1, source_target_pairs={{0,4},{1,5},{2,6},{3,7},{4,0},{5,1},{6,2},{7,3},{8,12},{9,13},{10,... | collective-permute-start | bytes 1572872 | tf_op jit(solution)/shard_map/ppermute | solution.py:367
  46.9 0.9 grad_out.1
  47.9 6.2 %lower.1.vg_ref = bf16[400,1024]{1,0:T(8,128)(2,1)S(1)} custom-call(bf16[1024,1024]{1,0:T(8,128)(2,1)S(1)} %get-tuple-element.72.pga_ref, bf16[1024,1024]{1,0:T(8,128)(2,1)S(1)} %get-tuple-element.77.pgb_ref, bf16[1024,2048]{1,0:T(8,128)(2,1)S(1)} %copy-done.6, bf16[1024,1024]{1,0:T(8,128)(2,1)S(1)} %get-tuple-element.64.refs_6_.nrm_ref, ...), custom_call_target="tpu_custom_call" | custom-call | flops 5100000256 | bytes 8000000 | tf_op jit(solution)/shard_map/lower/pallas_call | solution.py:343
  54.0 0.0 copy-start.1
  54.1 0.0 collective-permute-done.12
  54.1 0.3 add_convert_fusion.2.first_ref
  54.4 0.0 collective-permute-done.14
  54.4 0.3 add_convert_fusion.second_ref
  54.7 2.3 %collective-permute-start.16 = (bf16[400,1024]{1,0:T(8,128)(2,1)S(1)}, bf16[400,1024]{1,0:T(8,128)(2,1)S(1)}, u32[]{:S(2)}, u32[]{:S(2)}) collective-permute-start(bf16[400,1024]{1,0:T(8,128)(2,1)S(1)} %lower.1.vg_ref), channel_id=1, source_target_pairs={{0,16},{1,17},{2,18},{3,19},{4,20},{5,21},{6,22},{7,23},{8,24},{9,... | collective-permute-start | bytes 2457608 | tf_op jit(solution)/shard_map/ppermute | solution.py:367
  57.0 0.1 collective-permute-start.15
  57.1 2.2 %collective-permute-done.15.go_recv = bf16[128,1024]{1,0:T(8,128)(2,1)S(1)} collective-permute-done((bf16[128,1024]{1,0:T(8,128)(2,1)S(1)}, bf16[128,1024]{1,0:T(8,128)(2,1)S(1)}, u32[]{:S(2)}, u32[]{:S(2)}) %collective-permute-start.15) | collective-permute-done | bytes 262176 | tf_op jit(solution)/shard_map/ppermute | solution.py:367
  59.3 0.0 copy-done.1
  59.3 0.2 prepare.1
  59.5 0.0 collective-permute-done.16.vg_recv
  59.5 2.4 %grad_value.1 = bf16[512,2304]{1,0:T(8,128)(2,1)} custom-call(bf16[384,512]{1,0:T(8,128)(2,1)S(1)} %get-tuple-element.83.own_lat, bf16[384,512]{1,0:T(8,128)(2,1)S(1)} %collective-permute-done.3.lat_recv, bf16[400,1024]{1,0:T(8,128)(2,1)S(1)} %lower.1.vg_ref, bf16[400,1024]{1,0:T(8,128)(2,1)S(1)} %collective-permute-done.16.vg_recv, ...), custom_call_target="tpu_custom_call" | custom-call | flops 800000000 | bytes 6000000 | tf_op jit(solution)/shard_map/grad_value/pallas_call | solution.py:343
  61.9 8.4 %all-to-all-start = ((bf16[64,8,2304]{2,1,0:T(8,128)(2,1)}), bf16[64,8,2304]{2,1,0:T(8,128)(2,1)S(1)}, u32[]{:S(2)}, u32[]{:S(2)}) async-start(bf16[64,8,2304]{2,1,0:T(8,128)(2,1)} %bitcast.14), calls=%async_computation | async-start | bytes 4718592 | tf_op jit(solution)/shard_map/all_to_all | solution.py:444
  70.3 0.0 copy-start
  70.3 1.6 %copy-done = bf16[1024,1024]{1,0:T(8,128)(2,1)S(1)} copy-done((bf16[1024,1024]{1,0:T(8,128)(2,1)S(1)}, bf16[1024,1024]{1,0:T(8,128)(2,1)}, u32[]{:S(2)}) %copy-start) | copy-done | bytes 2097176
  71.9 1.9 %grad_latents.1 = bf16[384,1024]{1,0:T(8,128)(2,1)} custom-call(bf16[400,1024]{1,0:T(8,128)(2,1)S(1)} %lower.1.vg_ref, bf16[1024,1024]{1,0:T(8,128)(2,1)S(1)} %copy-done), custom_call_target="tpu_custom_call" | custom-call | flops 800000000 | bytes 4000000 | tf_op jit(solution)/shard_map/grad_latents/pallas_call | solution.py:343
  73.8 29.3 %all-to-all-done.met_ref = bf16[64,8,2304]{2,1,0:T(8,128)(2,1)S(1)} async-done(((bf16[64,8,2304]{2,1,0:T(8,128)(2,1)}), bf16[64,8,2304]{2,1,0:T(8,128)(2,1)S(1)}, u32[]{:S(2)}, u32[]{:S(2)}) %all-to-all-start) | async-done | bytes 2359328 | tf_op jit(solution)/shard_map/all_to_all | solution.py:444
  103.1 1.0 final.1
  (5 shorter events, 0.0 us)
Async XLA Ops:
  12.8 11.1 %collective-permute-start.3 = (bf16[384,512]{1,0:T(8,128)(2,1)S(1)}, bf16[384,512]{1,0:T(8,128)(2,1)S(1)}, u32[]{:S(2)}, u32[]{:S(2)}) collective-permute-start(bf16[384,512]{1,0:T(8,128)(2,1)S(1)} %get-tuple-element.57), channel_id=1, source_target_pairs={{0,16},{1,17},{2,18},{3,19},{4,20},{5,21},{6,22},{7,23},{8,24},{9,... | collective-permute-start | bytes 1179656 | tf_op jit(solution)/shard_map/ppermute | solution.py:367
  12.9 9.9 %collective-permute-start = (f32[104,256]{1,0:T(8,128)S(1)}, f32[104,256]{1,0:T(8,128)S(1)}, u32[]{:S(2)}, u32[]{:S(2)}) collective-permute-start(f32[104,256]{1,0:T(8,128)S(1)} %get-tuple-element.50), channel_id=1, source_target_pairs={{0,96},{1,97},{2,98},{3,99},{4,100},{5,101},{6,102},{7,103},{8,104... | collective-permute-start | bytes 319496 | tf_op jit(solution)/shard_map/ppermute | solution.py:367
  15.9 6.9 %collective-permute-start.1 = (f32[104,256]{1,0:T(8,128)S(1)}, f32[104,256]{1,0:T(8,128)S(1)}, u32[]{:S(2)}, u32[]{:S(2)}) collective-permute-start(f32[104,256]{1,0:T(8,128)S(1)} %get-tuple-element.51), channel_id=1, source_target_pairs={{0,32},{1,33},{2,34},{3,35},{4,36},{5,37},{6,38},{7,39},{8,40},{9,... | collective-permute-start | bytes 319496 | tf_op jit(solution)/shard_map/ppermute | solution.py:367
  16.1 6.8 %collective-permute-start.2 = (f32[104,256]{1,0:T(8,128)S(1)}, f32[104,256]{1,0:T(8,128)S(1)}, u32[]{:S(2)}, u32[]{:S(2)}) collective-permute-start(f32[104,256]{1,0:T(8,128)S(1)} %get-tuple-element.52), channel_id=1, source_target_pairs={{0,64},{1,65},{2,66},{3,67},{4,68},{5,69},{6,70},{7,71},{8,72},{9,... | collective-permute-start | bytes 319496 | tf_op jit(solution)/shard_map/ppermute | solution.py:367
  17.7 6.2 %collective-permute-start.4 = (f32[104,256]{1,0:T(8,128)S(1)}, f32[104,256]{1,0:T(8,128)S(1)}, u32[]{:S(2)}, u32[]{:S(2)}) collective-permute-start(f32[104,256]{1,0:T(8,128)S(1)} %get-tuple-element.49.f0), channel_id=1, source_target_pairs={{0,16},{1,17},{2,18},{3,19},{4,20},{5,21},{6,22},{7,23},{8,24},{9,... | collective-permute-start | bytes 319496 | tf_op jit(solution)/shard_map/ppermute | solution.py:367
  17.7 7.2 %copy-start.2 = (f32[100,1024]{1,0:T(8,128)S(1)}, f32[100,1024]{1,0:T(8,128)}, u32[]{:S(2)}) copy-start(f32[100,1024]{1,0:T(8,128)} %tg_ref.1) | copy-start | bytes 1228804
  17.7 7.2 %copy-start.3 = (f32[1024]{0:T(1024)S(1)}, f32[1024]{0:T(1024)}, u32[]{:S(2)}) copy-start(f32[1024]{0:T(1024)} %param.22) | copy-start | bytes 12292
  17.7 7.2 %copy-start.4 = (s32[16]{0:T(128)S(1)}, s32[16]{0:T(128)}, u32[]{:S(2)}) copy-start(s32[16]{0:T(128)} %vc_ref.1) | copy-start | bytes 196
  17.7 7.2 %copy-start.5 = (f32[100]{0:T(128)S(1)}, f32[100]{0:T(128)}, u32[]{:S(2)}) copy-start(f32[100]{0:T(128)} %param.21) | copy-start | bytes 1204
  17.7 17.0 %copy-start.7 = (bf16[100,2048]{1,0:T(8,128)(2,1)S(1)}, bf16[100,2048]{1,0:T(8,128)(2,1)}, u32[]{:S(2)}) copy-start(bf16[100,2048]{1,0:T(8,128)(2,1)} %refs_4_.3) | copy-start | bytes 1228804
  22.9 1.4 %collective-permute-start.5 = (f32[104,256]{1,0:T(8,128)S(1)}, f32[104,256]{1,0:T(8,128)S(1)}, u32[]{:S(2)}, u32[]{:S(2)}) collective-permute-start(f32[104,256]{1,0:T(8,128)S(1)} %collective-permute-done.f1), channel_id=1, source_target_pairs={{0,16},{1,17},{2,18},{3,19},{4,20},{5,21},{6,22},{7,23},{8,24},{9,... | collective-permute-start | bytes 319496 | tf_op jit(solution)/shard_map/ppermute | solution.py:367
  23.4 1.3 %collective-permute-start.6 = (f32[104,256]{1,0:T(8,128)S(1)}, f32[104,256]{1,0:T(8,128)S(1)}, u32[]{:S(2)}, u32[]{:S(2)}) collective-permute-start(f32[104,256]{1,0:T(8,128)S(1)} %collective-permute-done.1.f2), channel_id=1, source_target_pairs={{0,16},{1,17},{2,18},{3,19},{4,20},{5,21},{6,22},{7,23},{8,24},{9,... | collective-permute-start | bytes 319496 | tf_op jit(solution)/shard_map/ppermute | solution.py:367
  23.5 1.4 %collective-permute-start.7 = (f32[104,256]{1,0:T(8,128)S(1)}, f32[104,256]{1,0:T(8,128)S(1)}, u32[]{:S(2)}, u32[]{:S(2)}) collective-permute-start(f32[104,256]{1,0:T(8,128)S(1)} %collective-permute-done.2.f3), channel_id=1, source_target_pairs={{0,16},{1,17},{2,18},{3,19},{4,20},{5,21},{6,22},{7,23},{8,24},{9,... | collective-permute-start | bytes 319496 | tf_op jit(solution)/shard_map/ppermute | solution.py:367
  26.1 6.0 %collective-permute-start.8 = (bf16[112,256]{1,0:T(8,128)(2,1)S(1)}, bf16[112,256]{1,0:T(8,128)(2,1)S(1)}, u32[]{:S(2)}, u32[]{:S(2)}) collective-permute-start(bf16[112,256]{1,0:T(8,128)(2,1)S(1)} %get-tuple-element.60), channel_id=1, source_target_pairs={{0,96},{1,97},{2,98},{3,99},{4,100},{5,101},{6,102},{7,103},{8,104... | collective-permute-start | bytes 172040 | tf_op jit(solution)/shard_map/ppermute | solution.py:367
  29.0 4.2 %collective-permute-start.9 = (bf16[112,256]{1,0:T(8,128)(2,1)S(1)}, bf16[112,256]{1,0:T(8,128)(2,1)S(1)}, u32[]{:S(2)}, u32[]{:S(2)}) collective-permute-start(bf16[112,256]{1,0:T(8,128)(2,1)S(1)} %get-tuple-element.61), channel_id=1, source_target_pairs={{0,32},{1,33},{2,34},{3,35},{4,36},{5,37},{6,38},{7,39},{8,40},{9,... | collective-permute-start | bytes 172040 | tf_op jit(solution)/shard_map/ppermute | solution.py:367
  29.0 5.7 %collective-permute-start.10 = (bf16[112,256]{1,0:T(8,128)(2,1)S(1)}, bf16[112,256]{1,0:T(8,128)(2,1)S(1)}, u32[]{:S(2)}, u32[]{:S(2)}) collective-permute-start(bf16[112,256]{1,0:T(8,128)(2,1)S(1)} %get-tuple-element.62), channel_id=1, source_target_pairs={{0,64},{1,65},{2,66},{3,67},{4,68},{5,69},{6,70},{7,71},{8,72},{9,... | collective-permute-start | bytes 172040 | tf_op jit(solution)/shard_map/ppermute | solution.py:367
  38.0 4.1 %collective-permute-start.11 = (bf16[512,1024]{1,0:T(8,128)(2,1)S(1)}, bf16[512,1024]{1,0:T(8,128)(2,1)S(1)}, u32[]{:S(2)}, u32[]{:S(2)}) collective-permute-start(bf16[512,1024]{1,0:T(8,128)(2,1)S(1)} %get-tuple-element.66), channel_id=1, source_target_pairs={{0,16},{1,17},{2,18},{3,19},{4,20},{5,21},{6,22},{7,23},{8,24},{9,... | collective-permute-start | bytes 3145736 | tf_op jit(solution)/shard_map/ppermute | solution.py:367
  41.5 3.0 %collective-permute-start.13 = (bf16[512,1024]{1,0:T(8,128)(2,1)S(1)}, bf16[512,1024]{1,0:T(8,128)(2,1)S(1)}, u32[]{:S(2)}, u32[]{:S(2)}) collective-permute-start(bf16[512,1024]{1,0:T(8,128)(2,1)S(1)} %get-tuple-element.70), channel_id=1, source_target_pairs={{0,16},{1,17},{2,18},{3,19},{4,20},{5,21},{6,22},{7,23},{8,24},{9,... | collective-permute-start | bytes 3145736 | tf_op jit(solution)/shard_map/ppermute | solution.py:367
  42.4 11.7 %collective-permute-start.12 = (bf16[512,512]{1,0:T(8,128)(2,1)S(1)}, bf16[512,512]{1,0:T(8,128)(2,1)S(1)}, u32[]{:S(2)}, u32[]{:S(2)}) collective-permute-start(bf16[512,512]{1,0:T(8,128)(2,1)S(1)} %add_convert_fusion.3), channel_id=1, source_target_pairs={{0,32},{1,33},{2,34},{3,35},{4,36},{5,37},{6,38},{7,39},{8,40},{9,... | collective-permute-start | bytes 1572872 | tf_op jit(solution)/shard_map/ppermute | solution.py:367
  44.7 3.2 %copy-start.6 = (bf16[1024,2048]{1,0:T(8,128)(2,1)S(1)}, bf16[1024,2048]{1,0:T(8,128)(2,1)}, u32[]{:S(2)}) copy-start(bf16[1024,2048]{1,0:T(8,128)(2,1)} %wh_ref.1) | copy-start | bytes 12582916
  44.7 3.2 %copy-start.8 = (f32[1024]{0:T(1024)S(1)}, f32[1024]{0:T(1024)}, u32[]{:S(2)}) copy-start(f32[1024]{0:T(1024)} %param.17) | copy-start | bytes 12292
  44.7 9.7 %collective-permute-start.14 = (bf16[512,512]{1,0:T(8,128)(2,1)S(1)}, bf16[512,512]{1,0:T(8,128)(2,1)S(1)}, u32[]{:S(2)}, u32[]{:S(2)}) collective-permute-start(bf16[512,512]{1,0:T(8,128)(2,1)S(1)} %add_convert_fusion.1), channel_id=1, source_target_pairs={{0,4},{1,5},{2,6},{3,7},{4,0},{5,1},{6,2},{7,3},{8,12},{9,13},{10,... | collective-permute-start | bytes 1572872 | tf_op jit(solution)/shard_map/ppermute | solution.py:367
  54.0 5.2 %copy-start.1 = (bf16[1,384,1024]{2,1,0:T(8,128)(2,1)S(1)}, bf16[1,384,1024]{2,1,0:T(8,128)(2,1)}, u32[]{:S(2)}) copy-start(bf16[1,384,1024]{2,1,0:T(8,128)(2,1)} %param.12) | copy-start | bytes 2359300
  54.7 4.8 %collective-permute-start.16 = (bf16[400,1024]{1,0:T(8,128)(2,1)S(1)}, bf16[400,1024]{1,0:T(8,128)(2,1)S(1)}, u32[]{:S(2)}, u32[]{:S(2)}) collective-permute-start(bf16[400,1024]{1,0:T(8,128)(2,1)S(1)} %lower.1.vg_ref), channel_id=1, source_target_pairs={{0,16},{1,17},{2,18},{3,19},{4,20},{5,21},{6,22},{7,23},{8,24},{9,... | collective-permute-start | bytes 2457608 | tf_op jit(solution)/shard_map/ppermute | solution.py:367
  57.0 2.3 %collective-permute-start.15 = (bf16[128,1024]{1,0:T(8,128)(2,1)S(1)}, bf16[128,1024]{1,0:T(8,128)(2,1)S(1)}, u32[]{:S(2)}, u32[]{:S(2)}) collective-permute-start(bf16[128,1024]{1,0:T(8,128)(2,1)S(1)} %get-tuple-element.82), channel_id=1, source_target_pairs={{0,16},{1,17},{2,18},{3,19},{4,20},{5,21},{6,22},{7,23},{8,24},{9,... | collective-permute-start | bytes 786440 | tf_op jit(solution)/shard_map/ppermute | solution.py:367
  61.9 41.2 %all-to-all-start = ((bf16[64,8,2304]{2,1,0:T(8,128)(2,1)}), bf16[64,8,2304]{2,1,0:T(8,128)(2,1)S(1)}, u32[]{:S(2)}, u32[]{:S(2)}) async-start(bf16[64,8,2304]{2,1,0:T(8,128)(2,1)} %bitcast.14), calls=%async_computation | async-start | bytes 4718592 | tf_op jit(solution)/shard_map/all_to_all | solution.py:444
  70.3 1.6 %copy-start = (bf16[1024,1024]{1,0:T(8,128)(2,1)S(1)}, bf16[1024,1024]{1,0:T(8,128)(2,1)}, u32[]{:S(2)}) copy-start(bf16[1024,1024]{1,0:T(8,128)(2,1)} %wv_ref.1) | copy-start | bytes 6291460

commit v5 on v4

--- a/solution.py
+++ b/solution.py
@@ -63,11 +63,13 @@
     return 0.5 + 0.5 * jnp.tanh(pre * (GELU_C + (GELU_C * 0.044715) * (pre * pre)))
 
 
-def gelu_slope_kernel(pre_ref, dg_ref):
+def gelu_slope_kernel(half, pre_ref, dg_ref):
+    columns = slice(1024 * half, 1024 * half + 1024)
+
     def body(q, carry):
         for part in range(4):
             rows = pl.ds(pl.multiple_of(q * 64 + 16 * part, 16), 16)
-            pre = pre_ref[rows, :].astype(F32)
+            pre = pre_ref[rows, columns].astype(F32)
             square = pre * pre
             t = jnp.tanh(pre * (GELU_C + (GELU_C * 0.044715) * square))
             inner = pre * (GELU_C + (3 * GELU_C * 0.044715) * square)
@@ -200,7 +202,7 @@
     for r in range(points // 256):
         rows = slice(256 * r, 256 * r + 256)
         grad = dot(slopes[:, rows], own_w[...], ((0,), (0,)))
-        pg_ref[rows, :] = (dg_ref[rows, offset : offset + 1024].astype(F32) * grad).astype(BF)
+        pg_ref[rows, :] = (dg_ref[rows, :].astype(F32) * grad).astype(BF)
     for tile, result in enumerate((result_0, result_1)):
         result[...] = dot(nrm_ref[...], pg_ref[:, 512 * tile : 512 * tile + 512], ((0,), (0,)))
         columns = pl.ds(pl.multiple_of((tile ^ (own[axis] & 1)) * 512, 512), 512)
@@ -352,6 +354,13 @@
     )(*args)
 
 
+def gelu_slope(half, pre):
+    return in_vmem(
+        lambda *refs: gelu_slope_kernel(half, *refs), f"gelu_slope_{half}", pltpu.VMEM((pre.shape[0], 1024), BF), [],
+        cost(20_000_000, 4_000_000), 16, *held(pre),
+    )
+
+
 def upper(axis, parts, ow, dg, nrm):
     points, width = nrm.shape
     half = like((width // 2, 1024))
@@ -385,10 +394,8 @@
     r1 = permute(f1, x_pairs(1))
     r2 = permute(f2, x_pairs(2))
     lat_recv = permute(lat_send, core)
-    dg = in_vmem(
-        gelu_slope_kernel, "gelu_slope", pltpu.VMEM(pre.shape, BF), [], cost(40_000_000, 8_000_000), 16, *held(pre)
-    )
-    r1, r2, r3, dg = lax.optimization_barrier((r1, r2, r3, dg))
+    dg_x = gelu_slope(0, pre)
+    r1, dg_x = lax.optimization_barrier((r1, dg_x))
     c0, c1, c2, c3 = (permute(f, core) for f in (f0, r1, r2, r3))
     lat_recv, c0 = lax.optimization_barrier((lat_recv, c0))
     s0, s1, s2, s3 = in_vmem(
@@ -399,21 +406,17 @@
     q3 = permute(s3, x_pairs(3))
     q1 = permute(s1, x_pairs(1))
     q2 = permute(s2, x_pairs(2))
+    pre, s0 = lax.optimization_barrier((pre, s0))
+    dg_z = gelu_slope(1, pre)
+    q1, q2, q3, dg_z = lax.optimization_barrier((q1, q2, q3, dg_z))
     parts = [s0, q1, q2, q3]
-    pga, *first = upper("x", parts, output_weight, dg, nrm)
+    pga, *first = upper("x", parts, output_weight, dg_x, nrm)
     first[1] = permute(first[1], core)
     pga, parts[0] = lax.optimization_barrier((pga, s0))
-    pgb, keep, send = upper("z", parts, output_weight, dg, nrm)
+    pgb, keep, send = upper("z", parts, output_weight, dg_z, nrm)
     second = [keep, permute(send, core)]
     sent = total_of(first, 1).astype(BF)
-    sent_z, s0 = lax.optimization_barrier((total_of(second, 1).astype(BF), s0))
-    go_keep, go_send = in_vmem(
-        out_kernel, "grad_out", [like((128, 1024)), like((128, 1024))],
-        [pltpu.VMEM((128, 1024), BF), pltpu.VMEM((128, 2048), F32)], cost(550_000_000, 1_000_000), 16,
-        s0, q1, q2, q3, *held(hid),
-    )
-    go_send, pgb = lax.optimization_barrier((go_send, pgb))
-    go_recv = permute(go_send, core)
+    sent_z, pgb = lax.optimization_barrier((total_of(second, 1).astype(BF), pgb))
     first.append(permute(sent, ring_pairs("x")))
     nodes, width = lat.shape
     vg = in_vmem(
@@ -423,12 +426,18 @@
     )
     second.append(permute(sent_z, ring_pairs("z")))
     halves = [total_of(part, 0).astype(BF) for part in (first, second)]
-    *halves, vg, go_keep = lax.optimization_barrier((*halves, vg, go_keep))
+    *halves, vg, s0 = lax.optimization_barrier((*halves, vg, s0))
+    vg_recv = permute(vg, core)
+    go_keep, go_send = in_vmem(
+        out_kernel, "grad_out", [like((128, 1024)), like((128, 1024))],
+        [pltpu.VMEM((128, 1024), BF), pltpu.VMEM((128, 2048), F32)], cost(550_000_000, 1_000_000), 16,
+        s0, q1, q2, q3, *held(hid),
+    )
+    go_recv = permute(go_send, core)
     own_lat, out = in_vmem(
         prepare_kernel, "prepare", [like((nodes, width // 2)), like((width // 2, 256))], [], cost(1_000_000, 2_000_000), 16,
         lat, go_keep, go_recv,
     )
-    vg_recv = permute(vg, core)
     grad_latents = in_vmem(
         latents_kernel, "grad_latents", like(lat.shape), [], cost(800_000_000, 4_000_000), 16, vg, w_value
     )

time: 105 us -> 104 us (level)
    all_to_all x1, starting transfers between devices: 8.43 us -> 9.59 us  [per_device(): met = lax.all_to_all(sent, CORE_AXES, 0, 0, tiled=True)]
    ppermute x17, starting transfers between devices: 18.1 us -> 17 us  [permute(): return lax.ppermute(value, AXES, pairs)]
    pallas_call x10 -> x11, Pallas kernels: 25.4 us -> 25 us  [in_vmem(): pl.pallas_call(kernel, in_specs=[pl.BlockSpec(memory_space=pltpu.SMEM)] *...]
  transfers between devices with their start and end apart: 18 -> 18, of which waited for: 9 -> 10; matrix products, arithmetic and copies ran while one was open for 1% -> 1% of each run, Pallas kernels for 17% -> 16%
where the time goes in v5:
time: 104 us
  Pallas kernels  37.3 us (36%)
  waiting for transfers between devices  36.4 us (35%)
  starting transfers between devices  26.6 us (26%)
  local copies, waits for them, and re-layouts  1.62 us (2%)
    all_to_all x1, waiting for transfers between devices, per_device(): met = lax.all_to_all(sent, CORE_AXES, 0, 0, tiled=True)  29.1 us
    pallas_call x11, Pallas kernels, in_vmem(): pl.pallas_call(kernel, in_specs=[pl.BlockSpec(memory_space=pltpu.SMEM)] *...  25 us
    ppermute x17, starting transfers between devices, permute(): return lax.ppermute(value, AXES, pairs)  17 us
    pallas_call x1, Pallas kernels, forward(): pl.pallas_call(forward_kernel, in_specs=[raw] * 8, out_specs=[vm] * 10, o...  12.3 us
    all_to_all x1, starting transfers between devices, per_device(): met = lax.all_to_all(sent, CORE_AXES, 0, 0, tiled=True)  9.59 us
    ppermute x17, waiting for transfers between devices, permute(): return lax.ppermute(value, AXES, pairs)  7.29 us
  transfers between devices with their start and end apart: 18, of which 10 were waited for; matrix products, arithmetic and copies ran while one was open for 1% of the time, Pallas kernels for 16%

profile of v5, /device:TPU:0, one launch (start us, length us, event | category | flops | bytes accessed | tf_op | source)
XLA Modules:
  0.0 103.8 jit_solution(3790066253698328217)
XLA Ops:
  0.6 12.3 %forward.1 = (f32[104,256]{1,0:T(8,128)S(1)}, f32[104,256]{1,0:T(8,128)S(1)}, f32[104,256]{1,0:T(8,128)S(1)}, f32[104,256]{1,0:T(8,128)S(1)}, bf16[1024,2048]{1,...) custom-call(bf16[384,1024]{1,0:T(8,128)(2,1)} %bitcast.8, ...), custom_call_target="tpu_custom_call" | custom-call | flops 6400000000 | bytes 12000000 | tf_op jit(solution)/shard_map/forward/pallas_call | solution.py:321
  13.0 0.1 collective-permute-start.3
  13.1 2.9 %collective-permute-start = (f32[104,256]{1,0:T(8,128)S(1)}, f32[104,256]{1,0:T(8,128)S(1)}, u32[]{:S(2)}, u32[]{:S(2)}) collective-permute-start(f32[104,256]{1,0:T(8,128)S(1)} %get-tuple-element.53), channel_id=1, source_target_pairs={{0,96},{1,97},{2,98},{3,99},{4,100},{5,101},{6,102},{7,103},{8,104... | collective-permute-start | bytes 319496 | tf_op jit(solution)/shard_map/ppermute | solution.py:376
  16.0 0.2 collective-permute-start.1
  16.2 1.6 %collective-permute-start.2 = (f32[104,256]{1,0:T(8,128)S(1)}, f32[104,256]{1,0:T(8,128)S(1)}, u32[]{:S(2)}, u32[]{:S(2)}) collective-permute-start(f32[104,256]{1,0:T(8,128)S(1)} %get-tuple-element.56), channel_id=1, source_target_pairs={{0,64},{1,65},{2,66},{3,67},{4,68},{5,69},{6,70},{7,71},{8,72},{9,... | collective-permute-start | bytes 319496 | tf_op jit(solution)/shard_map/ppermute | solution.py:376
  17.9 0.0 collective-permute-start.4
  17.9 0.0 copy-start.5
  17.9 2.3 %gelu_slope_0.1.refs_5_ = bf16[1024,1024]{1,0:T(8,128)(2,1)S(1)} custom-call(bf16[1024,2048]{1,0:T(8,128)(2,1)S(1)} %get-tuple-element.64.refs_0_), custom_call_target="tpu_custom_call" | custom-call | flops 20000000 | bytes 4000000 | tf_op jit(solution)/shard_map/gelu_slope_0/pallas_call | solution.py:345
  20.2 0.4 collective-permute-done.f1
  20.5 1.0 collective-permute-done.1.f2
  21.5 0.0 collective-permute-start.6
  21.5 1.5 %collective-permute-done.2.f3 = f32[104,256]{1,0:T(8,128)S(1)} collective-permute-done((f32[104,256]{1,0:T(8,128)S(1)}, f32[104,256]{1,0:T(8,128)S(1)}, u32[]{:S(2)}, u32[]{:S(2)}) %collective-permute-start.2) | collective-permute-done | bytes 106528 | tf_op jit(solution)/shard_map/ppermute | solution.py:376
  23.1 0.0 collective-permute-start.7
  23.1 0.5 collective-permute-start.5
  23.6 0.0 collective-permute-done.4.c0
  23.6 0.0 collective-permute-done.3.lat_recv
  23.6 0.0 collective-permute-done.6.c2
  23.6 0.8 collective-permute-done.7.c3
  24.4 0.2 collective-permute-done.5.c1
  24.5 0.0 copy-done.2
  24.5 0.0 copy-done.3
  24.5 0.0 copy-done.4
  24.5 0.0 copy-done.5
  24.6 1.2 %slopes.1 = (bf16[112,256]{1,0:T(8,128)(2,1)S(1)}, bf16[112,256]{1,0:T(8,128)(2,1)S(1)}, bf16[112,256]{1,0:T(8,128)(2,1)S(1)}, bf16[112,256]{1,0:T(8,128)(2,1)S(1)}) custom-call(s32[16]{0:T(128)S(1)} %copy-done.4, f32[104,256]{1,0:T(8,128)S(1)} %get-tuple-element.52.f0, f32[104,256]{1,0:T(8,128)S(1)} %collective-permute-done.f1, ...), custom_call_target="tpu_custom_call" | custom-call | flops 20000000 | bytes 3000000 | tf_op jit(solution)/shard_map/slopes/pallas_call | solution.py:345
  25.7 2.5 %collective-permute-start.8 = (bf16[112,256]{1,0:T(8,128)(2,1)S(1)}, bf16[112,256]{1,0:T(8,128)(2,1)S(1)}, u32[]{:S(2)}, u32[]{:S(2)}) collective-permute-start(bf16[112,256]{1,0:T(8,128)(2,1)S(1)} %get-tuple-element.61), channel_id=1, source_target_pairs={{0,96},{1,97},{2,98},{3,99},{4,100},{5,101},{6,102},{7,103},{8,104... | collective-permute-start | bytes 172040 | tf_op jit(solution)/shard_map/ppermute | solution.py:376
  28.3 0.0 collective-permute-start.9
  28.3 2.4 %collective-permute-start.10 = (bf16[112,256]{1,0:T(8,128)(2,1)S(1)}, bf16[112,256]{1,0:T(8,128)(2,1)S(1)}, u32[]{:S(2)}, u32[]{:S(2)}) collective-permute-start(bf16[112,256]{1,0:T(8,128)(2,1)S(1)} %get-tuple-element.63), channel_id=1, source_target_pairs={{0,64},{1,65},{2,66},{3,67},{4,68},{5,69},{6,70},{7,71},{8,72},{9,... | collective-permute-start | bytes 172040 | tf_op jit(solution)/shard_map/ppermute | solution.py:376
  30.7 2.3 %gelu_slope_1.1.refs_5_ = bf16[1024,1024]{1,0:T(8,128)(2,1)S(1)} custom-call(bf16[1024,2048]{1,0:T(8,128)(2,1)S(1)} %get-tuple-element.64.refs_0_), custom_call_target="tpu_custom_call" | custom-call | flops 20000000 | bytes 4000000 | tf_op jit(solution)/shard_map/gelu_slope_1/pallas_call | solution.py:345
  33.0 0.0 collective-permute-done.8.refs_1_.s1
  33.0 0.0 collective-permute-done.9.refs_2_.s2
  33.0 1.1 %collective-permute-done.10.refs_3_.s3 = bf16[112,256]{1,0:T(8,128)(2,1)S(1)} collective-permute-done((bf16[112,256]{1,0:T(8,128)(2,1)S(1)}, bf16[112,256]{1,0:T(8,128)(2,1)S(1)}, u32[]{:S(2)}, u32[]{:S(2)}) %collective-permute-start.10) | collective-permute-done | bytes 57376 | tf_op jit(solution)/shard_map/ppermute | solution.py:376
  34.1 0.0 copy-done.7
  34.1 3.4 %upper_x.1 = (bf16[1024,1024]{1,0:T(8,128)(2,1)S(1)}, bf16[512,1024]{1,0:T(8,128)(2,1)S(1)}, bf16[512,1024]{1,0:T(8,128)(2,1)S(1)}) custom-call(bf16[112,256]{1,0:T(8,128)(2,1)S(1)} %get-tuple-element.83.refs_0_.s0, bf16[112,256]{1,0:T(8,128)(2,1)S(1)} %collective-permute-done.8.refs_1_.s1, bf16[112,256]{1,0:T(8,128)(2,1)S(1)} %collective-permute-done.9.refs_2_.s2, ...), custom_call_target="tpu_custom_call" | custom-call | flops 2700000000 | bytes 2000000 | tf_op jit(solution)/shard_map/upper_x/pallas_call | solution.py:345
  37.5 0.1 collective-permute-start.11
  37.5 0.0 copy-start.6
  37.6 3.4 %upper_z.1 = (bf16[1024,1024]{1,0:T(8,128)(2,1)S(1)}, bf16[512,1024]{1,0:T(8,128)(2,1)S(1)}, bf16[512,1024]{1,0:T(8,128)(2,1)S(1)}) custom-call(bf16[112,256]{1,0:T(8,128)(2,1)S(1)} %get-tuple-element.83.refs_0_.s0, bf16[112,256]{1,0:T(8,128)(2,1)S(1)} %collective-permute-done.8.refs_1_.s1, bf16[112,256]{1,0:T(8,128)(2,1)S(1)} %collective-permute-done.9.refs_2_.s2, ...), custom_call_target="tpu_custom_call" | custom-call | flops 2700000000 | bytes 2000000 | tf_op jit(solution)/shard_map/upper_z/pallas_call | solution.py:345
  40.9 0.0 copy-start.8
  41.0 0.6 collective-permute-start.13
  41.6 0.0 collective-permute-done.11
  41.6 0.2 add_convert_fusion.3
  41.8 2.0 %collective-permute-start.12 = (bf16[512,512]{1,0:T(8,128)(2,1)S(1)}, bf16[512,512]{1,0:T(8,128)(2,1)S(1)}, u32[]{:S(2)}, u32[]{:S(2)}) collective-permute-start(bf16[512,512]{1,0:T(8,128)(2,1)S(1)} %add_convert_fusion.3), channel_id=1, source_target_pairs={{0,32},{1,33},{2,34},{3,35},{4,36},{5,37},{6,38},{7,39},{8,40},{9,... | collective-permute-start | bytes 1572872 | tf_op jit(solution)/shard_map/ppermute | solution.py:376
  43.8 0.1 collective-permute-done.13
  43.9 0.2 add_convert_fusion.1
  44.1 2.2 %collective-permute-start.14 = (bf16[512,512]{1,0:T(8,128)(2,1)S(1)}, bf16[512,512]{1,0:T(8,128)(2,1)S(1)}, u32[]{:S(2)}, u32[]{:S(2)}) collective-permute-start(bf16[512,512]{1,0:T(8,128)(2,1)S(1)} %add_convert_fusion.1), channel_id=1, source_target_pairs={{0,4},{1,5},{2,6},{3,7},{4,0},{5,1},{6,2},{7,3},{8,12},{9,13},{10,... | collective-permute-start | bytes 1572872 | tf_op jit(solution)/shard_map/ppermute | solution.py:376
  46.3 0.0 copy-done.6
  46.3 0.0 copy-done.8
  46.3 6.2 %lower.1.vg_ref = bf16[400,1024]{1,0:T(8,128)(2,1)S(1)} custom-call(bf16[1024,1024]{1,0:T(8,128)(2,1)S(1)} %get-tuple-element.79.pga_ref, bf16[1024,1024]{1,0:T(8,128)(2,1)S(1)} %get-tuple-element.80.pgb_ref, bf16[1024,2048]{1,0:T(8,128)(2,1)S(1)} %copy-done.6, bf16[1024,1024]{1,0:T(8,128)(2,1)S(1)} %get-tuple-element.69.refs_6_.nrm_ref, ...), custom_call_target="tpu_custom_call" | custom-call | flops 5100000256 | bytes 8000000 | tf_op jit(solution)/shard_map/lower/pallas_call | solution.py:345
  52.5 0.0 collective-permute-done.12
  52.5 0.3 add_convert_fusion.2.first_ref
  52.8 0.7 collective-permute-done.14
  53.6 0.3 add_convert_fusion.second_ref
  53.9 1.6 %collective-permute-start.16 = (bf16[400,1024]{1,0:T(8,128)(2,1)S(1)}, bf16[400,1024]{1,0:T(8,128)(2,1)S(1)}, u32[]{:S(2)}, u32[]{:S(2)}) collective-permute-start(bf16[400,1024]{1,0:T(8,128)(2,1)S(1)} %lower.1.vg_ref), channel_id=1, source_target_pairs={{0,16},{1,17},{2,18},{3,19},{4,20},{5,21},{6,22},{7,23},{8,24},{9,... | collective-permute-start | bytes 2457608 | tf_op jit(solution)/shard_map/ppermute | solution.py:376
  55.5 1.0 grad_out.1
  56.4 0.1 collective-permute-start.15
  56.5 1.5 %collective-permute-done.15.go_recv = bf16[128,1024]{1,0:T(8,128)(2,1)S(1)} collective-permute-done((bf16[128,1024]{1,0:T(8,128)(2,1)S(1)}, bf16[128,1024]{1,0:T(8,128)(2,1)S(1)}, u32[]{:S(2)}, u32[]{:S(2)}) %collective-permute-start.15) | collective-permute-done | bytes 262176 | tf_op jit(solution)/shard_map/ppermute | solution.py:376
  58.1 0.2 prepare.1
  58.2 0.0 collective-permute-done.16.vg_recv
  58.3 2.4 %grad_value.1 = bf16[512,2304]{1,0:T(8,128)(2,1)} custom-call(bf16[384,512]{1,0:T(8,128)(2,1)S(1)} %get-tuple-element.87.own_lat, bf16[384,512]{1,0:T(8,128)(2,1)S(1)} %collective-permute-done.3.lat_recv, bf16[400,1024]{1,0:T(8,128)(2,1)S(1)} %lower.1.vg_ref, bf16[400,1024]{1,0:T(8,128)(2,1)S(1)} %collective-permute-done.16.vg_recv, ...), custom_call_target="tpu_custom_call" | custom-call | flops 800000000 | bytes 6000000 | tf_op jit(solution)/shard_map/grad_value/pallas_call | solution.py:345
  60.6 9.6 %all-to-all-start = ((bf16[64,8,2304]{2,1,0:T(8,128)(2,1)}), bf16[64,8,2304]{2,1,0:T(8,128)(2,1)S(1)}, u32[]{:S(2)}, u32[]{:S(2)}) async-start(bf16[64,8,2304]{2,1,0:T(8,128)(2,1)} %bitcast.14), calls=%async_computation | async-start | bytes 4718592 | tf_op jit(solution)/shard_map/all_to_all | solution.py:453
  70.2 0.0 copy-start
  70.2 1.6 %copy-done = bf16[1024,1024]{1,0:T(8,128)(2,1)S(1)} copy-done((bf16[1024,1024]{1,0:T(8,128)(2,1)S(1)}, bf16[1024,1024]{1,0:T(8,128)(2,1)}, u32[]{:S(2)}) %copy-start) | copy-done | bytes 2097176
  71.8 1.9 %grad_latents.1 = bf16[384,1024]{1,0:T(8,128)(2,1)} custom-call(bf16[400,1024]{1,0:T(8,128)(2,1)S(1)} %lower.1.vg_ref, bf16[1024,1024]{1,0:T(8,128)(2,1)S(1)} %copy-done), custom_call_target="tpu_custom_call" | custom-call | flops 800000000 | bytes 4000000 | tf_op jit(solution)/shard_map/grad_latents/pallas_call | solution.py:345
  73.7 29.1 %all-to-all-done.met_ref = bf16[64,8,2304]{2,1,0:T(8,128)(2,1)S(1)} async-done(((bf16[64,8,2304]{2,1,0:T(8,128)(2,1)}), bf16[64,8,2304]{2,1,0:T(8,128)(2,1)S(1)}, u32[]{:S(2)}, u32[]{:S(2)}) %all-to-all-start) | async-done | bytes 2359328 | tf_op jit(solution)/shard_map/all_to_all | solution.py:453
  102.9 1.0 final.1
  (6 shorter events, 0.0 us)
Async XLA Ops:
  13.0 10.6 %collective-permute-start.3 = (bf16[384,512]{1,0:T(8,128)(2,1)S(1)}, bf16[384,512]{1,0:T(8,128)(2,1)S(1)}, u32[]{:S(2)}, u32[]{:S(2)}) collective-permute-start(bf16[384,512]{1,0:T(8,128)(2,1)S(1)} %get-tuple-element.57), channel_id=1, source_target_pairs={{0,16},{1,17},{2,18},{3,19},{4,20},{5,21},{6,22},{7,23},{8,24},{9,... | collective-permute-start | bytes 1179656 | tf_op jit(solution)/shard_map/ppermute | solution.py:376
  13.1 7.5 %collective-permute-start = (f32[104,256]{1,0:T(8,128)S(1)}, f32[104,256]{1,0:T(8,128)S(1)}, u32[]{:S(2)}, u32[]{:S(2)}) collective-permute-start(f32[104,256]{1,0:T(8,128)S(1)} %get-tuple-element.53), channel_id=1, source_target_pairs={{0,96},{1,97},{2,98},{3,99},{4,100},{5,101},{6,102},{7,103},{8,104... | collective-permute-start | bytes 319496 | tf_op jit(solution)/shard_map/ppermute | solution.py:376
  16.0 5.5 %collective-permute-start.1 = (f32[104,256]{1,0:T(8,128)S(1)}, f32[104,256]{1,0:T(8,128)S(1)}, u32[]{:S(2)}, u32[]{:S(2)}) collective-permute-start(f32[104,256]{1,0:T(8,128)S(1)} %get-tuple-element.55), channel_id=1, source_target_pairs={{0,32},{1,33},{2,34},{3,35},{4,36},{5,37},{6,38},{7,39},{8,40},{9,... | collective-permute-start | bytes 319496 | tf_op jit(solution)/shard_map/ppermute | solution.py:376
  16.2 6.8 %collective-permute-start.2 = (f32[104,256]{1,0:T(8,128)S(1)}, f32[104,256]{1,0:T(8,128)S(1)}, u32[]{:S(2)}, u32[]{:S(2)}) collective-permute-start(f32[104,256]{1,0:T(8,128)S(1)} %get-tuple-element.56), channel_id=1, source_target_pairs={{0,64},{1,65},{2,66},{3,67},{4,68},{5,69},{6,70},{7,71},{8,72},{9,... | collective-permute-start | bytes 319496 | tf_op jit(solution)/shard_map/ppermute | solution.py:376
  17.9 5.7 %collective-permute-start.4 = (f32[104,256]{1,0:T(8,128)S(1)}, f32[104,256]{1,0:T(8,128)S(1)}, u32[]{:S(2)}, u32[]{:S(2)}) collective-permute-start(f32[104,256]{1,0:T(8,128)S(1)} %get-tuple-element.52.f0), channel_id=1, source_target_pairs={{0,16},{1,17},{2,18},{3,19},{4,20},{5,21},{6,22},{7,23},{8,24},{9,... | collective-permute-start | bytes 319496 | tf_op jit(solution)/shard_map/ppermute | solution.py:376
  17.9 6.7 %copy-start.2 = (f32[100,1024]{1,0:T(8,128)S(1)}, f32[100,1024]{1,0:T(8,128)}, u32[]{:S(2)}) copy-start(f32[100,1024]{1,0:T(8,128)} %tg_ref.1) | copy-start | bytes 1228804
  17.9 6.7 %copy-start.3 = (f32[1024]{0:T(1024)S(1)}, f32[1024]{0:T(1024)}, u32[]{:S(2)}) copy-start(f32[1024]{0:T(1024)} %param.22) | copy-start | bytes 12292
  17.9 6.7 %copy-start.4 = (s32[16]{0:T(128)S(1)}, s32[16]{0:T(128)}, u32[]{:S(2)}) copy-start(s32[16]{0:T(128)} %vc_ref.1) | copy-start | bytes 196
  17.9 6.7 %copy-start.5 = (f32[100]{0:T(128)S(1)}, f32[100]{0:T(128)}, u32[]{:S(2)}) copy-start(f32[100]{0:T(128)} %param.21) | copy-start | bytes 1204
  21.5 2.1 %collective-permute-start.6 = (f32[104,256]{1,0:T(8,128)S(1)}, f32[104,256]{1,0:T(8,128)S(1)}, u32[]{:S(2)}, u32[]{:S(2)}) collective-permute-start(f32[104,256]{1,0:T(8,128)S(1)} %collective-permute-done.1.f2), channel_id=1, source_target_pairs={{0,16},{1,17},{2,18},{3,19},{4,20},{5,21},{6,22},{7,23},{8,24},{9,... | collective-permute-start | bytes 319496 | tf_op jit(solution)/shard_map/ppermute | solution.py:376
  23.1 1.3 %collective-permute-start.7 = (f32[104,256]{1,0:T(8,128)S(1)}, f32[104,256]{1,0:T(8,128)S(1)}, u32[]{:S(2)}, u32[]{:S(2)}) collective-permute-start(f32[104,256]{1,0:T(8,128)S(1)} %collective-permute-done.2.f3), channel_id=1, source_target_pairs={{0,16},{1,17},{2,18},{3,19},{4,20},{5,21},{6,22},{7,23},{8,24},{9,... | collective-permute-start | bytes 319496 | tf_op jit(solution)/shard_map/ppermute | solution.py:376
  23.1 1.5 %collective-permute-start.5 = (f32[104,256]{1,0:T(8,128)S(1)}, f32[104,256]{1,0:T(8,128)S(1)}, u32[]{:S(2)}, u32[]{:S(2)}) collective-permute-start(f32[104,256]{1,0:T(8,128)S(1)} %collective-permute-done.f1), channel_id=1, source_target_pairs={{0,16},{1,17},{2,18},{3,19},{4,20},{5,21},{6,22},{7,23},{8,24},{9,... | collective-permute-start | bytes 319496 | tf_op jit(solution)/shard_map/ppermute | solution.py:376
  25.7 7.2 %collective-permute-start.8 = (bf16[112,256]{1,0:T(8,128)(2,1)S(1)}, bf16[112,256]{1,0:T(8,128)(2,1)S(1)}, u32[]{:S(2)}, u32[]{:S(2)}) collective-permute-start(bf16[112,256]{1,0:T(8,128)(2,1)S(1)} %get-tuple-element.61), channel_id=1, source_target_pairs={{0,96},{1,97},{2,98},{3,99},{4,100},{5,101},{6,102},{7,103},{8,104... | collective-permute-start | bytes 172040 | tf_op jit(solution)/shard_map/ppermute | solution.py:376
  28.3 4.7 %collective-permute-start.9 = (bf16[112,256]{1,0:T(8,128)(2,1)S(1)}, bf16[112,256]{1,0:T(8,128)(2,1)S(1)}, u32[]{:S(2)}, u32[]{:S(2)}) collective-permute-start(bf16[112,256]{1,0:T(8,128)(2,1)S(1)} %get-tuple-element.62), channel_id=1, source_target_pairs={{0,32},{1,33},{2,34},{3,35},{4,36},{5,37},{6,38},{7,39},{8,40},{9,... | collective-permute-start | bytes 172040 | tf_op jit(solution)/shard_map/ppermute | solution.py:376
  28.3 5.8 %collective-permute-start.10 = (bf16[112,256]{1,0:T(8,128)(2,1)S(1)}, bf16[112,256]{1,0:T(8,128)(2,1)S(1)}, u32[]{:S(2)}, u32[]{:S(2)}) collective-permute-start(bf16[112,256]{1,0:T(8,128)(2,1)S(1)} %get-tuple-element.63), channel_id=1, source_target_pairs={{0,64},{1,65},{2,66},{3,67},{4,68},{5,69},{6,70},{7,71},{8,72},{9,... | collective-permute-start | bytes 172040 | tf_op jit(solution)/shard_map/ppermute | solution.py:376
  30.7 3.4 %copy-start.7 = (bf16[100,2048]{1,0:T(8,128)(2,1)S(1)}, bf16[100,2048]{1,0:T(8,128)(2,1)}, u32[]{:S(2)}) copy-start(bf16[100,2048]{1,0:T(8,128)(2,1)} %refs_4_.3) | copy-start | bytes 1228804
  37.5 4.1 %collective-permute-start.11 = (bf16[512,1024]{1,0:T(8,128)(2,1)S(1)}, bf16[512,1024]{1,0:T(8,128)(2,1)S(1)}, u32[]{:S(2)}, u32[]{:S(2)}) collective-permute-start(bf16[512,1024]{1,0:T(8,128)(2,1)S(1)} %get-tuple-element.71), channel_id=1, source_target_pairs={{0,16},{1,17},{2,18},{3,19},{4,20},{5,21},{6,22},{7,23},{8,24},{9,... | collective-permute-start | bytes 3145736 | tf_op jit(solution)/shard_map/ppermute | solution.py:376
  37.5 8.8 %copy-start.6 = (bf16[1024,2048]{1,0:T(8,128)(2,1)S(1)}, bf16[1024,2048]{1,0:T(8,128)(2,1)}, u32[]{:S(2)}) copy-start(bf16[1024,2048]{1,0:T(8,128)(2,1)} %wh_ref.1) | copy-start | bytes 12582916
  40.9 5.4 %copy-start.8 = (f32[1024]{0:T(1024)S(1)}, f32[1024]{0:T(1024)}, u32[]{:S(2)}) copy-start(f32[1024]{0:T(1024)} %param.17) | copy-start | bytes 12292
  41.0 2.9 %collective-permute-start.13 = (bf16[512,1024]{1,0:T(8,128)(2,1)S(1)}, bf16[512,1024]{1,0:T(8,128)(2,1)S(1)}, u32[]{:S(2)}, u32[]{:S(2)}) collective-permute-start(bf16[512,1024]{1,0:T(8,128)(2,1)S(1)} %get-tuple-element.76), channel_id=1, source_target_pairs={{0,16},{1,17},{2,18},{3,19},{4,20},{5,21},{6,22},{7,23},{8,24},{9,... | collective-permute-start | bytes 3145736 | tf_op jit(solution)/shard_map/ppermute | solution.py:376
  41.8 10.7 %collective-permute-start.12 = (bf16[512,512]{1,0:T(8,128)(2,1)S(1)}, bf16[512,512]{1,0:T(8,128)(2,1)S(1)}, u32[]{:S(2)}, u32[]{:S(2)}) collective-permute-start(bf16[512,512]{1,0:T(8,128)(2,1)S(1)} %add_convert_fusion.3), channel_id=1, source_target_pairs={{0,32},{1,33},{2,34},{3,35},{4,36},{5,37},{6,38},{7,39},{8,40},{9,... | collective-permute-start | bytes 1572872 | tf_op jit(solution)/shard_map/ppermute | solution.py:376
  44.1 9.5 %collective-permute-start.14 = (bf16[512,512]{1,0:T(8,128)(2,1)S(1)}, bf16[512,512]{1,0:T(8,128)(2,1)S(1)}, u32[]{:S(2)}, u32[]{:S(2)}) collective-permute-start(bf16[512,512]{1,0:T(8,128)(2,1)S(1)} %add_convert_fusion.1), channel_id=1, source_target_pairs={{0,4},{1,5},{2,6},{3,7},{4,0},{5,1},{6,2},{7,3},{8,12},{9,13},{10,... | collective-permute-start | bytes 1572872 | tf_op jit(solution)/shard_map/ppermute | solution.py:376
  53.9 4.4 %collective-permute-start.16 = (bf16[400,1024]{1,0:T(8,128)(2,1)S(1)}, bf16[400,1024]{1,0:T(8,128)(2,1)S(1)}, u32[]{:S(2)}, u32[]{:S(2)}) collective-permute-start(bf16[400,1024]{1,0:T(8,128)(2,1)S(1)} %lower.1.vg_ref), channel_id=1, source_target_pairs={{0,16},{1,17},{2,18},{3,19},{4,20},{5,21},{6,22},{7,23},{8,24},{9,... | collective-permute-start | bytes 2457608 | tf_op jit(solution)/shard_map/ppermute | solution.py:376
  55.5 2.6 %copy-start.1 = (bf16[1,384,1024]{2,1,0:T(8,128)(2,1)S(1)}, bf16[1,384,1024]{2,1,0:T(8,128)(2,1)}, u32[]{:S(2)}) copy-start(bf16[1,384,1024]{2,1,0:T(8,128)(2,1)} %param.12) | copy-start | bytes 2359300
  56.4 1.6 %collective-permute-start.15 = (bf16[128,1024]{1,0:T(8,128)(2,1)S(1)}, bf16[128,1024]{1,0:T(8,128)(2,1)S(1)}, u32[]{:S(2)}, u32[]{:S(2)}) collective-permute-start(bf16[128,1024]{1,0:T(8,128)(2,1)S(1)} %get-tuple-element.86), channel_id=1, source_target_pairs={{0,16},{1,17},{2,18},{3,19},{4,20},{5,21},{6,22},{7,23},{8,24},{9,... | collective-permute-start | bytes 786440 | tf_op jit(solution)/shard_map/ppermute | solution.py:376
  60.6 42.2 %all-to-all-start = ((bf16[64,8,2304]{2,1,0:T(8,128)(2,1)}), bf16[64,8,2304]{2,1,0:T(8,128)(2,1)S(1)}, u32[]{:S(2)}, u32[]{:S(2)}) async-start(bf16[64,8,2304]{2,1,0:T(8,128)(2,1)} %bitcast.14), calls=%async_computation | async-start | bytes 4718592 | tf_op jit(solution)/shard_map/all_to_all | solution.py:453
  70.2 1.6 %copy-start = (bf16[1024,1024]{1,0:T(8,128)(2,1)S(1)}, bf16[1024,1024]{1,0:T(8,128)(2,1)}, u32[]{:S(2)}) copy-start(bf16[1024,1024]{1,0:T(8,128)(2,1)} %wv_ref.1) | copy-start | bytes 6291460

commit v6 on v5

--- a/solution.py
+++ b/solution.py
@@ -80,9 +80,9 @@
 
 
 def forward_kernel(
-    lat_hbm, wv_hbm, nb_hbm, cf_hbm, emb_hbm, gain_hbm, wh_hbm, ow_hbm,
+    lat_hbm, wv_hbm, nb_hbm, cf_hbm, emb_hbm, gain_hbm, wh_hbm, ow,
     f0, f1, f2, f3, hid_ref, pre_ref, nrm, inv_ref, st_ref, lat_send,
-    total, lat, wv, emb, wh, ow, nb_ref, cf_ref, gain_ref, sems,
+    total, lat, wv, emb, wh, nb_ref, cf_ref, gain_ref, sems,
 ):
     nodes, points = st_ref.shape
     hidden = wh.shape[1]
@@ -91,12 +91,12 @@
     pairs = [(lat_hbm, lat), (wv_hbm, wv), (emb_hbm, emb)]
     for first in range(0, hidden, wide):
         pairs.append((wh_hbm.at[:, first : first + wide], wh.at[:, first : first + wide]))
-    pairs += [(ow_hbm, ow), (nb_hbm, nb_ref), (cf_hbm, cf_ref), (gain_hbm, gain_ref)]
-    small = len(pairs) - 4
+    small = len(pairs)
+    pairs += [(nb_hbm, nb_ref), (cf_hbm, cf_ref), (gain_hbm, gain_ref)]
     copies = [pltpu.make_async_copy(source, target, sems.at[k]) for k, (source, target) in enumerate(pairs)]
-    for k in (*range(small + 1, small + 4), *range(small + 1)):
+    for k in (*range(small, small + 3), *range(small)):
         copies[k].start()
-    for copy in copies[small + 1 :]:
+    for copy in copies[small:]:
         copy.wait()
     rows_of = lax.broadcasted_iota(jnp.int32, (nodes, 256), 0)
     for r in range(points // 256):
@@ -119,7 +119,6 @@
         inv = lax.rsqrt(jnp.mean(summed * summed, axis=-1, keepdims=True) + norm_eps)
         inv_ref[rows, :] = inv
         nrm[rows, :] = (summed * inv * gain_ref[...]).astype(BF)
-    copies[small].wait()
     for tile in range(hidden // wide):
         copies[3 + tile].wait()
         for r in range(points // 256):
@@ -286,7 +285,10 @@
     for x in range(4):
         for z in range(4):
             for y in range(4):
-                block = met_ref[x * 16 + z * 4 + y].astype(F32)
+                source = x * 16 + z * 4 + y
+                if source % 2 == 0:
+                    two = met_ref[8 * source : 8 * source + 16, :].astype(F32)
+                block = two[0:8] if source % 2 == 0 else two[8:16]
                 for sums, k, columns in ((first, x & 1, slice(0, 512)), (second, z & 1, slice(512, 1024))):
                     sums[k] = block[:, columns] if sums[k] is None else sums[k] + block[:, columns]
                 rest = block[:, 1024:] if rest is None else rest + block[:, 1024:]
@@ -317,10 +319,10 @@
     hidden = wh.shape[1]
     vm = pl.BlockSpec(memory_space=pltpu.VMEM)
     raw = pl.BlockSpec(memory_space=pl.ANY)
-    args = [pltpu.with_memory_space_constraint(array, pltpu.HBM) for array in (lat, wv, nb, cf, emb, gain, wh, ow)]
+    args = [pltpu.with_memory_space_constraint(array, pltpu.HBM) for array in (lat, wv, nb, cf, emb, gain, wh)]
     return pl.pallas_call(
         forward_kernel,
-        in_specs=[raw] * 8,
+        in_specs=[raw] * 7 + [vm],
         out_specs=[vm] * 10,
         out_shape=[like((104, 256), F32)] * 4
         + [
@@ -329,14 +331,14 @@
         ],
         scratch_shapes=[
             pltpu.VMEM((104, points), F32), pltpu.VMEM((nodes, width), BF), pltpu.VMEM((width, width), BF),
-            pltpu.VMEM((points, width), BF), pltpu.VMEM((width, hidden), BF), pltpu.VMEM(ow.shape, BF),
+            pltpu.VMEM((points, width), BF), pltpu.VMEM((width, hidden), BF),
             pltpu.VMEM(nb.shape, jnp.int32), pltpu.VMEM(cf.shape, F32), pltpu.VMEM(gain.shape, F32),
-            pltpu.SemaphoreType.DMA((7 + hidden // 512,)),
+            pltpu.SemaphoreType.DMA((6 + hidden // 512,)),
         ],
         compiler_params=pltpu.CompilerParams(vmem_limit_bytes=24 * MIB),
         cost_estimate=cost(6_400_000_000, 12_000_000),
         name="forward",
-    )(*args)
+    )(*args, ow)
 
 
 def in_vmem(kernel, name, out_shape, scratch, estimate, limit, *args, scalars=0, in_hbm=False):
@@ -453,7 +455,7 @@
     met = lax.all_to_all(sent, CORE_AXES, 0, 0, tiled=True)
     grad_value, grad_gain, grad_hidden, grad_out = in_vmem(
         final_kernel, "final", [like((8, width), F32), like((1, 8), F32), like((8, 2048), F32), like((16, 100), F32)],
-        [], cost(2_000_000, 2_600_000), 16, met,
+        [], cost(2_000_000, 2_600_000), 16, met.reshape(mine.shape),
     )
     return (grad_value, grad_gain.reshape(8), grad_hidden, grad_out.T, grad_latents[None])
 

time: 104 us -> 105 us (level)
    unnamed x18 -> x20, local copies, waits for them, and re-layouts: 1.62 us -> 2.63 us
where the time goes in v6:
time: 105 us
  Pallas kernels  37.3 us (36%)
  waiting for transfers between devices  36.5 us (35%)
  starting transfers between devices  26.6 us (25%)
  local copies, waits for them, and re-layouts  2.63 us (3%)
    all_to_all x1, waiting for transfers between devices, per_device(): met = lax.all_to_all(sent, CORE_AXES, 0, 0, tiled=True)  29.1 us
    pallas_call x11, Pallas kernels, in_vmem(): pl.pallas_call(kernel, in_specs=[pl.BlockSpec(memory_space=pltpu.SMEM)] *...  24.9 us
    ppermute x17, starting transfers between devices, permute(): return lax.ppermute(value, AXES, pairs)  17 us
    pallas_call x1, Pallas kernels, forward(): pl.pallas_call(forward_kernel, in_specs=[raw] * 7 + [vm], out_specs=[vm]...  12.3 us
    all_to_all x1, starting transfers between devices, per_device(): met = lax.all_to_all(sent, CORE_AXES, 0, 0, tiled=True)  9.62 us
    ppermute x17, waiting for transfers between devices, permute(): return lax.ppermute(value, AXES, pairs)  7.31 us
    unnamed x20, local copies, waits for them, and re-layouts  2.63 us
  transfers between devices with their start and end apart: 18, of which 10 were waited for; matrix products, arithmetic and copies ran while one was open for 1% of the time, Pallas kernels for 16%

profile of v6, /device:TPU:0, one launch (start us, length us, event | category | flops | bytes accessed | tf_op | source)
XLA Modules:
  0.0 104.8 jit_solution(18393349497496349143)
XLA Ops:
  0.6 0.0 copy-start.7
  0.6 1.0 copy-done.7
  1.6 12.3 %forward.1 = (f32[104,256]{1,0:T(8,128)S(1)}, f32[104,256]{1,0:T(8,128)S(1)}, f32[104,256]{1,0:T(8,128)S(1)}, f32[104,256]{1,0:T(8,128)S(1)}, bf16[1024,2048]{1,...) custom-call(bf16[384,1024]{1,0:T(8,128)(2,1)} %bitcast.10, ...), custom_call_target="tpu_custom_call" | custom-call | flops 6400000000 | bytes 12000000 | tf_op jit(solution)/shard_map/forward/pallas_call | solution.py:323
  14.0 0.1 collective-permute-start.3
  14.1 2.9 %collective-permute-start = (f32[104,256]{1,0:T(8,128)S(1)}, f32[104,256]{1,0:T(8,128)S(1)}, u32[]{:S(2)}, u32[]{:S(2)}) collective-permute-start(f32[104,256]{1,0:T(8,128)S(1)} %get-tuple-element.53), channel_id=1, source_target_pairs={{0,96},{1,97},{2,98},{3,99},{4,100},{5,101},{6,102},{7,103},{8,104... | collective-permute-start | bytes 319496 | tf_op jit(solution)/shard_map/ppermute | solution.py:378
  17.0 0.2 collective-permute-start.1
  17.2 1.6 %collective-permute-start.2 = (f32[104,256]{1,0:T(8,128)S(1)}, f32[104,256]{1,0:T(8,128)S(1)}, u32[]{:S(2)}, u32[]{:S(2)}) collective-permute-start(f32[104,256]{1,0:T(8,128)S(1)} %get-tuple-element.56), channel_id=1, source_target_pairs={{0,64},{1,65},{2,66},{3,67},{4,68},{5,69},{6,70},{7,71},{8,72},{9,... | collective-permute-start | bytes 319496 | tf_op jit(solution)/shard_map/ppermute | solution.py:378
  18.9 0.0 collective-permute-start.4
  18.9 0.0 copy-start.5
  18.9 2.3 %gelu_slope_0.1.refs_5_ = bf16[1024,1024]{1,0:T(8,128)(2,1)S(1)} custom-call(bf16[1024,2048]{1,0:T(8,128)(2,1)S(1)} %get-tuple-element.64.refs_0_), custom_call_target="tpu_custom_call" | custom-call | flops 20000000 | bytes 4000000 | tf_op jit(solution)/shard_map/gelu_slope_0/pallas_call | solution.py:347
  21.2 0.4 collective-permute-done.f1
  21.5 1.0 collective-permute-done.1.f2
  22.5 0.0 collective-permute-start.6
  22.5 1.5 %collective-permute-done.2.f3 = f32[104,256]{1,0:T(8,128)S(1)} collective-permute-done((f32[104,256]{1,0:T(8,128)S(1)}, f32[104,256]{1,0:T(8,128)S(1)}, u32[]{:S(2)}, u32[]{:S(2)}) %collective-permute-start.2) | collective-permute-done | bytes 106528 | tf_op jit(solution)/shard_map/ppermute | solution.py:378
  24.1 0.0 collective-permute-start.7
  24.1 0.5 collective-permute-start.5
  24.6 0.0 collective-permute-done.4.c0
  24.6 0.0 collective-permute-done.3.lat_recv
  24.6 0.0 collective-permute-done.6.c2
  24.6 0.8 collective-permute-done.7.c3
  25.4 0.2 collective-permute-done.5.c1
  25.5 0.0 copy-done.2
  25.5 0.0 copy-done.4
  25.5 0.0 copy-done.5
  25.6 1.2 %slopes.1 = (bf16[112,256]{1,0:T(8,128)(2,1)S(1)}, bf16[112,256]{1,0:T(8,128)(2,1)S(1)}, bf16[112,256]{1,0:T(8,128)(2,1)S(1)}, bf16[112,256]{1,0:T(8,128)(2,1)S(1)}) custom-call(s32[16]{0:T(128)S(1)} %copy-done.4, f32[104,256]{1,0:T(8,128)S(1)} %get-tuple-element.52.f0, f32[104,256]{1,0:T(8,128)S(1)} %collective-permute-done.f1, ...), custom_call_target="tpu_custom_call" | custom-call | flops 20000000 | bytes 3000000 | tf_op jit(solution)/shard_map/slopes/pallas_call | solution.py:347
  26.7 2.5 %collective-permute-start.8 = (bf16[112,256]{1,0:T(8,128)(2,1)S(1)}, bf16[112,256]{1,0:T(8,128)(2,1)S(1)}, u32[]{:S(2)}, u32[]{:S(2)}) collective-permute-start(bf16[112,256]{1,0:T(8,128)(2,1)S(1)} %get-tuple-element.61), channel_id=1, source_target_pairs={{0,96},{1,97},{2,98},{3,99},{4,100},{5,101},{6,102},{7,103},{8,104... | collective-permute-start | bytes 172040 | tf_op jit(solution)/shard_map/ppermute | solution.py:378
  29.3 0.0 collective-permute-start.9
  29.3 2.4 %collective-permute-start.10 = (bf16[112,256]{1,0:T(8,128)(2,1)S(1)}, bf16[112,256]{1,0:T(8,128)(2,1)S(1)}, u32[]{:S(2)}, u32[]{:S(2)}) collective-permute-start(bf16[112,256]{1,0:T(8,128)(2,1)S(1)} %get-tuple-element.63), channel_id=1, source_target_pairs={{0,64},{1,65},{2,66},{3,67},{4,68},{5,69},{6,70},{7,71},{8,72},{9,... | collective-permute-start | bytes 172040 | tf_op jit(solution)/shard_map/ppermute | solution.py:378
  31.7 2.3 %gelu_slope_1.1.refs_5_ = bf16[1024,1024]{1,0:T(8,128)(2,1)S(1)} custom-call(bf16[1024,2048]{1,0:T(8,128)(2,1)S(1)} %get-tuple-element.64.refs_0_), custom_call_target="tpu_custom_call" | custom-call | flops 20000000 | bytes 4000000 | tf_op jit(solution)/shard_map/gelu_slope_1/pallas_call | solution.py:347
  34.0 0.0 collective-permute-done.8.refs_1_.s1
  34.0 0.0 collective-permute-done.9.refs_2_.s2
  34.0 1.1 %collective-permute-done.10.refs_3_.s3 = bf16[112,256]{1,0:T(8,128)(2,1)S(1)} collective-permute-done((bf16[112,256]{1,0:T(8,128)(2,1)S(1)}, bf16[112,256]{1,0:T(8,128)(2,1)S(1)}, u32[]{:S(2)}, u32[]{:S(2)}) %collective-permute-start.10) | collective-permute-done | bytes 57376 | tf_op jit(solution)/shard_map/ppermute | solution.py:378
  35.1 3.4 %upper_x.1 = (bf16[1024,1024]{1,0:T(8,128)(2,1)S(1)}, bf16[512,1024]{1,0:T(8,128)(2,1)S(1)}, bf16[512,1024]{1,0:T(8,128)(2,1)S(1)}) custom-call(bf16[112,256]{1,0:T(8,128)(2,1)S(1)} %get-tuple-element.83.refs_0_.s0, bf16[112,256]{1,0:T(8,128)(2,1)S(1)} %collective-permute-done.8.refs_1_.s1, bf16[112,256]{1,0:T(8,128)(2,1)S(1)} %collective-permute-done.9.refs_2_.s2, ...), custom_call_target="tpu_custom_call" | custom-call | flops 2700000000 | bytes 2000000 | tf_op jit(solution)/shard_map/upper_x/pallas_call | solution.py:347
  38.5 0.1 collective-permute-start.11
  38.6 0.0 copy-start.6
  38.6 3.4 %upper_z.1 = (bf16[1024,1024]{1,0:T(8,128)(2,1)S(1)}, bf16[512,1024]{1,0:T(8,128)(2,1)S(1)}, bf16[512,1024]{1,0:T(8,128)(2,1)S(1)}) custom-call(bf16[112,256]{1,0:T(8,128)(2,1)S(1)} %get-tuple-element.83.refs_0_.s0, bf16[112,256]{1,0:T(8,128)(2,1)S(1)} %collective-permute-done.8.refs_1_.s1, bf16[112,256]{1,0:T(8,128)(2,1)S(1)} %collective-permute-done.9.refs_2_.s2, ...), custom_call_target="tpu_custom_call" | custom-call | flops 2700000000 | bytes 2000000 | tf_op jit(solution)/shard_map/upper_z/pallas_call | solution.py:347
  41.9 0.0 copy-start.9
  42.0 0.6 collective-permute-start.13
  42.6 0.0 collective-permute-done.11
  42.6 0.2 add_convert_fusion.3
  42.8 2.0 %collective-permute-start.12 = (bf16[512,512]{1,0:T(8,128)(2,1)S(1)}, bf16[512,512]{1,0:T(8,128)(2,1)S(1)}, u32[]{:S(2)}, u32[]{:S(2)}) collective-permute-start(bf16[512,512]{1,0:T(8,128)(2,1)S(1)} %add_convert_fusion.3), channel_id=1, source_target_pairs={{0,32},{1,33},{2,34},{3,35},{4,36},{5,37},{6,38},{7,39},{8,40},{9,... | collective-permute-start | bytes 1572872 | tf_op jit(solution)/shard_map/ppermute | solution.py:378
  44.8 0.1 collective-permute-done.13
  44.9 0.2 add_convert_fusion.1
  45.1 2.2 %collective-permute-start.14 = (bf16[512,512]{1,0:T(8,128)(2,1)S(1)}, bf16[512,512]{1,0:T(8,128)(2,1)S(1)}, u32[]{:S(2)}, u32[]{:S(2)}) collective-permute-start(bf16[512,512]{1,0:T(8,128)(2,1)S(1)} %add_convert_fusion.1), channel_id=1, source_target_pairs={{0,4},{1,5},{2,6},{3,7},{4,0},{5,1},{6,2},{7,3},{8,12},{9,13},{10,... | collective-permute-start | bytes 1572872 | tf_op jit(solution)/shard_map/ppermute | solution.py:378
  47.3 0.0 copy-done.6
  47.3 6.2 %lower.1.vg_ref = bf16[400,1024]{1,0:T(8,128)(2,1)S(1)} custom-call(bf16[1024,1024]{1,0:T(8,128)(2,1)S(1)} %get-tuple-element.79.pga_ref, bf16[1024,1024]{1,0:T(8,128)(2,1)S(1)} %get-tuple-element.80.pgb_ref, bf16[1024,2048]{1,0:T(8,128)(2,1)S(1)} %copy-done.6, bf16[1024,1024]{1,0:T(8,128)(2,1)S(1)} %get-tuple-element.69.refs_6_.nrm_ref, ...), custom_call_target="tpu_custom_call" | custom-call | flops 5100000256 | bytes 8000000 | tf_op jit(solution)/shard_map/lower/pallas_call | solution.py:347
  53.5 0.0 collective-permute-done.12
  53.5 0.3 add_convert_fusion.2.first_ref
  53.8 0.8 collective-permute-done.14
  54.6 0.3 add_convert_fusion.second_ref
  54.9 1.6 %collective-permute-start.16 = (bf16[400,1024]{1,0:T(8,128)(2,1)S(1)}, bf16[400,1024]{1,0:T(8,128)(2,1)S(1)}, u32[]{:S(2)}, u32[]{:S(2)}) collective-permute-start(bf16[400,1024]{1,0:T(8,128)(2,1)S(1)} %lower.1.vg_ref), channel_id=1, source_target_pairs={{0,16},{1,17},{2,18},{3,19},{4,20},{5,21},{6,22},{7,23},{8,24},{9,... | collective-permute-start | bytes 2457608 | tf_op jit(solution)/shard_map/ppermute | solution.py:378
  56.5 0.9 grad_out.1
  57.4 0.1 collective-permute-start.15
  57.5 1.5 %collective-permute-done.15.go_recv = bf16[128,1024]{1,0:T(8,128)(2,1)S(1)} collective-permute-done((bf16[128,1024]{1,0:T(8,128)(2,1)S(1)}, bf16[128,1024]{1,0:T(8,128)(2,1)S(1)}, u32[]{:S(2)}, u32[]{:S(2)}) %collective-permute-start.15) | collective-permute-done | bytes 262176 | tf_op jit(solution)/shard_map/ppermute | solution.py:378
  59.0 0.0 copy-done.1
  59.0 0.2 prepare.1
  59.2 0.0 collective-permute-done.16.vg_recv
  59.2 2.3 %grad_value.1 = bf16[512,2304]{1,0:T(8,128)(2,1)} custom-call(bf16[384,512]{1,0:T(8,128)(2,1)S(1)} %get-tuple-element.87.own_lat, bf16[384,512]{1,0:T(8,128)(2,1)S(1)} %collective-permute-done.3.lat_recv, bf16[400,1024]{1,0:T(8,128)(2,1)S(1)} %lower.1.vg_ref, bf16[400,1024]{1,0:T(8,128)(2,1)S(1)} %collective-permute-done.16.vg_recv, ...), custom_call_target="tpu_custom_call" | custom-call | flops 800000000 | bytes 6000000 | tf_op jit(solution)/shard_map/grad_value/pallas_call | solution.py:347
  61.6 9.6 %all-to-all-start = ((bf16[64,8,2304]{2,1,0:T(8,128)(2,1)}), bf16[64,8,2304]{2,1,0:T(8,128)(2,1)S(1)}, u32[]{:S(2)}, u32[]{:S(2)}) async-start(bf16[64,8,2304]{2,1,0:T(8,128)(2,1)} %bitcast.16), calls=%async_computation | async-start | bytes 4718592 | tf_op jit(solution)/shard_map/all_to_all | solution.py:455
  71.2 0.0 copy-start
  71.2 1.6 %copy-done = bf16[1024,1024]{1,0:T(8,128)(2,1)S(1)} copy-done((bf16[1024,1024]{1,0:T(8,128)(2,1)S(1)}, bf16[1024,1024]{1,0:T(8,128)(2,1)}, u32[]{:S(2)}) %copy-start) | copy-done | bytes 2097176
  72.8 1.9 %grad_latents.1 = bf16[384,1024]{1,0:T(8,128)(2,1)} custom-call(bf16[400,1024]{1,0:T(8,128)(2,1)S(1)} %lower.1.vg_ref, bf16[1024,1024]{1,0:T(8,128)(2,1)S(1)} %copy-done), custom_call_target="tpu_custom_call" | custom-call | flops 800000000 | bytes 4000000 | tf_op jit(solution)/shard_map/grad_latents/pallas_call | solution.py:347
  74.7 29.1 %all-to-all-done = bf16[64,8,2304]{2,1,0:T(8,128)(2,1)S(1)} async-done(((bf16[64,8,2304]{2,1,0:T(8,128)(2,1)}), bf16[64,8,2304]{2,1,0:T(8,128)(2,1)S(1)}, u32[]{:S(2)}, u32[]{:S(2)}) %all-to-all-start) | async-done | bytes 2359328 | tf_op jit(solution)/shard_map/all_to_all | solution.py:455
  103.8 1.0 final.1
  (8 shorter events, 0.0 us)
Async XLA Ops:
  0.6 1.0 copy-start.7
  14.0 10.6 %collective-permute-start.3 = (bf16[384,512]{1,0:T(8,128)(2,1)S(1)}, bf16[384,512]{1,0:T(8,128)(2,1)S(1)}, u32[]{:S(2)}, u32[]{:S(2)}) collective-permute-start(bf16[384,512]{1,0:T(8,128)(2,1)S(1)} %get-tuple-element.57), channel_id=1, source_target_pairs={{0,16},{1,17},{2,18},{3,19},{4,20},{5,21},{6,22},{7,23},{8,24},{9,... | collective-permute-start | bytes 1179656 | tf_op jit(solution)/shard_map/ppermute | solution.py:378
  14.1 7.5 %collective-permute-start = (f32[104,256]{1,0:T(8,128)S(1)}, f32[104,256]{1,0:T(8,128)S(1)}, u32[]{:S(2)}, u32[]{:S(2)}) collective-permute-start(f32[104,256]{1,0:T(8,128)S(1)} %get-tuple-element.53), channel_id=1, source_target_pairs={{0,96},{1,97},{2,98},{3,99},{4,100},{5,101},{6,102},{7,103},{8,104... | collective-permute-start | bytes 319496 | tf_op jit(solution)/shard_map/ppermute | solution.py:378
  17.0 5.5 %collective-permute-start.1 = (f32[104,256]{1,0:T(8,128)S(1)}, f32[104,256]{1,0:T(8,128)S(1)}, u32[]{:S(2)}, u32[]{:S(2)}) collective-permute-start(f32[104,256]{1,0:T(8,128)S(1)} %get-tuple-element.55), channel_id=1, source_target_pairs={{0,32},{1,33},{2,34},{3,35},{4,36},{5,37},{6,38},{7,39},{8,40},{9,... | collective-permute-start | bytes 319496 | tf_op jit(solution)/shard_map/ppermute | solution.py:378
  17.2 6.8 %collective-permute-start.2 = (f32[104,256]{1,0:T(8,128)S(1)}, f32[104,256]{1,0:T(8,128)S(1)}, u32[]{:S(2)}, u32[]{:S(2)}) collective-permute-start(f32[104,256]{1,0:T(8,128)S(1)} %get-tuple-element.56), channel_id=1, source_target_pairs={{0,64},{1,65},{2,66},{3,67},{4,68},{5,69},{6,70},{7,71},{8,72},{9,... | collective-permute-start | bytes 319496 | tf_op jit(solution)/shard_map/ppermute | solution.py:378
  18.9 5.7 %collective-permute-start.4 = (f32[104,256]{1,0:T(8,128)S(1)}, f32[104,256]{1,0:T(8,128)S(1)}, u32[]{:S(2)}, u32[]{:S(2)}) collective-permute-start(f32[104,256]{1,0:T(8,128)S(1)} %get-tuple-element.52.f0), channel_id=1, source_target_pairs={{0,16},{1,17},{2,18},{3,19},{4,20},{5,21},{6,22},{7,23},{8,24},{9,... | collective-permute-start | bytes 319496 | tf_op jit(solution)/shard_map/ppermute | solution.py:378
  18.9 6.7 %copy-start.2 = (f32[100,1024]{1,0:T(8,128)S(1)}, f32[100,1024]{1,0:T(8,128)}, u32[]{:S(2)}) copy-start(f32[100,1024]{1,0:T(8,128)} %tg_ref.1) | copy-start | bytes 1228804
  18.9 6.7 %copy-start.3 = (f32[1024]{0:T(1024)S(1)}, f32[1024]{0:T(1024)}, u32[]{:S(2)}) copy-start(f32[1024]{0:T(1024)} %param.22) | copy-start | bytes 12292
  18.9 6.7 %copy-start.4 = (s32[16]{0:T(128)S(1)}, s32[16]{0:T(128)}, u32[]{:S(2)}) copy-start(s32[16]{0:T(128)} %vc_ref.1) | copy-start | bytes 196
  18.9 6.7 %copy-start.5 = (f32[100]{0:T(128)S(1)}, f32[100]{0:T(128)}, u32[]{:S(2)}) copy-start(f32[100]{0:T(128)} %param.21) | copy-start | bytes 1204
  22.5 2.1 %collective-permute-start.6 = (f32[104,256]{1,0:T(8,128)S(1)}, f32[104,256]{1,0:T(8,128)S(1)}, u32[]{:S(2)}, u32[]{:S(2)}) collective-permute-start(f32[104,256]{1,0:T(8,128)S(1)} %collective-permute-done.1.f2), channel_id=1, source_target_pairs={{0,16},{1,17},{2,18},{3,19},{4,20},{5,21},{6,22},{7,23},{8,24},{9,... | collective-permute-start | bytes 319496 | tf_op jit(solution)/shard_map/ppermute | solution.py:378
  24.1 1.3 %collective-permute-start.7 = (f32[104,256]{1,0:T(8,128)S(1)}, f32[104,256]{1,0:T(8,128)S(1)}, u32[]{:S(2)}, u32[]{:S(2)}) collective-permute-start(f32[104,256]{1,0:T(8,128)S(1)} %collective-permute-done.2.f3), channel_id=1, source_target_pairs={{0,16},{1,17},{2,18},{3,19},{4,20},{5,21},{6,22},{7,23},{8,24},{9,... | collective-permute-start | bytes 319496 | tf_op jit(solution)/shard_map/ppermute | solution.py:378
  24.1 1.5 %collective-permute-start.5 = (f32[104,256]{1,0:T(8,128)S(1)}, f32[104,256]{1,0:T(8,128)S(1)}, u32[]{:S(2)}, u32[]{:S(2)}) collective-permute-start(f32[104,256]{1,0:T(8,128)S(1)} %collective-permute-done.f1), channel_id=1, source_target_pairs={{0,16},{1,17},{2,18},{3,19},{4,20},{5,21},{6,22},{7,23},{8,24},{9,... | collective-permute-start | bytes 319496 | tf_op jit(solution)/shard_map/ppermute | solution.py:378
  26.7 7.2 %collective-permute-start.8 = (bf16[112,256]{1,0:T(8,128)(2,1)S(1)}, bf16[112,256]{1,0:T(8,128)(2,1)S(1)}, u32[]{:S(2)}, u32[]{:S(2)}) collective-permute-start(bf16[112,256]{1,0:T(8,128)(2,1)S(1)} %get-tuple-element.61), channel_id=1, source_target_pairs={{0,96},{1,97},{2,98},{3,99},{4,100},{5,101},{6,102},{7,103},{8,104... | collective-permute-start | bytes 172040 | tf_op jit(solution)/shard_map/ppermute | solution.py:378
  29.3 4.7 %collective-permute-start.9 = (bf16[112,256]{1,0:T(8,128)(2,1)S(1)}, bf16[112,256]{1,0:T(8,128)(2,1)S(1)}, u32[]{:S(2)}, u32[]{:S(2)}) collective-permute-start(bf16[112,256]{1,0:T(8,128)(2,1)S(1)} %get-tuple-element.62), channel_id=1, source_target_pairs={{0,32},{1,33},{2,34},{3,35},{4,36},{5,37},{6,38},{7,39},{8,40},{9,... | collective-permute-start | bytes 172040 | tf_op jit(solution)/shard_map/ppermute | solution.py:378
  29.3 5.8 %collective-permute-start.10 = (bf16[112,256]{1,0:T(8,128)(2,1)S(1)}, bf16[112,256]{1,0:T(8,128)(2,1)S(1)}, u32[]{:S(2)}, u32[]{:S(2)}) collective-permute-start(bf16[112,256]{1,0:T(8,128)(2,1)S(1)} %get-tuple-element.63), channel_id=1, source_target_pairs={{0,64},{1,65},{2,66},{3,67},{4,68},{5,69},{6,70},{7,71},{8,72},{9,... | collective-permute-start | bytes 172040 | tf_op jit(solution)/shard_map/ppermute | solution.py:378
  31.7 3.4 %copy-start.8 = (bf16[100,2048]{1,0:T(8,128)(2,1)S(1)}, bf16[100,2048]{1,0:T(8,128)(2,1)}, u32[]{:S(2)}) copy-start(bf16[100,2048]{1,0:T(8,128)(2,1)} %refs_4_.3) | copy-start | bytes 1228804
  38.5 4.1 %collective-permute-start.11 = (bf16[512,1024]{1,0:T(8,128)(2,1)S(1)}, bf16[512,1024]{1,0:T(8,128)(2,1)S(1)}, u32[]{:S(2)}, u32[]{:S(2)}) collective-permute-start(bf16[512,1024]{1,0:T(8,128)(2,1)S(1)} %get-tuple-element.71), channel_id=1, source_target_pairs={{0,16},{1,17},{2,18},{3,19},{4,20},{5,21},{6,22},{7,23},{8,24},{9,... | collective-permute-start | bytes 3145736 | tf_op jit(solution)/shard_map/ppermute | solution.py:378
  38.6 8.8 %copy-start.6 = (bf16[1024,2048]{1,0:T(8,128)(2,1)S(1)}, bf16[1024,2048]{1,0:T(8,128)(2,1)}, u32[]{:S(2)}) copy-start(bf16[1024,2048]{1,0:T(8,128)(2,1)} %wh_ref.1) | copy-start | bytes 12582916
  41.9 5.4 %copy-start.9 = (f32[1024]{0:T(1024)S(1)}, f32[1024]{0:T(1024)}, u32[]{:S(2)}) copy-start(f32[1024]{0:T(1024)} %param.17) | copy-start | bytes 12292
  42.0 2.9 %collective-permute-start.13 = (bf16[512,1024]{1,0:T(8,128)(2,1)S(1)}, bf16[512,1024]{1,0:T(8,128)(2,1)S(1)}, u32[]{:S(2)}, u32[]{:S(2)}) collective-permute-start(bf16[512,1024]{1,0:T(8,128)(2,1)S(1)} %get-tuple-element.76), channel_id=1, source_target_pairs={{0,16},{1,17},{2,18},{3,19},{4,20},{5,21},{6,22},{7,23},{8,24},{9,... | collective-permute-start | bytes 3145736 | tf_op jit(solution)/shard_map/ppermute | solution.py:378
  42.8 10.7 %collective-permute-start.12 = (bf16[512,512]{1,0:T(8,128)(2,1)S(1)}, bf16[512,512]{1,0:T(8,128)(2,1)S(1)}, u32[]{:S(2)}, u32[]{:S(2)}) collective-permute-start(bf16[512,512]{1,0:T(8,128)(2,1)S(1)} %add_convert_fusion.3), channel_id=1, source_target_pairs={{0,32},{1,33},{2,34},{3,35},{4,36},{5,37},{6,38},{7,39},{8,40},{9,... | collective-permute-start | bytes 1572872 | tf_op jit(solution)/shard_map/ppermute | solution.py:378
  45.1 9.5 %collective-permute-start.14 = (bf16[512,512]{1,0:T(8,128)(2,1)S(1)}, bf16[512,512]{1,0:T(8,128)(2,1)S(1)}, u32[]{:S(2)}, u32[]{:S(2)}) collective-permute-start(bf16[512,512]{1,0:T(8,128)(2,1)S(1)} %add_convert_fusion.1), channel_id=1, source_target_pairs={{0,4},{1,5},{2,6},{3,7},{4,0},{5,1},{6,2},{7,3},{8,12},{9,13},{10,... | collective-permute-start | bytes 1572872 | tf_op jit(solution)/shard_map/ppermute | solution.py:378
  54.9 4.4 %collective-permute-start.16 = (bf16[400,1024]{1,0:T(8,128)(2,1)S(1)}, bf16[400,1024]{1,0:T(8,128)(2,1)S(1)}, u32[]{:S(2)}, u32[]{:S(2)}) collective-permute-start(bf16[400,1024]{1,0:T(8,128)(2,1)S(1)} %lower.1.vg_ref), channel_id=1, source_target_pairs={{0,16},{1,17},{2,18},{3,19},{4,20},{5,21},{6,22},{7,23},{8,24},{9,... | collective-permute-start | bytes 2457608 | tf_op jit(solution)/shard_map/ppermute | solution.py:378
  56.5 2.6 %copy-start.1 = (bf16[1,384,1024]{2,1,0:T(8,128)(2,1)S(1)}, bf16[1,384,1024]{2,1,0:T(8,128)(2,1)}, u32[]{:S(2)}) copy-start(bf16[1,384,1024]{2,1,0:T(8,128)(2,1)} %param.12) | copy-start | bytes 2359300
  57.4 1.6 %collective-permute-start.15 = (bf16[128,1024]{1,0:T(8,128)(2,1)S(1)}, bf16[128,1024]{1,0:T(8,128)(2,1)S(1)}, u32[]{:S(2)}, u32[]{:S(2)}) collective-permute-start(bf16[128,1024]{1,0:T(8,128)(2,1)S(1)} %get-tuple-element.86), channel_id=1, source_target_pairs={{0,16},{1,17},{2,18},{3,19},{4,20},{5,21},{6,22},{7,23},{8,24},{9,... | collective-permute-start | bytes 786440 | tf_op jit(solution)/shard_map/ppermute | solution.py:378
  61.6 42.3 %all-to-all-start = ((bf16[64,8,2304]{2,1,0:T(8,128)(2,1)}), bf16[64,8,2304]{2,1,0:T(8,128)(2,1)S(1)}, u32[]{:S(2)}, u32[]{:S(2)}) async-start(bf16[64,8,2304]{2,1,0:T(8,128)(2,1)} %bitcast.16), calls=%async_computation | async-start | bytes 4718592 | tf_op jit(solution)/shard_map/all_to_all | solution.py:455
  71.2 1.6 %copy-start = (bf16[1024,1024]{1,0:T(8,128)(2,1)S(1)}, bf16[1024,1024]{1,0:T(8,128)(2,1)}, u32[]{:S(2)}) copy-start(bf16[1024,1024]{1,0:T(8,128)(2,1)} %wv_ref.1) | copy-start | bytes 6291460
